TPU v7x, 128 devices: a whole 4x4x4 slice. The times are simulated.
128 devices in a mesh: tmpl: 16 (over z, y), seg: 8 (over x, core).
Axes of the slice: x: 4, y: 4, z: 4, core: 2. Of those that a mesh axis runs over, the one named last changes fastest.
Arguments:
- strain: bfloat16 [2, 2, 8, 512, 1024], P(None, None, 'seg', 'tmpl'), may hold values from -6 to 6
- templates: bfloat16 [2, 16, 512, 1024], P(None, 'tmpl', 'seg'), may hold values from -400 to 400
- trig_pair: int32 [128, 256], P(('tmpl', 'seg')), may hold values from 0 to 127, as said below
- trig_time: int32 [128, 256], P(('tmpl', 'seg')), may hold values from 0 to 524287
- trig_counts: int32 [128], P(('tmpl', 'seg')), may hold values from 128 to 256, as said below
Outputs:
- snr_series: float32 [16, 8, 1024, 512], P('tmpl', 'seg')
- peak: float32 [16, 8], P('tmpl', 'seg')
- chi_square: float32 [128, 256], P(('tmpl', 'seg'))
- trigger_snr: float32 [128, 256], P(('tmpl', 'seg'))
Inputs may be any that keep to these rules, and one draw needn't show every extreme that they name: `trig_pair`: among the live rows of one device's list no value appears more than 2 times, and one value, the same for every device, appears exactly 2 times in every device's live rows. `trig_counts`: some device's list is live in full.
All inputs are finite; a program needn't handle non-finite values.
Results may differ from a plain program's by a relative error of at most 0.0055.
Values may be sent and summed in bfloat16 or wider, within the bound.
No kernel may reach another device: no remote copies, remote signals or barrier semaphores. Data moves between devices by JAX's collectives and lax.ppermute only.
A program may use at most 64 MiB of HBM per device.

v0:
```python
import functools
import math

import jax
import jax.numpy as jnp
import numpy as np
import ml_dtypes
from jax import lax
from jax.experimental import pallas as pl
from jax.experimental.pallas import tpu as pltpu
from jax.sharding import PartitionSpec as P

BANDS = 16
ROWS = 512
COLS = 1024
BINS = ROWS * COLS
BLOCK = 32
SLOTS = 256
OFFSETS = (0, 3, 1, 2)
F32 = jnp.float32
BF16 = jnp.bfloat16
VMEM = pl.BlockSpec(memory_space=pltpu.VMEM)
SMEM = pl.BlockSpec(memory_space=pltpu.SMEM)
LIMIT = 48 * 1024 * 1024


def unit(numerator, modulus):
    angle = 2.0 * math.pi * (np.asarray(numerator, np.int64) % modulus) / modulus
    return np.cos(angle), np.sin(angle)


def row_matrices():
    out = np.zeros((4, 4, 256, 256), np.float32)
    u = np.arange(128)
    for y in range(4):
        a = np.concatenate([32 * ((y + o) % 4) + np.arange(32) for o in OFFSETS])
        for p in range(4):
            c, s = unit(a[None, :] * (4 * u[:, None] + p), ROWS)
            out[y, p] = np.block([[c, -s], [s, c]])
    return out.astype(ml_dtypes.bfloat16)


def col_matrices():
    out = np.zeros((4, 512, 512), np.float32)
    n = np.arange(256)
    for p in range(4):
        c, s = unit(n[:, None] * (4 * n[None, :] + p), COLS)
        out[p] = np.block([[c, s], [-s, c]])
    return out.astype(ml_dtypes.bfloat16)


def twiddles():
    out = np.zeros((4, 2, 128, COLS), np.float32)
    u = np.arange(128)
    for p in range(4):
        c, s = unit((4 * u[:, None] + p) * np.arange(COLS)[None, :], BINS)
        out[p, 0], out[p, 1] = c, s
    return out


def along_tmpl(x, dz, dy):
    pairs = [
        (z * 4 + y, ((z + dz) % 4) * 4 + (y + dy) % 4) for z in range(4) for y in range(4)
    ]
    return lax.ppermute(x, "tmpl", pairs)


def along_seg(x, dx, dc):
    pairs = [(k * 2 + c, ((k + dx) % 4) * 2 + (c + dc) % 2) for k in range(4) for c in range(2)]
    return lax.ppermute(x, "seg", pairs)


def angle_parts(numerator, modulus):
    angles = (2.0 * math.pi / modulus) * (numerator & (modulus - 1)).astype(F32)
    return jnp.cos(angles), jnp.sin(angles)


def probe_kernel(time_ref, one_ref, two_ref, shift_ref, band_ref):
    t = jnp.maximum(time_ref[...], 0)
    step = lax.broadcasted_iota(jnp.int32, (32, SLOTS), 0)
    low_r, low_i = angle_parts(step * t, BINS)
    high_r, high_i = angle_parts(step * 32 * t, BINS)
    shift_ref[0], shift_ref[1] = angle_parts(step * t, ROWS)
    band_ref[0], band_ref[1] = angle_parts(step[:BANDS] * t, BANDS)
    for h in range(32):
        hr, hi = high_r[h : h + 1], high_i[h : h + 1]
        pr = (hr * low_r - hi * low_i).astype(BF16)
        pi = (hr * low_i + hi * low_r).astype(BF16)
        rows = pl.ds(32 * h, 32)
        one_ref[rows, :SLOTS] = pr
        one_ref[rows, SLOTS:] = pi
        two_ref[rows, :SLOTS] = -pi
        two_ref[rows, SLOTS:] = pr


def probes(times):
    return pl.pallas_call(
        probe_kernel,
        out_shape=(
            jax.ShapeDtypeStruct((COLS, 2 * SLOTS), BF16),
            jax.ShapeDtypeStruct((COLS, 2 * SLOTS), BF16),
            jax.ShapeDtypeStruct((2, 32, SLOTS), F32),
            jax.ShapeDtypeStruct((2, BANDS, SLOTS), F32),
        ),
        in_specs=[VMEM],
        out_specs=(VMEM,) * 4,
        compiler_params=pltpu.CompilerParams(vmem_limit_bytes=LIMIT),
        cost_estimate=pl.CostEstimate(flops=4_000_000, bytes_accessed=2_200_000, transcendentals=60_000),
        name="probes",
    )(times)


def veto_kernel(zones, prior, final, *refs):
    n = len(zones)
    place, own_ref, other_ref, one_ref, two_ref, shift_ref, band_ref = refs[:7]
    parts = refs[7 : 7 + 2 * n]
    refs = refs[7 + 2 * n :]
    before = refs[: 2 * prior]
    refs = refs[2 * prior :]
    if final:
        time_ref, refs = refs[0], refs[1:]
    specs, refs = refs[:n], refs[n:]
    if final:
        result_ref, sigma_ref, sum_ref, power_ref = refs
    else:
        sum_ref, power_ref = refs
    z, y, x, core = place[0], place[1], place[2], place[3]
    sr, si = shift_ref[0], shift_ref[1]

    def block_place(det, zone, m):
        om = jnp.where(m == 0, 0, jnp.where(m == 1, 3, m - 1))
        oz, oy = (OFFSETS[zone], om) if det == 0 else (om, OFFSETS[zone])
        return (z + oz) & 3, (y + oy) & 3

    for index, zone in enumerate(zones):
        spec = specs[index]
        for det in range(2):
            part = parts[2 * index + det]

            def one_block(m, carry, det=det, part=part, zone=zone, spec=spec, index=index):
                zz, yy = block_place(det, zone, m)
                rel = (zz - x) & 3
                pos = jnp.where(rel == 0, 0, jnp.where(rel == 3, 1, rel + 1))
                mine = (yy >> 1) == core
                rows = pl.ds(pl.multiple_of(32 * (yy & 1), 32), 32)
                total = jnp.zeros((8, 128), F32)
                for lane in range(0, COLS, 256):
                    cols = pl.ds(lane, 256)
                    h = [
                        jnp.where(
                            mine,
                            own_ref[pos, k, rows, cols].astype(F32),
                            other_ref[pos, k, rows, cols].astype(F32),
                        )
                        for k in range(2)
                    ]
                    xr = part[m, 0, :, cols].astype(F32)
                    xi = part[m, 1, :, cols].astype(F32)
                    spec[0, 4 * det + m, :, cols] = (h[0] * xr + h[1] * xi).astype(BF16)
                    spec[1, 4 * det + m, :, cols] = (h[0] * xi - h[1] * xr).astype(BF16)
                    power = h[0] * h[0] + h[1] * h[1]
                    for r in range(0, 32, 8):
                        for c in range(0, 256, 128):
                            total = total + power[r : r + 8, c : c + 128]
                whole = jnp.sum(total, axis=(0, 1), keepdims=True)
                power_ref[pl.ds(8 * index + 4 * det + m, 1), :] = jnp.broadcast_to(whole, (1, SLOTS))
                return carry

            lax.fori_loop(0, 4, one_block, 0)
        out = jnp.dot(spec[0].reshape(256, COLS), one_ref[...], preferred_element_type=F32)
        out = out + jnp.dot(spec[1].reshape(256, COLS), two_ref[...], preferred_element_type=F32)
        for det in range(2):
            for m in range(4):
                i = 4 * det + m
                yr = out[32 * i : 32 * i + 32, :SLOTS]
                yi = out[32 * i : 32 * i + 32, SLOTS:]
                ar = jnp.sum(yr * sr - yi * si, axis=0, keepdims=True)
                ai = jnp.sum(yr * si + yi * sr, axis=0, keepdims=True)
                zz, yy = block_place(det, zone, m)
                band = 4 * zz + yy
                er = band_ref[0, pl.ds(band, 1), :]
                ei = band_ref[1, pl.ds(band, 1), :]
                sum_ref[8 * index + i : 8 * index + i + 1, :SLOTS] = ar * er - ai * ei
                sum_ref[8 * index + i : 8 * index + i + 1, SLOTS:] = ar * ei + ai * er
    if not final:
        return
    sums = [before[2 * k][...] for k in range(prior)] + [sum_ref[...]]
    powers = [before[2 * k + 1][...] for k in range(prior)] + [power_ref[...]]
    sums = jnp.concatenate(sums, axis=0)
    powers = jnp.concatenate(powers, axis=0)
    groups = sums.shape[0] // 8
    per_det = []
    for det in range(2):
        pick = lambda v: jnp.concatenate(
            [v[8 * g + 4 * det : 8 * g + 4 * det + 4] for g in range(groups)], axis=0
        )
        per_det.append((pick(sums), pick(powers)))
    sigma = jnp.sum(per_det[0][1], axis=0, keepdims=True)
    chi = jnp.zeros((1, SLOTS), F32)
    snr = jnp.zeros((1, SLOTS), F32)
    for both, power in per_det:
        br, bi = both[:, :SLOTS], both[:, SLOTS:]
        tr = jnp.sum(br, axis=0, keepdims=True)
        ti = jnp.sum(bi, axis=0, keepdims=True)
        weight = power / sigma
        dr = br - weight * tr
        di = bi - weight * ti
        chi = chi + jnp.sum((dr * dr + di * di) / (weight * sigma), axis=0, keepdims=True)
        snr = snr + (tr * tr + ti * ti)
    usable = time_ref[...] >= 0
    result_ref[0:1, :] = jnp.where(usable, chi / (4.0 * (BANDS - 1)), 0.0)
    result_ref[1:2, :] = jnp.where(usable, snr / (2.0 * sigma), 0.0)
    sigma_ref[...] = sigma


def veto(zones, place, own, other, tables, parts, before=(), times=None):
    n = len(zones)
    final = times is not None
    inputs = [place, own, other, *tables, *parts, *before] + ([times] if final else [])
    specs = [jax.ShapeDtypeStruct((2, 8, 32, COLS), BF16)] * n
    sums = [
        jax.ShapeDtypeStruct((8 * n, 2 * SLOTS), F32),
        jax.ShapeDtypeStruct((8 * n, SLOTS), F32),
    ]
    if final:
        outs = specs + [
            jax.ShapeDtypeStruct((2, SLOTS), F32),
            jax.ShapeDtypeStruct((1, SLOTS), F32),
        ]
        scratch = [pltpu.VMEM(s.shape, s.dtype) for s in sums]
    else:
        outs = specs + sums
        scratch = []
    return pl.pallas_call(
        functools.partial(veto_kernel, zones, len(before) // 2, final),
        out_shape=tuple(outs),
        in_specs=[SMEM] + [VMEM] * (len(inputs) - 1),
        out_specs=(VMEM,) * len(outs),
        scratch_shapes=scratch,
        compiler_params=pltpu.CompilerParams(vmem_limit_bytes=LIMIT),
        cost_estimate=pl.CostEstimate(
            flops=n * 560_000_000, bytes_accessed=n * 2_000_000 + 4_000_000, transcendentals=0
        ),
        name="veto_last" if final else "veto_part",
    )(*inputs)


def series_kernel(s0, s1, s2, s3, rows_ref, turn_ref, cols_ref, sigma_ref, out_ref, peak_ref, x_ref, w_ref, t_ref, o_ref):
    specs = (s0, s1, s2, s3)

    def four(q):
        (r0, i0), (r3, i3), (r1, i1), (r2, i2) = q
        ar, ai = r0 + r2, i0 + i2
        br, bi = r1 + r3, i1 + i3
        cr, ci = r0 - r2, i0 - i2
        dr, di = r1 - r3, i1 - i3
        return (
            (ar + br, ai + bi),
            (cr - di, ci + dr),
            (ar - br, ai - bi),
            (cr + di, ci - dr),
        )

    def fold(det, m, load):
        def chunk(k, carry):
            cols = pl.ds(pl.multiple_of(k * 256, 256), 256)
            q = [(load(o, 0, cols).astype(F32), load(o, 1, cols).astype(F32)) for o in range(4)]
            for p, (re, im) in enumerate(four(q)):
                x_ref[det, p, pl.ds(32 * m, 32), cols] = re.astype(BF16)
                x_ref[det, p, pl.ds(128 + 32 * m, 32), cols] = im.astype(BF16)
            return carry

        lax.fori_loop(0, 4, chunk, 0)

    for m in range(4):
        fold(0, m, lambda o, part, cols: specs[o][part, m, :, cols])
        fold(1, m, lambda o, part, cols: specs[m][part, 4 + o, :, cols])

    def first(step, carry):
        det = step // 4
        p = step % 4
        matrix = rows_ref[p]
        h = []
        for j in range(4):
            cols = pl.ds(256 * j, 256)
            g = jnp.dot(matrix, x_ref[det, p, :, cols], preferred_element_type=F32)
            gr, gi = g[:128], g[128:]
            tr = turn_ref[p, 0, :, cols]
            ti = turn_ref[p, 1, :, cols]
            h.append((gr * tr - gi * ti, gr * ti + gi * tr))
        (r0, i0), (r1, i1), (r2, i2), (r3, i3) = h
        for k, (re, im) in enumerate(four(((r0, i0), (r3, i3), (r1, i1), (r2, i2)))):
            rows = pl.ds(pl.multiple_of(128 * p, 128), 128)
            w_ref[k, det, rows, :256] = re.astype(BF16)
            w_ref[k, det, rows, 256:] = im.astype(BF16)
        return carry

    lax.fori_loop(0, 8, first, 0)

    scale = 1.0 / (2.0 * sigma_ref[0, 0])

    def second(k, best):
        total = None
        for det in range(2):
            out = jnp.dot(w_ref[k, det], cols_ref[k], preferred_element_type=F32)
            re, im = out[:, :256], out[:, 256:]
            power = re * re + im * im
            total = power if total is None else total + power
        total = total * scale
        for p in range(4):
            for half in range(2):
                t_ref[2 * k + half, pl.ds(p, 128, stride=4), :] = total[
                    128 * p : 128 * p + 128, 128 * half : 128 * half + 128
                ]
        best = jnp.maximum(best, jnp.max(total.reshape(64, 8, 256), axis=0))
        return best

    best = lax.fori_loop(0, 4, second, jnp.zeros((8, 256), F32))
    peak_ref[...] = jnp.max(best, axis=(0, 1), keepdims=True)
    for k in range(4):
        for half in range(2):
            for i in range(4):
                tile = t_ref[2 * k + half, pl.ds(128 * i, 128), :]
                o_ref[i, pl.ds(512 * half + k, 128, stride=4), :] = tile.T
    for i in range(4):
        out_ref[:, pl.ds(128 * i, 128)] = o_ref[i]


def series(specs, rows, turns, cols, sigma):
    return pl.pallas_call(
        series_kernel,
        out_shape=(
            jax.ShapeDtypeStruct((COLS, ROWS), F32),
            jax.ShapeDtypeStruct((1, 1), F32),
        ),
        in_specs=[VMEM] * 8,
        out_specs=(VMEM, VMEM),
        scratch_shapes=[
            pltpu.VMEM((2, 4, 256, COLS), BF16),
            pltpu.VMEM((4, 2, ROWS, 512), BF16),
            pltpu.VMEM((8, ROWS, 128), F32),
            pltpu.VMEM((4, COLS, 128), F32),
        ],
        compiler_params=pltpu.CompilerParams(vmem_limit_bytes=LIMIT),
        cost_estimate=pl.CostEstimate(
            flops=3_300_000_000, bytes_accessed=13_000_000, transcendentals=0
        ),
        name="series",
    )(*specs, rows, turns, cols, sigma)


def shards(strain, templates, trig_pair, trig_time, trig_counts):
    device = lax.axis_index("tmpl")
    seat = lax.axis_index("seg")
    place = jnp.stack([device // 4, device % 4, seat // 2, seat % 2]).astype(jnp.int32)
    rows = lax.dynamic_index_in_dim(jnp.asarray(row_matrices()), device % 4, 0, keepdims=False)
    turns = jnp.asarray(twiddles())
    cols = jnp.asarray(col_matrices())

    a, b, t = strain[:, 0, 0], strain[:, 1, 0], templates[:, 0]
    a = [a, along_tmpl(a, 0, 1), along_tmpl(a, 0, 3), along_tmpl(a, 0, 2)]
    b = [b, along_tmpl(b, 1, 0), along_tmpl(b, 3, 0), along_tmpl(b, 2, 0)]
    t = [t, along_seg(t, 1, 0), along_seg(t, 3, 0), along_seg(t, 2, 0)]
    a, b, t = jnp.stack(a), jnp.stack(b), jnp.stack(t)
    a = [a, along_tmpl(a, 1, 0), along_tmpl(a, 3, 0), along_tmpl(a, 2, 0)]
    b = [b, along_tmpl(b, 0, 1), along_tmpl(b, 0, 3), along_tmpl(b, 0, 2)]
    other = along_seg(t, 0, 1)

    device_total = lax.axis_size("tmpl") * lax.axis_size("seg")
    pair_list = trig_pair[0]
    time_list = trig_time[0]
    slots_each = SLOTS // device_total
    positions = jnp.arange(SLOTS, dtype=jnp.int32)
    live_rows = positions < trig_counts[0]
    same = (pair_list[:, None] == pair_list[None, :]) & (positions[None, :] < positions[:, None])
    slot_rank = jnp.sum((same & live_rows[None, :]).astype(jnp.int32), axis=1)
    slot_of = pair_list * slots_each + slot_rank
    slot_match = (slot_of[:, None] == positions[None, :]) & live_rows[:, None]
    outgoing = jnp.sum(jnp.where(slot_match, time_list[:, None] + 1, 0), axis=0) - 1
    incoming = lax.all_to_all(
        outgoing.reshape(device_total, slots_each),
        ("tmpl", "seg"),
        split_axis=0,
        concat_axis=0,
        tiled=True,
    )
    times = incoming.reshape(1, SLOTS)
    tables = probes(times)
    spec0, sum0, power0 = veto((0,), place, t, other, tables, (a[0], b[0]))
    parts = [v for k in (1, 2, 3) for v in (a[k], b[k])]
    *rest, result, sigma = veto((1, 2, 3), place, t, other, tables, parts, (sum0, power0), times)
    back = lax.all_to_all(
        result.reshape(2, device_total, slots_each),
        ("tmpl", "seg"),
        split_axis=1,
        concat_axis=1,
        tiled=True,
    ).reshape(2, SLOTS)
    snr_series, peak = series((spec0, *rest), rows, turns, cols, sigma)
    mine = jnp.sum(jnp.where(slot_match[None], back[:, None, :], 0.0), axis=2)
    return (snr_series[None, None], peak, mine[0][None], mine[1][None])


def solution(mesh):
    in_specs = (
        P(None, None, "seg", "tmpl", None),
        P(None, "tmpl", "seg", None),
        P(("tmpl", "seg"), None),
        P(("tmpl", "seg"), None),
        P(("tmpl", "seg")),
    )
    out_specs = (
        P("tmpl", "seg", None, None),
        P("tmpl", "seg"),
        P(("tmpl", "seg"), None),
        P(("tmpl", "seg"), None),
    )
    return jax.shard_map(shards, mesh=mesh, in_specs=in_specs, out_specs=out_specs, check_vma=False)
```

profile of v0, /device:TPU:1, one launch (start us, length us, event | category | flops | bytes accessed | tf_op | source)
XLA Modules:
  0.0 105.6 jit_solution(10079202087449015986)
XLA Ops:
  0.7 3.7 %collective-permute-start.2 = (bf16[2,64,1024]{2,1,0:T(8,128)(2,1)}, bf16[2,64,1024]{2,1,0:T(8,128)(2,1)S(1)}, u32[]{:S(2)}, u32[]{:S(2)}) collective-permute-start(bf16[2,64,1024]{2,1,0:T(8,128)(2,1)} %bitcast.37), channel_id=1, source_target_pairs={{0,4},{1,5},{2,6},{3,7},{4,0},{5,1},{6,2},{7,3},{8,12},{9,13},{10,... | collective-permute-start | bytes 786440 | tf_op jit(solution)/shard_map/ppermute | solution.py:70
  4.3 0.9 collective-permute-start.1
  5.8 1.0 slice_bitcast_fusion
  6.8 3.0 %collective-permute-start.6 = (bf16[2,32,1024]{2,1,0:T(8,128)(2,1)S(1)}, bf16[2,32,1024]{2,1,0:T(8,128)(2,1)S(1)}, u32[]{:S(2)}, u32[]{:S(2)}) collective-permute-start(bf16[2,32,1024]{2,1,0:T(8,128)(2,1)S(1)} %get-tuple-element.34), channel_id=1, source_target_pairs={{0,16},{8,24},{16,0},{24,8},{32,48},{40,56},{48,32},{56,40},{64,80... | collective-permute-start | bytes 393224 | tf_op jit(solution)/shard_map/ppermute | solution.py:65
  9.8 0.8 collective-permute-start.5
  12.0 4.3 %collective-permute-done.1 = bf16[2,64,1024]{2,1,0:T(8,128)(2,1)S(1)} collective-permute-done((bf16[2,64,1024]{2,1,0:T(8,128)(2,1)}, bf16[2,64,1024]{2,1,0:T(8,128)(2,1)S(1)}, u32[]{:S(2)}, u32[]{:S(2)}) %collective-permute-start.1) | collective-permute-done | bytes 262176 | tf_op jit(solution)/shard_map/ppermute | solution.py:70
  16.3 3.6 %collective-permute-start.9 = (bf16[2,32,1024]{2,1,0:T(8,128)(2,1)S(1)}, bf16[2,32,1024]{2,1,0:T(8,128)(2,1)S(1)}, u32[]{:S(2)}, u32[]{:S(2)}) collective-permute-start(bf16[2,32,1024]{2,1,0:T(8,128)(2,1)S(1)} %get-tuple-element.35), channel_id=1, source_target_pairs={{0,64},{8,72},{16,80},{24,88},{32,96},{40,104},{48,112},{56,120},{... | collective-permute-start | bytes 393224 | tf_op jit(solution)/shard_map/ppermute | solution.py:65
  19.9 1.1 %pad_maximum_fusion.refs_1_ = bf16[4,2,64,1024]{3,2,1,0:T(8,128)(2,1)S(1)} fusion(bf16[1,2,64,1024]{3,2,1,0:T(8,128)(2,1)S(1)} %bitcast.41, bf16[1,2,64,1024]{3,2,1,0:T(8,128)(2,1)S(1)} %bitcast.42, bf16[1,2,64,1024]{3,2,1,0:T(8,128)(2,1)S(1)} %bitcast.43, bf16[1,2,64,1024]{3,2,1,0:T(8,128)(2,1)} %bitcast.40), kind=kLoop, calls=%fused_computation | loop fusion | flops 1572864 | bytes 2097152 | tf_op jit(solution)/shard_map/stack | solution.py:364
  21.0 1.8 %collective-permute-start.3 = (bf16[4,2,64,1024]{3,2,1,0:T(8,128)(2,1)S(1)}, bf16[4,2,64,1024]{3,2,1,0:T(8,128)(2,1)S(1)}, u32[]{:S(2)}, u32[]{:S(2)}) collective-permute-start(bf16[4,2,64,1024]{3,2,1,0:T(8,128)(2,1)S(1)} %pad_maximum_fusion.refs_1_), channel_id=1, source_target_pairs={{0,1},{1,0},{2,3},{3,2},{4,5},{5,4},{6,7},{7,6},{8,9},{9,8},{10,11... | collective-permute-start | bytes 3145736 | tf_op jit(solution)/shard_map/ppermute | solution.py:70
  23.5 1.0 collective-permute-start.7
  24.6 0.8 collective-permute-start.10
  25.6 2.0 %collective-permute-start.12 = (bf16[4,2,32,1024]{3,2,1,0:T(8,128)(2,1)S(1)}, bf16[4,2,32,1024]{3,2,1,0:T(8,128)(2,1)}, u32[]{:S(2)}, u32[]{:S(2)}) collective-permute-start(bf16[4,2,32,1024]{3,2,1,0:T(8,128)(2,1)S(1)} %pad_maximum_fusion.1.refs_7_), channel_id=1, source_target_pairs={{0,96},{8,104},{16,112},{24,120},{32,0},{40,8},{48,16},{56,24},{64... | collective-permute-start | bytes 1572872 | tf_op jit(solution)/shard_map/ppermute | solution.py:65
  28.2 1.3 %collective-permute-done.7 = bf16[2,32,1024]{2,1,0:T(8,128)(2,1)S(1)} collective-permute-done((bf16[2,32,1024]{2,1,0:T(8,128)(2,1)S(1)}, bf16[2,32,1024]{2,1,0:T(8,128)(2,1)S(1)}, u32[]{:S(2)}, u32[]{:S(2)}) %collective-permute-start.7) | collective-permute-done | bytes 131104 | tf_op jit(solution)/shard_map/ppermute | solution.py:65
  29.6 1.4 %collective-permute-start.11 = (bf16[4,2,32,1024]{3,2,1,0:T(8,128)(2,1)S(1)}, bf16[4,2,32,1024]{3,2,1,0:T(8,128)(2,1)}, u32[]{:S(2)}, u32[]{:S(2)}) collective-permute-start(bf16[4,2,32,1024]{3,2,1,0:T(8,128)(2,1)S(1)} %pad_maximum_fusion.2.refs_8_), channel_id=1, source_target_pairs={{0,8},{8,16},{16,24},{24,0},{32,40},{40,48},{48,56},{56,32},{64,72... | collective-permute-start | bytes 1572872 | tf_op jit(solution)/shard_map/ppermute | solution.py:65
  30.9 1.5 %collective-permute-start.13 = (bf16[4,2,32,1024]{3,2,1,0:T(8,128)(2,1)S(1)}, bf16[4,2,32,1024]{3,2,1,0:T(8,128)(2,1)}, u32[]{:S(2)}, u32[]{:S(2)}) collective-permute-start(bf16[4,2,32,1024]{3,2,1,0:T(8,128)(2,1)S(1)} %pad_maximum_fusion.2.refs_8_), channel_id=1, source_target_pairs={{0,24},{8,0},{16,8},{24,16},{32,56},{40,32},{48,40},{56,48},{64,88... | collective-permute-start | bytes 1572872 | tf_op jit(solution)/shard_map/ppermute | solution.py:65
  32.5 8.4 %collective-permute-done.10.refs_7_ = bf16[4,2,32,1024]{3,2,1,0:T(8,128)(2,1)S(1)} collective-permute-done((bf16[4,2,32,1024]{3,2,1,0:T(8,128)(2,1)S(1)}, bf16[4,2,32,1024]{3,2,1,0:T(8,128)(2,1)S(1)}, u32[]{:S(2)}, u32[]{:S(2)}) %collective-permute-start.10) | collective-permute-done | bytes 524320 | tf_op jit(solution)/shard_map/ppermute | solution.py:65
  40.8 0.8 copy-done.4
  41.6 0.9 collective-permute-start.14
  42.5 2.9 %collective-permute-start.15 = (bf16[4,2,32,1024]{3,2,1,0:T(8,128)(2,1)S(1)}, bf16[4,2,32,1024]{3,2,1,0:T(8,128)(2,1)}, u32[]{:S(2)}, u32[]{:S(2)}) collective-permute-start(bf16[4,2,32,1024]{3,2,1,0:T(8,128)(2,1)S(1)} %pad_maximum_fusion.2.refs_8_), channel_id=1, source_target_pairs={{0,16},{8,24},{16,0},{24,8},{32,48},{40,56},{48,32},{56,40},{64,80... | collective-permute-start | bytes 1572872 | tf_op jit(solution)/shard_map/ppermute | solution.py:65
  46.2 7.4 %all-to-all-start = ((s32[128,1,2]{2,1,0:T(1,128)}), s32[128,1,2]{2,1,0:T(1,128)S(1)}, u32[]{:S(2)}, u32[]{:S(2)}) async-start(s32[128,1,2]{2,1,0:T(1,128)} %bitcast.12), calls=%async_computation | async-start | bytes 131072 | tf_op jit(solution)/shard_map/all_to_all | solution.py:380
  53.7 1.9 %dynamic-slice_bitcast_fusion.rows_ref = bf16[4,256,256]{2,1,0:T(8,128)(2,1)} fusion(bf16[4,4,256,256]{3,2,1,0:T(8,128)(2,1)} %constant.70.clone, s32[]{:T(128)S(6)} %select_n.37), kind=kLoop, calls=%fused_computation.4 | loop fusion | bytes 1048580 | tf_op jit(solution)/shard_map/jit(dynamic_index_in_dim)/squeeze | solution.py:356
  55.8 7.4 %all-to-all-done = s32[128,1,2]{2,1,0:T(1,128)S(1)} async-done(((s32[128,1,2]{2,1,0:T(1,128)}), s32[128,1,2]{2,1,0:T(1,128)S(1)}, u32[]{:S(2)}, u32[]{:S(2)}) %all-to-all-start) | async-done | bytes 1056 | tf_op jit(solution)/shard_map/all_to_all | solution.py:380
  63.7 0.8 reduce.3
  65.4 1.0 copy-done.3
  66.3 4.1 %veto_part.1 = (bf16[2,8,32,1024]{3,2,1,0:T(8,128)(2,1)S(1)}, f32[8,512]{1,0:T(8,128)S(1)}, f32[8,256]{1,0:T(8,128)S(1)}) custom-call(s32[4]{0:T(128)S(1)} %pad_add_fusion.refs_0_, bf16[4,2,64,1024]{3,2,1,0:T(8,128)(2,1)S(1)} %pad_maximum_fusion.refs_1_, bf16[4,2,64,1024]{3,2,1,0:T(8,128)(2,1)S(1)} %collective-permute-done.3.refs_2_, ...), custom_call_target="tpu_custom_call" | custom-call | flops 560000000 | bytes 6000000 | tf_op jit(solution)/shard_map/veto_part/pallas_call | solution.py:234
  70.5 1.0 copy-done.7
  71.6 11.4 %veto_last.1 = (bf16[2,8,32,1024]{3,2,1,0:T(8,128)(2,1)S(1)}, bf16[2,8,32,1024]{3,2,1,0:T(8,128)(2,1)S(1)}, bf16[2,8,32,1024]{3,2,1,0:T(8,128)(2,1)}, f32[2,256]{1,0:T(2,128)S(1)}, f32[1,256]{1,0:T(1,128)S(1)}) custom-call(s32[4]{0:T(128)S(1)} %pad_add_fusion.refs_0_, bf16[4,2,64,1024]{3,2,1,0:T(8,128)(2,1)} %copy-done, bf16[4,2,64,1024]{3,2,1,0:T(8,128)(2,1)} %copy-done.1, ...), custom_call_target="tpu_custom_call" | custom-call | flops 1680000000 | bytes 10000000 | tf_op jit(solution)/shard_map/veto_last/pallas_call | solution.py:234
  82.9 1.0 copy-done.9
  84.8 4.5 %all-to-all-start.1 = ((f32[2,128,2]{2,0,1:T(2,128)}), f32[2,128,2]{2,0,1:T(2,128)S(1)}, u32[]{:S(2)}, u32[]{:S(2)}) async-start(f32[2,128,2]{2,0,1:T(2,128)} %copy.24), calls=%async_computation.1 | async-start | bytes 262144 | tf_op jit(solution)/shard_map/all_to_all | solution.py:392
  89.4 1.2 %copy-done.10 = bf16[2,8,32,1024]{3,2,1,0:T(8,128)(2,1)S(1)} copy-done((bf16[2,8,32,1024]{3,2,1,0:T(8,128)(2,1)S(1)}, bf16[2,8,32,1024]{3,2,1,0:T(8,128)(2,1)}, u32[]{:S(2)}) %copy-start.10) | copy-done | bytes 1048600
  90.6 1.2 %copy-done.11 = bf16[2,8,32,1024]{3,2,1,0:T(8,128)(2,1)S(1)} copy-done((bf16[2,8,32,1024]{3,2,1,0:T(8,128)(2,1)S(1)}, bf16[2,8,32,1024]{3,2,1,0:T(8,128)(2,1)}, u32[]{:S(2)}) %copy-start.11) | copy-done | bytes 1048600
  91.8 12.9 %series.1 = (f32[1024,512]{1,0:T(8,128)}, f32[1,1]{1,0:T(1,128)}) custom-call(bf16[2,8,32,1024]{3,2,1,0:T(8,128)(2,1)S(1)} %copy-done.8, bf16[2,8,32,1024]{3,2,1,0:T(8,128)(2,1)S(1)} %get-tuple-element.25.s1, bf16[2,8,32,1024]{3,2,1,0:T(8,128)(2,1)S(1)} %copy-done.10, bf16[2,8,32,1024]{3,2,1,0:T(8,128)(2,1)S(1)} %copy-done.11, ...), custom_call_target="tpu_custom_call" | custom-call | flops 3300000000 | bytes 13000000 | tf_op jit(solution)/shard_map/series/pallas_call | solution.py:330
  (59 shorter events, 7.2 us)
Async XLA Ops:
  0.6 22.2 %copy-start.12 = (s32[1,256]{1,0:T(1,128)S(1)}, s32[1,256]{1,0:T(1,128)}, u32[]{:S(2)}) copy-start(s32[1,256]{1,0:T(1,128)} %param.10) | copy-start | bytes 3076
  0.6 24.8 %copy-start.13 = (s32[1,256]{1,0:T(1,128)S(1)}, s32[1,256]{1,0:T(1,128)}, u32[]{:S(2)}) copy-start(s32[1,256]{1,0:T(1,128)} %param.11) | copy-start | bytes 3076
  0.7 10.6 %collective-permute-start.2 = (bf16[2,64,1024]{2,1,0:T(8,128)(2,1)}, bf16[2,64,1024]{2,1,0:T(8,128)(2,1)S(1)}, u32[]{:S(2)}, u32[]{:S(2)}) collective-permute-start(bf16[2,64,1024]{2,1,0:T(8,128)(2,1)} %bitcast.37), channel_id=1, source_target_pairs={{0,4},{1,5},{2,6},{3,7},{4,0},{5,1},{6,2},{7,3},{8,12},{9,13},{10,... | collective-permute-start | bytes 786440 | tf_op jit(solution)/shard_map/ppermute | solution.py:70
  4.3 12.0 %collective-permute-start.1 = (bf16[2,64,1024]{2,1,0:T(8,128)(2,1)}, bf16[2,64,1024]{2,1,0:T(8,128)(2,1)S(1)}, u32[]{:S(2)}, u32[]{:S(2)}) collective-permute-start(bf16[2,64,1024]{2,1,0:T(8,128)(2,1)} %bitcast.38), channel_id=1, source_target_pairs={{0,6},{1,7},{2,0},{3,1},{4,2},{5,3},{6,4},{7,5},{8,14},{9,15},{10,... | collective-permute-start | bytes 786440 | tf_op jit(solution)/shard_map/ppermute | solution.py:70
  5.2 14.7 %collective-permute-start = (bf16[2,64,1024]{2,1,0:T(8,128)(2,1)}, bf16[2,64,1024]{2,1,0:T(8,128)(2,1)S(1)}, u32[]{:S(2)}, u32[]{:S(2)}) collective-permute-start(bf16[2,64,1024]{2,1,0:T(8,128)(2,1)} %bitcast.39), channel_id=1, source_target_pairs={{0,2},{1,3},{2,4},{3,5},{4,6},{5,7},{6,0},{7,1},{8,10},{9,11},{10,... | collective-permute-start | bytes 786440 | tf_op jit(solution)/shard_map/ppermute | solution.py:70
  6.8 16.2 %collective-permute-start.6 = (bf16[2,32,1024]{2,1,0:T(8,128)(2,1)S(1)}, bf16[2,32,1024]{2,1,0:T(8,128)(2,1)S(1)}, u32[]{:S(2)}, u32[]{:S(2)}) collective-permute-start(bf16[2,32,1024]{2,1,0:T(8,128)(2,1)S(1)} %get-tuple-element.34), channel_id=1, source_target_pairs={{0,16},{8,24},{16,0},{24,8},{32,48},{40,56},{48,32},{56,40},{64,80... | collective-permute-start | bytes 393224 | tf_op jit(solution)/shard_map/ppermute | solution.py:65
  9.8 13.7 %collective-permute-start.5 = (bf16[2,32,1024]{2,1,0:T(8,128)(2,1)S(1)}, bf16[2,32,1024]{2,1,0:T(8,128)(2,1)S(1)}, u32[]{:S(2)}, u32[]{:S(2)}) collective-permute-start(bf16[2,32,1024]{2,1,0:T(8,128)(2,1)S(1)} %get-tuple-element.34), channel_id=1, source_target_pairs={{0,24},{8,0},{16,8},{24,16},{32,56},{40,32},{48,40},{56,48},{64,88... | collective-permute-start | bytes 393224 | tf_op jit(solution)/shard_map/ppermute | solution.py:65
  11.2 13.3 %collective-permute-start.4 = (bf16[2,32,1024]{2,1,0:T(8,128)(2,1)S(1)}, bf16[2,32,1024]{2,1,0:T(8,128)(2,1)S(1)}, u32[]{:S(2)}, u32[]{:S(2)}) collective-permute-start(bf16[2,32,1024]{2,1,0:T(8,128)(2,1)S(1)} %get-tuple-element.34), channel_id=1, source_target_pairs={{0,8},{8,16},{16,24},{24,0},{32,40},{40,48},{48,56},{56,32},{64,72... | collective-permute-start | bytes 393224 | tf_op jit(solution)/shard_map/ppermute | solution.py:65
  16.3 9.3 %collective-permute-start.9 = (bf16[2,32,1024]{2,1,0:T(8,128)(2,1)S(1)}, bf16[2,32,1024]{2,1,0:T(8,128)(2,1)S(1)}, u32[]{:S(2)}, u32[]{:S(2)}) collective-permute-start(bf16[2,32,1024]{2,1,0:T(8,128)(2,1)S(1)} %get-tuple-element.35), channel_id=1, source_target_pairs={{0,64},{8,72},{16,80},{24,88},{32,96},{40,104},{48,112},{56,120},{... | collective-permute-start | bytes 393224 | tf_op jit(solution)/shard_map/ppermute | solution.py:65
  21.0 49.5 %copy-start = (bf16[4,2,64,1024]{3,2,1,0:T(8,128)(2,1)}, bf16[4,2,64,1024]{3,2,1,0:T(8,128)(2,1)S(1)}, u32[]{:S(2)}) copy-start(bf16[4,2,64,1024]{3,2,1,0:T(8,128)(2,1)S(1)} %pad_maximum_fusion.refs_1_) | copy-start | bytes 3145732
  21.0 21.5 %collective-permute-start.3 = (bf16[4,2,64,1024]{3,2,1,0:T(8,128)(2,1)S(1)}, bf16[4,2,64,1024]{3,2,1,0:T(8,128)(2,1)S(1)}, u32[]{:S(2)}, u32[]{:S(2)}) collective-permute-start(bf16[4,2,64,1024]{3,2,1,0:T(8,128)(2,1)S(1)} %pad_maximum_fusion.refs_1_), channel_id=1, source_target_pairs={{0,1},{1,0},{2,3},{3,2},{4,5},{5,4},{6,7},{7,6},{8,9},{9,8},{10,11... | collective-permute-start | bytes 3145736 | tf_op jit(solution)/shard_map/ppermute | solution.py:70
  23.0 5.2 %collective-permute-start.8 = (bf16[2,32,1024]{2,1,0:T(8,128)(2,1)S(1)}, bf16[2,32,1024]{2,1,0:T(8,128)(2,1)S(1)}, u32[]{:S(2)}, u32[]{:S(2)}) collective-permute-start(bf16[2,32,1024]{2,1,0:T(8,128)(2,1)S(1)} %get-tuple-element.35), channel_id=1, source_target_pairs={{0,96},{8,104},{16,112},{24,120},{32,0},{40,8},{48,16},{56,24},{64... | collective-permute-start | bytes 393224 | tf_op jit(solution)/shard_map/ppermute | solution.py:65
  23.5 6.0 %collective-permute-start.7 = (bf16[2,32,1024]{2,1,0:T(8,128)(2,1)S(1)}, bf16[2,32,1024]{2,1,0:T(8,128)(2,1)S(1)}, u32[]{:S(2)}, u32[]{:S(2)}) collective-permute-start(bf16[2,32,1024]{2,1,0:T(8,128)(2,1)S(1)} %get-tuple-element.35), channel_id=1, source_target_pairs={{0,32},{8,40},{16,48},{24,56},{32,64},{40,72},{48,80},{56,88},{64,... | collective-permute-start | bytes 393224 | tf_op jit(solution)/shard_map/ppermute | solution.py:65
  24.6 16.2 %collective-permute-start.10 = (bf16[4,2,32,1024]{3,2,1,0:T(8,128)(2,1)S(1)}, bf16[4,2,32,1024]{3,2,1,0:T(8,128)(2,1)S(1)}, u32[]{:S(2)}, u32[]{:S(2)}) collective-permute-start(bf16[4,2,32,1024]{3,2,1,0:T(8,128)(2,1)S(1)} %pad_maximum_fusion.1.refs_7_), channel_id=1, source_target_pairs={{0,32},{8,40},{16,48},{24,56},{32,64},{40,72},{48,80},{56,88},{64,... | collective-permute-start | bytes 1572872 | tf_op jit(solution)/shard_map/ppermute | solution.py:65
  25.6 45.9 %collective-permute-start.12 = (bf16[4,2,32,1024]{3,2,1,0:T(8,128)(2,1)S(1)}, bf16[4,2,32,1024]{3,2,1,0:T(8,128)(2,1)}, u32[]{:S(2)}, u32[]{:S(2)}) collective-permute-start(bf16[4,2,32,1024]{3,2,1,0:T(8,128)(2,1)S(1)} %pad_maximum_fusion.1.refs_7_), channel_id=1, source_target_pairs={{0,96},{8,104},{16,112},{24,120},{32,0},{40,8},{48,16},{56,24},{64... | collective-permute-start | bytes 1572872 | tf_op jit(solution)/shard_map/ppermute | solution.py:65
  29.6 41.9 %collective-permute-start.11 = (bf16[4,2,32,1024]{3,2,1,0:T(8,128)(2,1)S(1)}, bf16[4,2,32,1024]{3,2,1,0:T(8,128)(2,1)}, u32[]{:S(2)}, u32[]{:S(2)}) collective-permute-start(bf16[4,2,32,1024]{3,2,1,0:T(8,128)(2,1)S(1)} %pad_maximum_fusion.2.refs_8_), channel_id=1, source_target_pairs={{0,8},{8,16},{16,24},{24,0},{32,40},{40,48},{48,56},{56,32},{64,72... | collective-permute-start | bytes 1572872 | tf_op jit(solution)/shard_map/ppermute | solution.py:65
  30.9 40.6 %collective-permute-start.13 = (bf16[4,2,32,1024]{3,2,1,0:T(8,128)(2,1)S(1)}, bf16[4,2,32,1024]{3,2,1,0:T(8,128)(2,1)}, u32[]{:S(2)}, u32[]{:S(2)}) collective-permute-start(bf16[4,2,32,1024]{3,2,1,0:T(8,128)(2,1)S(1)} %pad_maximum_fusion.2.refs_8_), channel_id=1, source_target_pairs={{0,24},{8,0},{16,8},{24,16},{32,56},{40,32},{48,40},{56,48},{64,88... | collective-permute-start | bytes 1572872 | tf_op jit(solution)/shard_map/ppermute | solution.py:65
  40.8 0.8 copy-start.4
  41.6 29.9 %collective-permute-start.14 = (bf16[4,2,32,1024]{3,2,1,0:T(8,128)(2,1)S(1)}, bf16[4,2,32,1024]{3,2,1,0:T(8,128)(2,1)}, u32[]{:S(2)}, u32[]{:S(2)}) collective-permute-start(bf16[4,2,32,1024]{3,2,1,0:T(8,128)(2,1)S(1)} %pad_maximum_fusion.1.refs_7_), channel_id=1, source_target_pairs={{0,64},{8,72},{16,80},{24,88},{32,96},{40,104},{48,112},{56,120},{... | collective-permute-start | bytes 1572872 | tf_op jit(solution)/shard_map/ppermute | solution.py:65
  42.5 28.0 %copy-start.1 = (bf16[4,2,64,1024]{3,2,1,0:T(8,128)(2,1)}, bf16[4,2,64,1024]{3,2,1,0:T(8,128)(2,1)S(1)}, u32[]{:S(2)}) copy-start(bf16[4,2,64,1024]{3,2,1,0:T(8,128)(2,1)S(1)} %collective-permute-done.3.refs_2_) | copy-start | bytes 3145732
  42.5 29.0 %collective-permute-start.15 = (bf16[4,2,32,1024]{3,2,1,0:T(8,128)(2,1)S(1)}, bf16[4,2,32,1024]{3,2,1,0:T(8,128)(2,1)}, u32[]{:S(2)}, u32[]{:S(2)}) collective-permute-start(bf16[4,2,32,1024]{3,2,1,0:T(8,128)(2,1)S(1)} %pad_maximum_fusion.2.refs_8_), channel_id=1, source_target_pairs={{0,16},{8,24},{16,0},{24,8},{32,48},{40,56},{48,32},{56,40},{64,80... | collective-permute-start | bytes 1572872 | tf_op jit(solution)/shard_map/ppermute | solution.py:65
  46.2 16.9 %all-to-all-start = ((s32[128,1,2]{2,1,0:T(1,128)}), s32[128,1,2]{2,1,0:T(1,128)S(1)}, u32[]{:S(2)}, u32[]{:S(2)}) async-start(s32[128,1,2]{2,1,0:T(1,128)} %bitcast.12), calls=%async_computation | async-start | bytes 131072 | tf_op jit(solution)/shard_map/all_to_all | solution.py:380
  65.4 1.0 copy-start.3
  66.3 4.1 %copy-start.2 = (bf16[1024,512]{1,0:T(8,128)(2,1)}, bf16[1024,512]{1,0:T(8,128)(2,1)S(1)}, u32[]{:S(2)}) copy-start(bf16[1024,512]{1,0:T(8,128)(2,1)S(1)} %get-tuple-element.18.refs_3_) | copy-start | bytes 3145732
  66.3 5.2 %copy-start.5 = (bf16[4,2,32,1024]{3,2,1,0:T(8,128)(2,1)S(1)}, bf16[4,2,32,1024]{3,2,1,0:T(8,128)(2,1)}, u32[]{:S(2)}) copy-start(bf16[4,2,32,1024]{3,2,1,0:T(8,128)(2,1)} %copy-done.4) | copy-start | bytes 1572868
  70.5 1.0 copy-start.7
  71.5 17.8 %copy-start.6 = (bf16[4,256,256]{2,1,0:T(8,128)(2,1)S(1)}, bf16[4,256,256]{2,1,0:T(8,128)(2,1)}, u32[]{:S(2)}) copy-start(bf16[4,256,256]{2,1,0:T(8,128)(2,1)} %dynamic-slice_bitcast_fusion.rows_ref) | copy-start | bytes 1572868
  71.5 17.8 %copy-start.8 = (bf16[2,8,32,1024]{3,2,1,0:T(8,128)(2,1)S(1)}, bf16[2,8,32,1024]{3,2,1,0:T(8,128)(2,1)}, u32[]{:S(2)}) copy-start(bf16[2,8,32,1024]{3,2,1,0:T(8,128)(2,1)} %copy-done.7) | copy-start | bytes 3145732
  82.9 1.0 copy-start.9
  84.8 19.9 %all-to-all-start.1 = ((f32[2,128,2]{2,0,1:T(2,128)}), f32[2,128,2]{2,0,1:T(2,128)S(1)}, u32[]{:S(2)}, u32[]{:S(2)}) async-start(f32[2,128,2]{2,0,1:T(2,128)} %copy.24), calls=%async_computation.1 | async-start | bytes 262144 | tf_op jit(solution)/shard_map/all_to_all | solution.py:392
  89.3 1.2 %copy-start.10 = (bf16[2,8,32,1024]{3,2,1,0:T(8,128)(2,1)S(1)}, bf16[2,8,32,1024]{3,2,1,0:T(8,128)(2,1)}, u32[]{:S(2)}) copy-start(bf16[2,8,32,1024]{3,2,1,0:T(8,128)(2,1)} %copy-done.9) | copy-start | bytes 3145732
  90.6 1.2 %copy-start.11 = (bf16[2,8,32,1024]{3,2,1,0:T(8,128)(2,1)S(1)}, bf16[2,8,32,1024]{3,2,1,0:T(8,128)(2,1)}, u32[]{:S(2)}) copy-start(bf16[2,8,32,1024]{3,2,1,0:T(8,128)(2,1)} %get-tuple-element.27.s3) | copy-start | bytes 3145732
where the time goes:
time: 106 us
  starting transfers between devices  38 us (36%)
  Pallas kernels  29.2 us (28%)
  waiting for transfers between devices  22 us (21%)
  local copies, waits for them, and re-layouts  12.1 us (11%)
  other arithmetic  2.78 us (3%)
  between operations  1.59 us (2%)
    ppermute x12, starting transfers between devices, along_tmpl(): return lax.ppermute(x, 'tmpl', pairs)  19.1 us
    pallas_call x2, Pallas kernels, veto(): pl.pallas_call(functools.partial(veto_kernel, zones, len(before) // 2, fi...  15.5 us
    pallas_call x1, Pallas kernels, series(): pl.pallas_call(series_kernel, out_shape=(jax.ShapeDtypeStruct((COLS, ROWS...  12.9 us
    ppermute x12, waiting for transfers between devices, along_tmpl(): return lax.ppermute(x, 'tmpl', pairs)  10.3 us
    all_to_all x1, starting transfers between devices, shards(): lax.all_to_all(outgoing.reshape(device_total, slots_each), ('tmpl', 'seg'...  7.39 us
    all_to_all x1, waiting for transfers between devices, shards(): lax.all_to_all(outgoing.reshape(device_total, slots_each), ('tmpl', 'seg'...  7.38 us
    ppermute x4, starting transfers between devices, along_seg(): return lax.ppermute(x, 'seg', pairs)  6.93 us
    unnamed x28, local copies, waits for them, and re-layouts  6.2 us
  transfers between devices with their start and end apart: 18, of which 5 were waited for; matrix products, arithmetic and copies ran while one was open for 7% of the time, Pallas kernels for 17%

commit v1 on v0

v1 whole, which is shorter than its diff:
```python
import functools
import math

import jax
import jax.numpy as jnp
import numpy as np
import ml_dtypes
from jax import lax
from jax.experimental import pallas as pl
from jax.experimental.pallas import tpu as pltpu
from jax.sharding import PartitionSpec as P

BANDS = 16
ROWS = 512
COLS = 1024
BINS = ROWS * COLS
BLOCK = 32
SLOTS = 256
PAIRS = 128
F32 = jnp.float32
BF16 = jnp.bfloat16
VMEM = pl.BlockSpec(memory_space=pltpu.VMEM)
SMEM = pl.BlockSpec(memory_space=pltpu.SMEM)
LIMIT = 48 * 1024 * 1024


def unit(numerator, modulus):
    angle = 2.0 * math.pi * (np.asarray(numerator, np.int64) % modulus) / modulus
    return np.cos(angle), np.sin(angle)


def row_matrices():
    out = np.zeros((4, 256, 256), np.float32)
    n = np.arange(128)
    for p in range(4):
        c, s = unit(n[None, :] * (4 * n[:, None] + p), ROWS)
        out[p] = np.block([[c, -s], [s, c]])
    return out.astype(ml_dtypes.bfloat16)


def col_matrices():
    out = np.zeros((4, 512, 512), np.float32)
    n = np.arange(256)
    for p in range(4):
        c, s = unit(n[:, None] * (4 * n[None, :] + p), COLS)
        out[p] = np.block([[c, s], [-s, c]])
    return out.astype(ml_dtypes.bfloat16)


def twiddles():
    out = np.zeros((4, 2, 128, COLS), np.float32)
    u = np.arange(128)
    for p in range(4):
        c, s = unit((4 * u[:, None] + p) * np.arange(COLS)[None, :], BINS)
        out[p, 0], out[p, 1] = c, s
    return out


def swap(x, *moves):
    pairs = []
    for z in range(4):
        for y in range(4):
            for k in range(4):
                for core in range(2):
                    axis, mask = moves[core]
                    to = {
                        "z": (z ^ mask, y, k, core),
                        "y": (z, y ^ mask, k, core),
                        "x": (z, y, k ^ mask, core),
                        "core": (z, y, k, core ^ mask),
                    }[axis]
                    number = lambda v: ((v[0] * 4 + v[1]) * 4 + v[2]) * 2 + v[3]
                    pairs.append((number((z, y, k, core)), number(to)))
    return lax.ppermute(x, ("tmpl", "seg"), pairs)


def distance(position, swapped):
    apart = position ^ (position >> 1)
    return jnp.where(swapped, (4 - apart) & 3, apart)


def order_kernel(place, own_ref, other_ref, out_ref, power_ref):
    x, core = place[2], place[3]
    for turned, ref in enumerate((own_ref, other_ref)):
        holder = core ^ turned

        def one(position, carry, ref=ref, holder=holder):
            rank = 2 * (x ^ distance(position, holder == 1)) + holder
            for half in range(2):
                total = jnp.zeros((8, 128), F32)
                for part in range(2):
                    h = ref[position, part, pl.ds(32 * half, 32), :]
                    out_ref[part, pl.ds(pl.multiple_of(64 * rank + 32 * half, 32), 32), :] = h
                    h = h.astype(F32)
                    power = h * h
                    for r in range(0, 32, 8):
                        for c in range(0, COLS, 128):
                            total = total + power[r : r + 8, c : c + 128]
                whole = jnp.sum(total, axis=(0, 1), keepdims=True)
                power_ref[pl.ds(2 * rank + half, 1), :] = jnp.broadcast_to(whole, (1, SLOTS))
            return carry

        lax.fori_loop(0, 4, one, 0)


def order_template(place, own, other):
    return pl.pallas_call(
        order_kernel,
        out_shape=(
            jax.ShapeDtypeStruct((2, ROWS, COLS), BF16),
            jax.ShapeDtypeStruct((BANDS, SLOTS), F32),
        ),
        in_specs=[SMEM, VMEM, VMEM],
        out_specs=(VMEM, VMEM),
        compiler_params=pltpu.CompilerParams(vmem_limit_bytes=12 * 1024 * 1024),
        cost_estimate=pl.CostEstimate(flops=3_000_000, bytes_accessed=4_000_000, transcendentals=0),
        name="order_template",
    )(place, own, other)


def list_masks(pair_ref, count_ref):
    shape = (PAIRS, SLOTS)
    row = lax.broadcasted_iota(jnp.int32, shape, 1).astype(F32)
    owner = lax.broadcasted_iota(jnp.int32, shape, 0)
    hit = (pair_ref[...] == owner) & (row < count_ref[0].astype(F32))
    low = jnp.min(jnp.where(hit, row, 1e6), axis=1, keepdims=True)
    high = jnp.max(jnp.where(hit, row, -1.0), axis=1, keepdims=True)
    return hit & (row == low), hit & (row == high) & (high > low)


def send_kernel(pair_ref, time_ref, count_ref, out_ref):
    times = time_ref[...].astype(F32) + 1.0
    lane = lax.broadcasted_iota(jnp.int32, (PAIRS, 128), 1)
    out = jnp.zeros((PAIRS, 128), F32)
    for slot, mask in enumerate(list_masks(pair_ref, count_ref)):
        value = jnp.sum(jnp.where(mask, times, 0.0), axis=1, keepdims=True)
        out = jnp.where(lane == slot, value, out)
    out_ref[...] = out.astype(jnp.int32) - 1


def send_lists(pairs, times, counts):
    return pl.pallas_call(
        send_kernel,
        out_shape=jax.ShapeDtypeStruct((PAIRS, 128), jnp.int32),
        in_specs=[VMEM, VMEM, SMEM],
        out_specs=VMEM,
        cost_estimate=pl.CostEstimate(flops=500_000, bytes_accessed=70_000, transcendentals=0),
        name="send_lists",
    )(pairs, times, counts)


def take_kernel(pair_ref, count_ref, back_ref, chi_ref, snr_ref):
    first, second = list_masks(pair_ref, count_ref)
    for part, out_ref in enumerate((chi_ref, snr_ref)):
        one = jnp.where(first, back_ref[:, 2 * part : 2 * part + 1], 0.0)
        two = jnp.where(second, back_ref[:, 2 * part + 1 : 2 * part + 2], 0.0)
        out_ref[...] = jnp.sum(one + two, axis=0, keepdims=True)


def take_results(pairs, counts, back):
    return pl.pallas_call(
        take_kernel,
        out_shape=(jax.ShapeDtypeStruct((1, SLOTS), F32),) * 2,
        in_specs=[VMEM, SMEM, VMEM],
        out_specs=(VMEM, VMEM),
        cost_estimate=pl.CostEstimate(flops=500_000, bytes_accessed=70_000, transcendentals=0),
        name="take_results",
    )(pairs, counts, back)


def angle_parts(numerator, modulus):
    angles = (2.0 * math.pi / modulus) * (numerator & (modulus - 1)).astype(F32)
    return jnp.cos(angles), jnp.sin(angles)


def probe_kernel(list_ref, one_ref, two_ref, shift_ref, band_ref, time_ref):
    lists = list_ref[...].astype(F32).T
    t = jnp.concatenate([lists[0:1], lists[1:2]], axis=1).astype(jnp.int32)
    time_ref[...] = t
    t = jnp.maximum(t, 0)
    step = lax.broadcasted_iota(jnp.int32, (32, SLOTS), 0)
    low_r, low_i = angle_parts(step * t, BINS)
    high_r, high_i = angle_parts(step * 32 * t, BINS)
    shift_ref[0], shift_ref[1] = angle_parts(step * t, ROWS)
    band_ref[0], band_ref[1] = angle_parts(step[:BANDS] * t, BANDS)
    for h in range(32):
        hr, hi = high_r[h : h + 1], high_i[h : h + 1]
        pr = (hr * low_r - hi * low_i).astype(BF16)
        pi = (hr * low_i + hi * low_r).astype(BF16)
        rows = pl.ds(32 * h, 32)
        one_ref[rows, :SLOTS] = pr
        one_ref[rows, SLOTS:] = pi
        two_ref[rows, :SLOTS] = -pi
        two_ref[rows, SLOTS:] = pr


def probes(lists):
    return pl.pallas_call(
        probe_kernel,
        out_shape=(
            jax.ShapeDtypeStruct((COLS, 2 * SLOTS), BF16),
            jax.ShapeDtypeStruct((COLS, 2 * SLOTS), BF16),
            jax.ShapeDtypeStruct((2, 32, SLOTS), F32),
            jax.ShapeDtypeStruct((2, BANDS, SLOTS), F32),
            jax.ShapeDtypeStruct((1, SLOTS), jnp.int32),
        ),
        in_specs=[VMEM],
        out_specs=(VMEM,) * 5,
        compiler_params=pltpu.CompilerParams(vmem_limit_bytes=LIMIT),
        cost_estimate=pl.CostEstimate(flops=4_000_000, bytes_accessed=2_200_000, transcendentals=60_000),
        name="probes",
    )(lists)


def block_place(place, det, late, early):
    z, y, core = place[0], place[1], place[3]
    late, early = distance(late, core == 1), distance(early, core == 1)
    return (z ^ late, y ^ early) if det == 0 else (z ^ early, y ^ late)


def spectra_kernel(half, place, template_ref, part0, part1, spec):
    for det, part in enumerate((part0, part1)):

        def one_block(m, carry, det=det, part=part):
            zz, yy = block_place(place, det, 2 * half + (m >> 2), m & 3)
            rows = pl.ds(pl.multiple_of(128 * zz + 32 * yy, 32), 32)
            for lane in range(0, COLS, 256):
                cols = pl.ds(lane, 256)
                hr = template_ref[0, rows, cols].astype(F32)
                hi = template_ref[1, rows, cols].astype(F32)
                xr = part[m, 0, :, cols].astype(F32)
                xi = part[m, 1, :, cols].astype(F32)
                spec[0, 8 * det + m, :, cols] = (hr * xr + hi * xi).astype(BF16)
                spec[1, 8 * det + m, :, cols] = (hr * xi - hi * xr).astype(BF16)
            return carry

        lax.fori_loop(0, 8, one_block, 0, unroll=2)


def spectra(half, place, template, parts):
    return pl.pallas_call(
        functools.partial(spectra_kernel, half),
        out_shape=jax.ShapeDtypeStruct((2, 16, 32, COLS), BF16),
        in_specs=[SMEM, VMEM, VMEM, VMEM],
        out_specs=VMEM,
        compiler_params=pltpu.CompilerParams(vmem_limit_bytes=12 * 1024 * 1024),
        cost_estimate=pl.CostEstimate(flops=3_000_000, bytes_accessed=6_000_000, transcendentals=0),
        name=("spectra_early", "spectra_late")[half],
    )(place, template, *parts)


def veto_kernel(place, power_ref, time_ref, one_ref, two_ref, shift_ref, band_ref, s0, s1, result_ref, sum_ref):
    sr, si = shift_ref[0], shift_ref[1]
    for half, spec in enumerate((s0, s1)):
        out = jnp.dot(spec[0].reshape(512, COLS), one_ref[...], preferred_element_type=F32)
        out = out + jnp.dot(spec[1].reshape(512, COLS), two_ref[...], preferred_element_type=F32)
        for det in range(2):
            for m in range(8):
                i = 8 * det + m
                yr = out[32 * i : 32 * i + 32, :SLOTS]
                yi = out[32 * i : 32 * i + 32, SLOTS:]
                ar = jnp.sum(yr * sr - yi * si, axis=0, keepdims=True)
                ai = jnp.sum(yr * si + yi * sr, axis=0, keepdims=True)
                zz, yy = block_place(place, det, 2 * half + (m >> 2), m & 3)
                band = 4 * zz + yy
                er = band_ref[0, pl.ds(band, 1), :]
                ei = band_ref[1, pl.ds(band, 1), :]
                sum_ref[pl.ds(BANDS * det + band, 1), :SLOTS] = ar * er - ai * ei
                sum_ref[pl.ds(BANDS * det + band, 1), SLOTS:] = ar * ei + ai * er
    power = power_ref[...]
    sigma = jnp.sum(power, axis=0, keepdims=True)
    weight = power / sigma
    chi = jnp.zeros((1, SLOTS), F32)
    snr = jnp.zeros((1, SLOTS), F32)
    for det in range(2):
        rows = pl.ds(BANDS * det, BANDS)
        br, bi = sum_ref[rows, :SLOTS], sum_ref[rows, SLOTS:]
        tr = jnp.sum(br, axis=0, keepdims=True)
        ti = jnp.sum(bi, axis=0, keepdims=True)
        dr = br - weight * tr
        di = bi - weight * ti
        chi = chi + jnp.sum((dr * dr + di * di) / (weight * sigma), axis=0, keepdims=True)
        snr = snr + (tr * tr + ti * ti)
    usable = time_ref[...] >= 0
    chi = jnp.where(usable, chi / (4.0 * (BANDS - 1)), 0.0)
    snr = jnp.where(usable, snr / (2.0 * sigma), 0.0)
    lines = [chi[:, :128], chi[:, 128:], snr[:, :128], snr[:, 128:], sigma[:, :128], jnp.zeros((123, 128), F32)]
    result_ref[...] = jnp.concatenate(lines, axis=0).T


def veto(place, power, times, tables, specs):
    return pl.pallas_call(
        veto_kernel,
        out_shape=jax.ShapeDtypeStruct((PAIRS, 128), F32),
        in_specs=[SMEM] + [VMEM] * 8,
        out_specs=VMEM,
        scratch_shapes=[pltpu.VMEM((2 * BANDS, 2 * SLOTS), F32)],
        compiler_params=pltpu.CompilerParams(vmem_limit_bytes=20 * 1024 * 1024),
        cost_estimate=pl.CostEstimate(
            flops=2_200_000_000, bytes_accessed=6_000_000, transcendentals=0
        ),
        name="veto",
    )(place, power, times, *tables, *specs)


def series_kernel(
    place, s0_hbm, s1_hbm, result_hbm, rows_hbm, turn_hbm, cols_hbm, out_ref, peak_ref,
    s0, s1, sigma_ref, rows_ref, turn_ref, cols_ref, x_ref, g_ref, w_ref, v_ref, t_ref, o_ref, sems,
):
    copies = [
        pltpu.make_async_copy(src, dst, sems.at[k])
        for k, (src, dst) in enumerate(
            (
                (s0_hbm.at[:, :8], s0.at[:, :8]),
                (s1_hbm.at[:, :8], s1.at[:, :8]),
                (s0_hbm.at[:, 8:], s0.at[:, 8:]),
                (s1_hbm.at[:, 8:], s1.at[:, 8:]),
                (rows_hbm, rows_ref),
                (turn_hbm, turn_ref),
                (cols_hbm, cols_ref),
                (result_hbm.at[:8], sigma_ref),
            )
        )
    ]
    for copy in copies:
        copy.start()
    specs = (s0, s1)
    z, y, core = place[0], place[1], place[3]

    def four(q):
        (r0, i0), (r1, i1), (r2, i2), (r3, i3) = q
        ar, ai = r0 + r2, i0 + i2
        br, bi = r1 + r3, i1 + i3
        cr, ci = r0 - r2, i0 - i2
        dr, di = r1 - r3, i1 - i3
        return (
            (ar + br, ai + bi),
            (cr - di, ci + dr),
            (ar - br, ai - bi),
            (cr + di, ci - dr),
        )

    turned = ((z & 1) ^ core) == 1

    def fold(det, yy, load):
        def chunk(k, carry):
            cols = pl.ds(pl.multiple_of(k * 256, 256), 256)
            q = [(load(o, 0, cols).astype(F32), load(o, 1, cols).astype(F32)) for o in (0, 1, 3, 2)]
            for p, (re, im) in enumerate(four(q)):
                to = jnp.where(turned, (4 - p) & 3, p)
                x_ref[det, to, pl.ds(pl.multiple_of(32 * yy, 32), 32), cols] = re.astype(BF16)
                x_ref[det, to, pl.ds(pl.multiple_of(128 + 32 * yy, 32), 32), cols] = im.astype(BF16)
            return carry

        lax.fori_loop(0, 4, chunk, 0)

    for det in range(2):
        copies[2 * det].wait()
        copies[2 * det + 1].wait()

        for m in range(4):
            if det == 0:
                load = lambda o, k, cols: specs[o >> 1][k, 4 * (o & 1) + m, :, cols]
            else:
                load = lambda o, k, cols: specs[m >> 1][k, 8 + 4 * (m & 1) + o, :, cols]
            fold(det, y ^ distance(m, core == 1), load)

    copies[4].wait()
    copies[5].wait()

    def first(step):
        g_ref[step % 2] = jnp.dot(
            rows_ref[step % 4], x_ref[step // 4, step % 4], preferred_element_type=F32
        )

    def turn(step):
        det, p = divmod(step, 4)
        for r in range(0, 128, 16):
            h = []
            for j in range(4):
                cols = pl.ds(256 * j, 256)
                gr = g_ref[step % 2, pl.ds(r, 16), cols]
                gi = g_ref[step % 2, pl.ds(128 + r, 16), cols]
                tr = turn_ref[p, 0, pl.ds(r, 16), cols]
                ti = turn_ref[p, 1, pl.ds(r, 16), cols]
                h.append((gr * tr - gi * ti, gr * ti + gi * tr))
            rows = pl.ds(128 * p + r, 16)
            for k, (re, im) in enumerate(four(h)):
                w_ref[k, det, rows, :256] = re.astype(BF16)
                w_ref[k, det, rows, 256:] = im.astype(BF16)

    first(0)
    for step in range(8):
        if step < 7:
            first(step + 1)
        turn(step)
    copies[6].wait()
    copies[7].wait()

    scale = 1.0 / (2.0 * sigma_ref[0, 4])

    def second(k):
        for det in range(2):
            v_ref[k % 2, det] = jnp.dot(w_ref[k, det], cols_ref[k], preferred_element_type=F32)

    def power(k, best):
        for p in range(4):
            for r in range(0, 128, 16):
                rows = pl.ds(128 * p + r, 16)
                v = [
                    v_ref[k % 2, det, rows, pl.ds(256 * part, 256)]
                    for det in range(2)
                    for part in range(2)
                ]
                total = (v[0] * v[0] + v[1] * v[1] + v[2] * v[2] + v[3] * v[3]) * scale
                best = jnp.maximum(best, jnp.maximum(total[:8], total[8:]))
                for half in range(2):
                    t_ref[2 * k + half, pl.ds(4 * r + p, 16, stride=4), :] = total[
                        :, 128 * half : 128 * half + 128
                    ]
        return best

    best = jnp.zeros((8, 256), F32)
    second(0)
    for k in range(4):
        if k < 3:
            second(k + 1)
        best = power(k, best)
    peak_ref[...] = jnp.max(best, axis=(0, 1), keepdims=True)
    for k in range(4):
        for half in range(2):
            for i in range(4):
                tile = t_ref[2 * k + half, pl.ds(128 * i, 128), :]
                o_ref[i, pl.ds(512 * half + k, 128, stride=4), :] = tile.T
    for i in range(4):
        out_ref[:, pl.ds(128 * i, 128)] = o_ref[i]


def series(place, specs, result, rows, turns, cols):
    hbm = pl.BlockSpec(memory_space=pltpu.HBM)
    return pl.pallas_call(
        series_kernel,
        out_shape=(
            jax.ShapeDtypeStruct((COLS, ROWS), F32),
            jax.ShapeDtypeStruct((1, 1), F32),
        ),
        in_specs=[SMEM] + [hbm] * 6,
        out_specs=(VMEM, VMEM),
        scratch_shapes=[
            pltpu.VMEM(specs[0].shape, BF16),
            pltpu.VMEM(specs[1].shape, BF16),
            pltpu.VMEM((8, 128), F32),
            pltpu.VMEM(rows.shape, rows.dtype),
            pltpu.VMEM(turns.shape, turns.dtype),
            pltpu.VMEM(cols.shape, cols.dtype),
            pltpu.VMEM((2, 4, 256, COLS), BF16),
            pltpu.VMEM((2, 256, COLS), F32),
            pltpu.VMEM((4, 2, ROWS, 512), BF16),
            pltpu.VMEM((2, 2, ROWS, 512), F32),
            pltpu.VMEM((8, ROWS, 128), F32),
            pltpu.VMEM((4, COLS, 128), F32),
            pltpu.SemaphoreType.DMA((8,)),
        ],
        compiler_params=pltpu.CompilerParams(vmem_limit_bytes=60 * 1024 * 1024),
        cost_estimate=pl.CostEstimate(
            flops=3_300_000_000, bytes_accessed=13_000_000, transcendentals=0
        ),
        name="series",
    )(place, *specs, result, rows, turns, cols)


def shards(strain, templates, trig_pair, trig_time, trig_counts):
    device = lax.axis_index("tmpl")
    seat = lax.axis_index("seg")
    place = jnp.stack([device // 4, device % 4, seat // 2, seat % 2]).astype(jnp.int32)

    a, b = strain[:, 0, 0][None], strain[:, 1, 0][None]
    t = templates[:, 0][None]
    outgoing = send_lists(trig_pair, trig_time, trig_counts)
    incoming = lax.all_to_all(
        outgoing, ("tmpl", "seg"), split_axis=0, concat_axis=0, tiled=True
    )
    for step, (near, far) in enumerate(((1, 3), (3, 1), (1, 3), (3, 1))):
        if step == 2:
            a, b, incoming = lax.optimization_barrier((a, b, incoming))
        more_a = swap(a, ("yyzz"[step], near), ("yyzz"[step], far))
        more_b = swap(b, ("zzyy"[step], near), ("zzyy"[step], far))
        if step < 2:
            t = jnp.concatenate([t, swap(t, ("x", near), ("x", far))])
        if step < 3:
            a, b = jnp.concatenate([a, more_a]), jnp.concatenate([b, more_b])
    other_t = swap(t, ("core", 1), ("core", 1))

    template, power = order_template(place, t, other_t)
    specs = spectra(0, place, template, (a, b)), spectra(1, place, template, (more_a, more_b))
    *tables, times = probes(incoming)
    result = veto(place, power, times, tables, specs)
    back = lax.all_to_all(result, ("tmpl", "seg"), split_axis=0, concat_axis=0, tiled=True)
    snr_series, peak = series(
        place,
        specs,
        result,
        jnp.asarray(row_matrices()),
        jnp.asarray(twiddles()),
        jnp.asarray(col_matrices()),
    )
    chi, snr = take_results(trig_pair, trig_counts, back)
    return (snr_series[None, None], peak, chi, snr)


def solution(mesh):
    in_specs = (
        P(None, None, "seg", "tmpl", None),
        P(None, "tmpl", "seg", None),
        P(("tmpl", "seg"), None),
        P(("tmpl", "seg"), None),
        P(("tmpl", "seg")),
    )
    out_specs = (
        P("tmpl", "seg", None, None),
        P("tmpl", "seg"),
        P(("tmpl", "seg"), None),
        P(("tmpl", "seg"), None),
    )
    return jax.shard_map(shards, mesh=mesh, in_specs=in_specs, out_specs=out_specs, check_vma=False)
```

time: 106 us -> 85 us (0.80)
  starting transfers between devices: 38 us -> 28.1 us
  local copies, waits for them, and re-layouts: 12.1 us -> 3.93 us
  Pallas kernels: 29.2 us -> 25.8 us
  other arithmetic: 2.78 us -> 4.09 us
    ppermute x16 -> x11, starting transfers between devices: 26.1 us -> 14 us  [swap(): return lax.ppermute(x, ('tmpl', 'seg'), pairs)]
    concatenate x0 -> x6, other arithmetic: none -> 4.01 us  [the longest x2 2.24 us: shards(): t = jnp.concatenate([t, swap(t, ('x', near), ('x', far))])]
    unnamed x28 -> x16, local copies, waits for them, and re-layouts: 6.2 us -> 2.87 us
    all_to_all x2, starting transfers between devices: 11.9 us -> 14.2 us  [the longest x1 7.12 us: shards(): lax.all_to_all(outgoing, ('tmpl', 'seg'), split_axis=0, concat_axis=0, ti...]
    all_to_all x2, waiting for transfers between devices: 7.38 us -> 5.26 us  [the longest x1 5.25 us: shards(): lax.all_to_all(outgoing, ('tmpl', 'seg'), split_axis=0, concat_axis=0, ti...]
    squeeze x1 -> x0, local copies, waits for them, and re-layouts: 1.88 us -> none  [shards(): lax.dynamic_index_in_dim(jnp.asarray(row_matrices()), device % 4, 0, keep...]
    pallas_call x1, Pallas kernels: 12.9 us -> 11.1 us  [series(): pl.pallas_call(series_kernel, out_shape=(jax.ShapeDtypeStruct((COLS, ROWS...]
    pallas_call x2 -> x6, Pallas kernels: 15.5 us -> 13.9 us  [the longest x1 3.88 us: veto(): pl.pallas_call(veto_kernel, out_shape=jax.ShapeDtypeStruct((PAIRS, 128),...]
  transfers between devices with their start and end apart: 18 -> 13, of which waited for: 5 -> 6; matrix products, arithmetic and copies ran while one was open for 7% -> 8% of each run, Pallas kernels for 17% -> 21%
where the time goes in v1:
time: 85 us; the launch traced here: 84.5 us
  starting transfers between devices  28.1 us (33%)
  Pallas kernels  25.8 us (30%)
  waiting for transfers between devices  21 us (25%)
  other arithmetic  4.09 us (5%)
  local copies, waits for them, and re-layouts  3.93 us (5%)
  between operations  1.55 us (2%)
    ppermute x11, waiting for transfers between devices, swap(): return lax.ppermute(x, ('tmpl', 'seg'), pairs)  15.8 us
    ppermute x11, starting transfers between devices, swap(): return lax.ppermute(x, ('tmpl', 'seg'), pairs)  14 us
    pallas_call x1, Pallas kernels, series(): pl.pallas_call(series_kernel, out_shape=(jax.ShapeDtypeStruct((COLS, ROWS...  11.1 us
    all_to_all x1, starting transfers between devices, shards(): lax.all_to_all(outgoing, ('tmpl', 'seg'), split_axis=0, concat_axis=0, ti...  7.12 us
    all_to_all x1, starting transfers between devices, shards(): lax.all_to_all(result, ('tmpl', 'seg'), split_axis=0, concat_axis=0, tile...  7.06 us
    all_to_all x1, waiting for transfers between devices, shards(): lax.all_to_all(outgoing, ('tmpl', 'seg'), split_axis=0, concat_axis=0, ti...  5.25 us
    pallas_call x1, Pallas kernels, veto(): pl.pallas_call(veto_kernel, out_shape=jax.ShapeDtypeStruct((PAIRS, 128),...  3.88 us
    pallas_call x2, Pallas kernels, spectra(): pl.pallas_call(functools.partial(spectra_kernel, half), out_shape=jax.Sha...  3.8 us
  transfers between devices with their start and end apart: 13, of which 6 were waited for; matrix products, arithmetic and copies ran while one was open for 8% of the time, Pallas kernels for 21%

profile of v1, /device:TPU:1, one launch (start us, length us, event | category | flops | bytes accessed | tf_op | source)
XLA Modules:
  0.0 84.5 jit_solution(7357949602619279395)
XLA Ops:
  0.6 1.0 %slice_bitcast_fusion = (bf16[1,2,32,1024]{3,2,1,0:T(8,128)(2,1)S(1)}, bf16[1,2,32,1024]{3,2,1,0:T(8,128)(2,1)S(1)}) fusion(bf16[2,2,1,32,1024]{4,3,2,1,0:T(8,128)(2,1)} %param.8), kind=kLoop, calls=%fused_computation.6 | loop fusion | bytes 524288 | tf_op jit(solution)/shard_map/broadcast_in_dim;squeeze | solution.py:477
  1.6 4.7 %collective-permute-start.5 = (bf16[1,2,32,1024]{3,2,1,0:T(8,128)(2,1)S(1)}, bf16[1,2,32,1024]{3,2,1,0:T(8,128)(2,1)S(1)}, u32[]{:S(2)}, u32[]{:S(2)}) collective-permute-start(bf16[1,2,32,1024]{3,2,1,0:T(8,128)(2,1)S(1)} %get-tuple-element.32), channel_id=1, source_target_pairs={{0,32},{1,97},{2,34},{3,99},{4,36},{5,101},{6,38},{7,103},{8,40},{... | collective-permute-start | bytes 393224 | tf_op jit(solution)/shard_map/ppermute | solution.py:74
  6.3 2.5 %collective-permute-start = (bf16[1,2,64,1024]{3,2,1,0:T(8,128)(2,1)}, bf16[1,2,64,1024]{3,2,1,0:T(8,128)(2,1)S(1)}, u32[]{:S(2)}, u32[]{:S(2)}) collective-permute-start(bf16[1,2,64,1024]{3,2,1,0:T(8,128)(2,1)} %bitcast.23), channel_id=1, source_target_pairs={{0,2},{1,7},{2,0},{3,5},{4,6},{5,3},{6,4},{7,1},{8,10},{9,15},{10,... | collective-permute-start | bytes 786440 | tf_op jit(solution)/shard_map/ppermute | solution.py:74
  8.8 2.7 %collective-permute-start.3 = (bf16[1,2,32,1024]{3,2,1,0:T(8,128)(2,1)S(1)}, bf16[1,2,32,1024]{3,2,1,0:T(8,128)(2,1)S(1)}, u32[]{:S(2)}, u32[]{:S(2)}) collective-permute-start(bf16[1,2,32,1024]{3,2,1,0:T(8,128)(2,1)S(1)} %get-tuple-element.33), channel_id=1, source_target_pairs={{0,8},{1,25},{2,10},{3,27},{4,12},{5,29},{6,14},{7,31},{8,0},{9,17... | collective-permute-start | bytes 393224 | tf_op jit(solution)/shard_map/ppermute | solution.py:74
  11.6 2.5 %collective-permute-done.3 = bf16[1,2,32,1024]{3,2,1,0:T(8,128)(2,1)S(1)} collective-permute-done((bf16[1,2,32,1024]{3,2,1,0:T(8,128)(2,1)S(1)}, bf16[1,2,32,1024]{3,2,1,0:T(8,128)(2,1)S(1)}, u32[]{:S(2)}, u32[]{:S(2)}) %collective-permute-start.3) | collective-permute-done | bytes 131104 | tf_op jit(solution)/shard_map/ppermute | solution.py:74
  14.9 1.5 %send_lists.1 = s32[128,128]{1,0:T(8,128)} custom-call(s32[1,256]{1,0:T(1,128)} %pair_ref.3, s32[1,256]{1,0:T(1,128)} %time_ref.1, s32[1]{0:T(128)S(6)} %copy.22.count_ref), custom_call_target="tpu_custom_call" | custom-call | flops 500000 | bytes 70000 | tf_op jit(solution)/shard_map/send_lists/pallas_call | solution.py:142
  16.5 7.1 %all-to-all-start = ((s32[128,1,128]{2,1,0:T(1,128)}), s32[128,1,128]{2,1,0:T(1,128)S(1)}, u32[]{:S(2)}, u32[]{:S(2)}) async-start(s32[128,1,128]{2,1,0:T(1,128)} %bitcast.26), calls=%async_computation | async-start | bytes 131072 | tf_op jit(solution)/shard_map/all_to_all | solution.py:480
  23.6 1.1 %pad_maximum_fusion.1 = bf16[2,2,64,1024]{3,2,1,0:T(8,128)(2,1)S(1)} fusion(bf16[1,2,64,1024]{3,2,1,0:T(8,128)(2,1)S(1)} %collective-permute-done, bf16[1,2,64,1024]{3,2,1,0:T(8,128)(2,1)} %bitcast.24), kind=kLoop, calls=%fused_computation.1 | loop fusion | flops 262144 | bytes 1048576 | tf_op jit(solution)/shard_map/concatenate | solution.py:489
  24.7 1.5 %collective-permute-start.1 = (bf16[2,2,64,1024]{3,2,1,0:T(8,128)(2,1)S(1)}, bf16[2,2,64,1024]{3,2,1,0:T(8,128)(2,1)}, u32[]{:S(2)}, u32[]{:S(2)}) collective-permute-start(bf16[2,2,64,1024]{3,2,1,0:T(8,128)(2,1)S(1)} %pad_maximum_fusion.1), channel_id=1, source_target_pairs={{0,6},{1,3},{2,4},{3,1},{4,2},{5,7},{6,0},{7,5},{8,14},{9,11},{10,... | collective-permute-start | bytes 1572872 | tf_op jit(solution)/shard_map/ppermute | solution.py:74
  26.2 0.9 %pad_maximum_fusion.3 = bf16[4,2,32,1024]{3,2,1,0:T(8,128)(2,1)} fusion(bf16[2,2,32,1024]{3,2,1,0:T(8,128)(2,1)S(1)} %collective-permute-done.6, bf16[1,2,32,1024]{3,2,1,0:T(8,128)(2,1)S(1)} %collective-permute-done.5, bf16[1,2,32,1024]{3,2,1,0:T(8,128)(2,1)S(1)} %get-tuple-element.32), kind=kLoop, calls=%fused_computation.3 | loop fusion | flops 524288 | bytes 1048576 | tf_op jit(solution)/shard_map/concatenate | solution.py:491
  27.1 0.8 %pad_maximum_fusion.2 = bf16[4,2,32,1024]{3,2,1,0:T(8,128)(2,1)} fusion(bf16[2,2,32,1024]{3,2,1,0:T(8,128)(2,1)S(1)} %collective-permute-done.4, bf16[1,2,32,1024]{3,2,1,0:T(8,128)(2,1)S(1)} %collective-permute-done.3, bf16[1,2,32,1024]{3,2,1,0:T(8,128)(2,1)S(1)} %get-tuple-element.33), kind=kLoop, calls=%fused_computation.2 | loop fusion | flops 524288 | bytes 1048576 | tf_op jit(solution)/shard_map/concatenate | solution.py:491
  27.9 5.3 %all-to-all-done = s32[128,1,128]{2,1,0:T(1,128)S(1)} async-done(((s32[128,1,128]{2,1,0:T(1,128)}), s32[128,1,128]{2,1,0:T(1,128)S(1)}, u32[]{:S(2)}, u32[]{:S(2)}) %all-to-all-start) | async-done | bytes 65568 | tf_op jit(solution)/shard_map/all_to_all | solution.py:480
  33.2 0.9 %collective-permute-start.8 = (bf16[4,2,32,1024]{3,2,1,0:T(8,128)(2,1)}, bf16[4,2,32,1024]{3,2,1,0:T(8,128)(2,1)S(1)}, u32[]{:S(2)}, u32[]{:S(2)}) collective-permute-start(bf16[4,2,32,1024]{3,2,1,0:T(8,128)(2,1)} %pad_maximum_fusion.3), channel_id=1, source_target_pairs={{0,8},{1,25},{2,10},{3,27},{4,12},{5,29},{6,14},{7,31},{8,0},{9,17... | collective-permute-start | bytes 1572872 | tf_op jit(solution)/shard_map/ppermute | solution.py:74
  34.1 0.6 collective-permute-start.7
  34.7 1.1 %constant_dynamic-update-slice_fusion.1 = bf16[8,2,32,1024]{3,2,1,0:T(8,128)(2,1)S(1)} fusion(bf16[4,2,32,1024]{3,2,1,0:T(8,128)(2,1)} %pad_maximum_fusion.2), kind=kLoop, calls=%fused_computation.9 | loop fusion | bytes 1048576
  35.8 1.1 %constant_dynamic-update-slice_fusion.3 = bf16[8,2,32,1024]{3,2,1,0:T(8,128)(2,1)S(1)} fusion(bf16[4,2,32,1024]{3,2,1,0:T(8,128)(2,1)} %pad_maximum_fusion.3), kind=kLoop, calls=%fused_computation.11 | loop fusion | bytes 1048576
  36.9 1.1 %pad_maximum_fusion.own_ref = bf16[4,2,64,1024]{3,2,1,0:T(8,128)(2,1)S(1)} fusion(bf16[2,2,64,1024]{3,2,1,0:T(8,128)(2,1)} %collective-permute-done.1, bf16[1,2,64,1024]{3,2,1,0:T(8,128)(2,1)S(1)} %copy-done.5, bf16[1,2,64,1024]{3,2,1,0:T(8,128)(2,1)S(1)} %bitcast.25), kind=kLoop, calls=%fused_computation | loop fusion | flops 1048576 | bytes 2097152 | tf_op jit(solution)/shard_map/concatenate | solution.py:489
  38.1 0.8 collective-permute-start.2
  38.8 3.8 %collective-permute-done.8 = bf16[4,2,32,1024]{3,2,1,0:T(8,128)(2,1)S(1)} collective-permute-done((bf16[4,2,32,1024]{3,2,1,0:T(8,128)(2,1)}, bf16[4,2,32,1024]{3,2,1,0:T(8,128)(2,1)S(1)}, u32[]{:S(2)}, u32[]{:S(2)}) %collective-permute-start.8) | collective-permute-done | bytes 524320 | tf_op jit(solution)/shard_map/ppermute | solution.py:74
  42.7 0.8 collective-permute-done.7
  43.6 0.1 collective-permute-start.9
  43.8 0.8 probes.1
  44.6 3.0 %order_template.1 = (bf16[2,512,1024]{2,1,0:T(8,128)(2,1)S(1)}, f32[16,256]{1,0:T(8,128)S(1)}) custom-call(s32[4]{0:T(128)S(1)} %pad_add_fusion.place, bf16[4,2,64,1024]{3,2,1,0:T(8,128)(2,1)S(1)} %pad_maximum_fusion.own_ref, bf16[4,2,64,1024]{3,2,1,0:T(8,128)(2,1)} %collective-permute-done.2.other_ref), custom_call_target="tpu_custom_call" | custom-call | flops 3000000 | bytes 4000000 | tf_op jit(solution)/shard_map/order_template/pallas_call | solution.py:107
  47.6 1.4 %spectra_early.1.s0.s0_hbm = bf16[2,16,32,1024]{3,2,1,0:T(8,128)(2,1)S(1)} custom-call(s32[4]{0:T(128)S(1)} %pad_add_fusion.place, bf16[2,512,1024]{2,1,0:T(8,128)(2,1)S(1)} %get-tuple-element.18.template_ref, bf16[8,2,32,1024]{3,2,1,0:T(8,128)(2,1)S(1)} %constant_dynamic-update-slice_fusion.part0, ...), custom_call_target="tpu_custom_call" | custom-call | flops 3000000 | bytes 6000000 | tf_op jit(solution)/shard_map/spectra_early/pallas_call | solution.py:241
  49.0 7.8 %collective-permute-done.10.part1 = bf16[8,2,32,1024]{3,2,1,0:T(8,128)(2,1)} collective-permute-done((bf16[8,2,32,1024]{3,2,1,0:T(8,128)(2,1)S(1)}, bf16[8,2,32,1024]{3,2,1,0:T(8,128)(2,1)}, u32[]{:S(2)}, u32[]{:S(2)}) %collective-permute-start.10) | collective-permute-done | bytes 1048608 | tf_op jit(solution)/shard_map/ppermute | solution.py:74
  56.8 0.9 %collective-permute-done.9.part0 = bf16[8,2,32,1024]{3,2,1,0:T(8,128)(2,1)} collective-permute-done((bf16[8,2,32,1024]{3,2,1,0:T(8,128)(2,1)S(1)}, bf16[8,2,32,1024]{3,2,1,0:T(8,128)(2,1)}, u32[]{:S(2)}, u32[]{:S(2)}) %collective-permute-start.9) | collective-permute-done | bytes 1048608 | tf_op jit(solution)/shard_map/ppermute | solution.py:74
  57.7 2.4 %spectra_late.1.s1.s1_hbm = bf16[2,16,32,1024]{3,2,1,0:T(8,128)(2,1)S(1)} custom-call(s32[4]{0:T(128)S(1)} %pad_add_fusion.place, bf16[2,512,1024]{2,1,0:T(8,128)(2,1)S(1)} %get-tuple-element.18.template_ref, bf16[8,2,32,1024]{3,2,1,0:T(8,128)(2,1)} %collective-permute-done.9.part0, bf16[8,2,32,1024]{3,2,1,0:T(8,128)(2,1)} %collective-permute-done.10.part1), custom_call_target="tpu_custom_call" | custom-call | flops 3000000 | bytes 6000000 | tf_op jit(solution)/shard_map/spectra_late/pallas_call | solution.py:241
  60.1 3.9 %veto.1.result_hbm = f32[128,128]{1,0:T(8,128)} custom-call(s32[4]{0:T(128)S(1)} %pad_add_fusion.place, f32[16,256]{1,0:T(8,128)S(1)} %get-tuple-element.21.power_ref, s32[1,256]{1,0:T(1,128)S(1)} %get-tuple-element.23.time_ref, bf16[1024,512]{1,0:T(8,128)(2,1)S(1)} %get-tuple-element.24.one_ref, bf16[1024,512]{1,0:T(8,128)(2,1)S(1)} %get-tuple-element.25.two_ref, ...), custom_call_target="tpu_custom_call" | custom-call | flops 2200000000 | bytes 6000000 | tf_op jit(solution)/shard_map/veto/pallas_call | solution.py:292
  64.0 7.1 %all-to-all-start.1 = ((f32[128,1,128]{2,1,0:T(1,128)}), f32[128,1,128]{2,1,0:T(1,128)S(1)}, u32[]{:S(2)}, u32[]{:S(2)}) async-start(f32[128,1,128]{2,1,0:T(1,128)} %bitcast.12), calls=%async_computation.1 | async-start | bytes 131072 | tf_op jit(solution)/shard_map/all_to_all | solution.py:498
  71.1 11.1 %series.1 = (f32[1024,512]{1,0:T(8,128)}, f32[1,1]{1,0:T(1,128)}) custom-call(s32[4]{0:T(128)} %copy-done.2, bf16[2,16,32,1024]{3,2,1,0:T(8,128)(2,1)} %copy-done, bf16[2,16,32,1024]{3,2,1,0:T(8,128)(2,1)} %copy-done.1, f32[128,128]{1,0:T(8,128)} %veto.1.result_hbm, bf16[4,256,256]{2,1,0:T(8,128)(2,1)} %constant.57.clone.rows_hbm, ...), custom_call_target="tpu_custom_call" | custom-call | flops 3300000000 | bytes 13000000 | tf_op jit(solution)/shard_map/series/pallas_call | solution.py:441
  82.2 0.6 copy-done.6
  82.8 1.7 %take_results.1 = (f32[1,256]{1,0:T(1,128)}, f32[1,256]{1,0:T(1,128)}) custom-call(s32[1,256]{1,0:T(1,128)} %pair_ref.3, s32[1]{0:T(128)S(6)} %copy.22.count_ref, f32[128,128]{1,0:T(8,128)} %bitcast.27), custom_call_target="tpu_custom_call" | custom-call | flops 500000 | bytes 70000 | tf_op jit(solution)/shard_map/take_results/pallas_call | solution.py:161
  (28 shorter events, 0.5 us)
Async XLA Ops:
  1.6 9.9 %collective-permute-start.5 = (bf16[1,2,32,1024]{3,2,1,0:T(8,128)(2,1)S(1)}, bf16[1,2,32,1024]{3,2,1,0:T(8,128)(2,1)S(1)}, u32[]{:S(2)}, u32[]{:S(2)}) collective-permute-start(bf16[1,2,32,1024]{3,2,1,0:T(8,128)(2,1)S(1)} %get-tuple-element.32), channel_id=1, source_target_pairs={{0,32},{1,97},{2,34},{3,99},{4,36},{5,101},{6,38},{7,103},{8,40},{... | collective-permute-start | bytes 393224 | tf_op jit(solution)/shard_map/ppermute | solution.py:74
  6.3 17.3 %collective-permute-start = (bf16[1,2,64,1024]{3,2,1,0:T(8,128)(2,1)}, bf16[1,2,64,1024]{3,2,1,0:T(8,128)(2,1)S(1)}, u32[]{:S(2)}, u32[]{:S(2)}) collective-permute-start(bf16[1,2,64,1024]{3,2,1,0:T(8,128)(2,1)} %bitcast.23), channel_id=1, source_target_pairs={{0,2},{1,7},{2,0},{3,5},{4,6},{5,3},{6,4},{7,1},{8,10},{9,15},{10,... | collective-permute-start | bytes 786440 | tf_op jit(solution)/shard_map/ppermute | solution.py:74
  8.8 5.4 %collective-permute-start.3 = (bf16[1,2,32,1024]{3,2,1,0:T(8,128)(2,1)S(1)}, bf16[1,2,32,1024]{3,2,1,0:T(8,128)(2,1)S(1)}, u32[]{:S(2)}, u32[]{:S(2)}) collective-permute-start(bf16[1,2,32,1024]{3,2,1,0:T(8,128)(2,1)S(1)} %get-tuple-element.33), channel_id=1, source_target_pairs={{0,8},{1,25},{2,10},{3,27},{4,12},{5,29},{6,14},{7,31},{8,0},{9,17... | collective-permute-start | bytes 393224 | tf_op jit(solution)/shard_map/ppermute | solution.py:74
  11.5 14.6 %collective-permute-start.6 = (bf16[2,2,32,1024]{3,2,1,0:T(8,128)(2,1)S(1)}, bf16[2,2,32,1024]{3,2,1,0:T(8,128)(2,1)S(1)}, u32[]{:S(2)}, u32[]{:S(2)}) collective-permute-start(bf16[2,2,32,1024]{3,2,1,0:T(8,128)(2,1)S(1)} %pad_maximum_fusion.5), channel_id=1, source_target_pairs={{0,96},{1,33},{2,98},{3,35},{4,100},{5,37},{6,102},{7,39},{8,104},... | collective-permute-start | bytes 786440 | tf_op jit(solution)/shard_map/ppermute | solution.py:74
  14.2 12.9 %collective-permute-start.4 = (bf16[2,2,32,1024]{3,2,1,0:T(8,128)(2,1)S(1)}, bf16[2,2,32,1024]{3,2,1,0:T(8,128)(2,1)S(1)}, u32[]{:S(2)}, u32[]{:S(2)}) collective-permute-start(bf16[2,2,32,1024]{3,2,1,0:T(8,128)(2,1)S(1)} %pad_maximum_fusion.4), channel_id=1, source_target_pairs={{0,24},{1,9},{2,26},{3,11},{4,28},{5,13},{6,30},{7,15},{8,16},{9,1... | collective-permute-start | bytes 786440 | tf_op jit(solution)/shard_map/ppermute | solution.py:74
  16.5 16.7 %all-to-all-start = ((s32[128,1,128]{2,1,0:T(1,128)}), s32[128,1,128]{2,1,0:T(1,128)S(1)}, u32[]{:S(2)}, u32[]{:S(2)}) async-start(s32[128,1,128]{2,1,0:T(1,128)} %bitcast.26), calls=%async_computation | async-start | bytes 131072 | tf_op jit(solution)/shard_map/all_to_all | solution.py:480
  23.6 10.5 %copy-start.4 = (bf16[1,2,64,1024]{3,2,1,0:T(8,128)(2,1)}, bf16[1,2,64,1024]{3,2,1,0:T(8,128)(2,1)S(1)}, u32[]{:S(2)}) copy-start(bf16[1,2,64,1024]{3,2,1,0:T(8,128)(2,1)S(1)} %collective-permute-done) | copy-start | bytes 786436
  24.7 12.2 %copy-start.3 = (bf16[2,1,64,1024]{3,2,1,0:T(8,128)(2,1)S(1)}, bf16[2,1,64,1024]{3,2,1,0:T(8,128)(2,1)}, u32[]{:S(2)}) copy-start(bf16[2,1,64,1024]{3,2,1,0:T(8,128)(2,1)} %param.9) | copy-start | bytes 786436
  24.7 12.2 %collective-permute-start.1 = (bf16[2,2,64,1024]{3,2,1,0:T(8,128)(2,1)S(1)}, bf16[2,2,64,1024]{3,2,1,0:T(8,128)(2,1)}, u32[]{:S(2)}, u32[]{:S(2)}) collective-permute-start(bf16[2,2,64,1024]{3,2,1,0:T(8,128)(2,1)S(1)} %pad_maximum_fusion.1), channel_id=1, source_target_pairs={{0,6},{1,3},{2,4},{3,1},{4,2},{5,7},{6,0},{7,5},{8,14},{9,11},{10,... | collective-permute-start | bytes 1572872 | tf_op jit(solution)/shard_map/ppermute | solution.py:74
  33.2 9.5 %collective-permute-start.8 = (bf16[4,2,32,1024]{3,2,1,0:T(8,128)(2,1)}, bf16[4,2,32,1024]{3,2,1,0:T(8,128)(2,1)S(1)}, u32[]{:S(2)}, u32[]{:S(2)}) collective-permute-start(bf16[4,2,32,1024]{3,2,1,0:T(8,128)(2,1)} %pad_maximum_fusion.3), channel_id=1, source_target_pairs={{0,8},{1,25},{2,10},{3,27},{4,12},{5,29},{6,14},{7,31},{8,0},{9,17... | collective-permute-start | bytes 1572872 | tf_op jit(solution)/shard_map/ppermute | solution.py:74
  34.1 9.5 %collective-permute-start.7 = (bf16[4,2,32,1024]{3,2,1,0:T(8,128)(2,1)}, bf16[4,2,32,1024]{3,2,1,0:T(8,128)(2,1)S(1)}, u32[]{:S(2)}, u32[]{:S(2)}) collective-permute-start(bf16[4,2,32,1024]{3,2,1,0:T(8,128)(2,1)} %pad_maximum_fusion.2), channel_id=1, source_target_pairs={{0,32},{1,97},{2,34},{3,99},{4,36},{5,101},{6,38},{7,103},{8,40},{... | collective-permute-start | bytes 1572872 | tf_op jit(solution)/shard_map/ppermute | solution.py:74
  34.7 2.3 %copy-start.5 = (bf16[1,2,64,1024]{3,2,1,0:T(8,128)(2,1)S(1)}, bf16[1,2,64,1024]{3,2,1,0:T(8,128)(2,1)}, u32[]{:S(2)}) copy-start(bf16[1,2,64,1024]{3,2,1,0:T(8,128)(2,1)} %copy-done.4) | copy-start | bytes 786436
  38.1 6.5 %collective-permute-start.2 = (bf16[4,2,64,1024]{3,2,1,0:T(8,128)(2,1)S(1)}, bf16[4,2,64,1024]{3,2,1,0:T(8,128)(2,1)}, u32[]{:S(2)}, u32[]{:S(2)}) collective-permute-start(bf16[4,2,64,1024]{3,2,1,0:T(8,128)(2,1)S(1)} %pad_maximum_fusion.own_ref), channel_id=1, source_target_pairs={{0,1},{1,0},{2,3},{3,2},{4,5},{5,4},{6,7},{7,6},{8,9},{9,8},{10,11... | collective-permute-start | bytes 3145736 | tf_op jit(solution)/shard_map/ppermute | solution.py:74
  42.7 14.1 %collective-permute-start.10 = (bf16[8,2,32,1024]{3,2,1,0:T(8,128)(2,1)S(1)}, bf16[8,2,32,1024]{3,2,1,0:T(8,128)(2,1)}, u32[]{:S(2)}, u32[]{:S(2)}) collective-permute-start(bf16[8,2,32,1024]{3,2,1,0:T(8,128)(2,1)S(1)} %constant_dynamic-update-slice_fusion.2.part1), channel_id=1, source_target_pairs={{0,24},{1,9},{2,26},{3,11},{4,28},{5,13},{6,30},{7,15},{8,16},{9,1... | collective-permute-start | bytes 3145736 | tf_op jit(solution)/shard_map/ppermute | solution.py:74
  43.6 14.1 %collective-permute-start.9 = (bf16[8,2,32,1024]{3,2,1,0:T(8,128)(2,1)S(1)}, bf16[8,2,32,1024]{3,2,1,0:T(8,128)(2,1)}, u32[]{:S(2)}, u32[]{:S(2)}) collective-permute-start(bf16[8,2,32,1024]{3,2,1,0:T(8,128)(2,1)S(1)} %constant_dynamic-update-slice_fusion.part0), channel_id=1, source_target_pairs={{0,96},{1,33},{2,98},{3,35},{4,100},{5,37},{6,102},{7,39},{8,104},... | collective-permute-start | bytes 3145736 | tf_op jit(solution)/shard_map/ppermute | solution.py:74
  43.8 16.3 %copy-start.2 = (s32[4]{0:T(128)}, s32[4]{0:T(128)S(1)}, u32[]{:S(2)}) copy-start(s32[4]{0:T(128)S(1)} %pad_add_fusion.place) | copy-start | bytes 52
  49.0 11.1 %copy-start = (bf16[2,16,32,1024]{3,2,1,0:T(8,128)(2,1)}, bf16[2,16,32,1024]{3,2,1,0:T(8,128)(2,1)S(1)}, u32[]{:S(2)}) copy-start(bf16[2,16,32,1024]{3,2,1,0:T(8,128)(2,1)S(1)} %spectra_early.1.s0.s0_hbm) | copy-start | bytes 6291460
  60.1 3.9 %copy-start.1 = (bf16[2,16,32,1024]{3,2,1,0:T(8,128)(2,1)}, bf16[2,16,32,1024]{3,2,1,0:T(8,128)(2,1)S(1)}, u32[]{:S(2)}) copy-start(bf16[2,16,32,1024]{3,2,1,0:T(8,128)(2,1)S(1)} %spectra_late.1.s1.s1_hbm) | copy-start | bytes 6291460
  64.0 18.1 %all-to-all-start.1 = ((f32[128,1,128]{2,1,0:T(1,128)}), f32[128,1,128]{2,1,0:T(1,128)S(1)}, u32[]{:S(2)}, u32[]{:S(2)}) async-start(f32[128,1,128]{2,1,0:T(1,128)} %bitcast.12), calls=%async_computation.1 | async-start | bytes 131072 | tf_op jit(solution)/shard_map/all_to_all | solution.py:498
  82.2 0.6 copy-start.6

commit v2 on v1

--- a/solution.py
+++ b/solution.py
@@ -30,11 +30,12 @@
 
 
 def row_matrices():
-    out = np.zeros((4, 256, 256), np.float32)
+    out = np.zeros((4, 4, 256, 256), np.float32)
     n = np.arange(128)
     for p in range(4):
-        c, s = unit(n[None, :] * (4 * n[:, None] + p), ROWS)
-        out[p] = np.block([[c, -s], [s, c]])
+        for j in range(4):
+            c, s = unit((4 * n[None, :] + j) * (4 * n[:, None] + p), 4 * ROWS)
+            out[p, j] = np.block([[c, -s], [s, c]])
     return out.astype(ml_dtypes.bfloat16)
 
 
@@ -48,10 +49,10 @@
 
 
 def twiddles():
-    out = np.zeros((4, 2, 128, COLS), np.float32)
+    out = np.zeros((4, 2, 128, 256), np.float32)
     u = np.arange(128)
     for p in range(4):
-        c, s = unit((4 * u[:, None] + p) * np.arange(COLS)[None, :], BINS)
+        c, s = unit((4 * u[:, None] + p) * np.arange(256)[None, :], BINS)
         out[p, 0], out[p, 1] = c, s
     return out
 
@@ -79,6 +80,63 @@
     return jnp.where(swapped, (4 - apart) & 3, apart)
 
 
+def pack_kernel(template_ref, pair_ref, time_ref, count_ref, out_ref):
+    out_ref[0, :64] = template_ref[0]
+    out_ref[0, 64:128] = template_ref[1]
+    time = time_ref[...]
+    row = lax.broadcasted_iota(jnp.int32, (1, SLOTS), 1)
+    pair = jnp.where(row < count_ref[0], pair_ref[...], 255)
+    line = jnp.concatenate([pair, time >> 16, (time >> 8) & 255, time & 255], axis=1)
+    out_ref[0, 128:] = jnp.broadcast_to(line.astype(F32), (16, COLS)).astype(BF16)
+
+
+def pack_lists(template, pairs, times, counts):
+    return pl.pallas_call(
+        pack_kernel,
+        out_shape=jax.ShapeDtypeStruct((1, 144, COLS), BF16),
+        in_specs=[VMEM, VMEM, VMEM, SMEM],
+        out_specs=VMEM,
+        cost_estimate=pl.CostEstimate(flops=100_000, bytes_accessed=600_000, transcendentals=0),
+        name="pack_lists",
+    )(template, pairs, times, counts)
+
+
+def route_kernel(place, own_ref, other_ref, out_ref):
+    z, y, x, core = place[0], place[1], place[2], place[3]
+    seat = 2 * x + core
+    row = lax.broadcasted_iota(jnp.int32, (16, SLOTS), 1).astype(F32)
+    owner = (lax.broadcasted_iota(jnp.int32, (16, SLOTS), 0) * 8 + seat).astype(F32)
+    lane = lax.broadcasted_iota(jnp.int32, (16, SLOTS), 1)
+    out = jnp.zeros((16, SLOTS), F32)
+    for turned, ref in enumerate((own_ref, other_ref)):
+        holder = core ^ turned
+        for position in range(4):
+            line = ref[position, 128:144, :].astype(F32)[0:1]
+            pair, high, mid, low = [line[:, 256 * k : 256 * k + 256] for k in range(4)]
+            time = (high * 65536.0 + mid * 256.0 + low) + 1.0
+            hit = pair == owner
+            start = jnp.min(jnp.where(hit, row, 1e6), axis=1, keepdims=True)
+            end = jnp.max(jnp.where(hit, row, -1.0), axis=1, keepdims=True)
+            masks = (row == start, (row == end) & (end > start))
+            source = 8 * (4 * z + y) + 2 * (x ^ distance(position, holder == 1)) + holder
+            for slot, mask in enumerate(masks):
+                value = jnp.sum(jnp.where(mask, time, 0.0), axis=1, keepdims=True)
+                out = jnp.where(lane == PAIRS * slot + source, value, out)
+    out_ref[...] = out.astype(jnp.int32)
+
+
+def route_lists(place, own, other):
+    return pl.pallas_call(
+        route_kernel,
+        out_shape=jax.ShapeDtypeStruct((16, SLOTS), jnp.int32),
+        in_specs=[SMEM, VMEM, VMEM],
+        out_specs=VMEM,
+        compiler_params=pltpu.CompilerParams(vmem_limit_bytes=8 * 1024 * 1024),
+        cost_estimate=pl.CostEstimate(flops=1_000_000, bytes_accessed=300_000, transcendentals=0),
+        name="route_lists",
+    )(place, own, other)
+
+
 def order_kernel(place, own_ref, other_ref, out_ref, power_ref):
     x, core = place[2], place[3]
     for turned, ref in enumerate((own_ref, other_ref)):
@@ -89,7 +147,8 @@
             for half in range(2):
                 total = jnp.zeros((8, 128), F32)
                 for part in range(2):
-                    h = ref[position, part, pl.ds(32 * half, 32), :]
+                    rows = pl.ds(64 * part + 32 * half, 32)
+                    h = ref[position, rows, :]
                     out_ref[part, pl.ds(pl.multiple_of(64 * rank + 32 * half, 32), 32), :] = h
                     h = h.astype(F32)
                     power = h * h
@@ -128,27 +187,6 @@
     return hit & (row == low), hit & (row == high) & (high > low)
 
 
-def send_kernel(pair_ref, time_ref, count_ref, out_ref):
-    times = time_ref[...].astype(F32) + 1.0
-    lane = lax.broadcasted_iota(jnp.int32, (PAIRS, 128), 1)
-    out = jnp.zeros((PAIRS, 128), F32)
-    for slot, mask in enumerate(list_masks(pair_ref, count_ref)):
-        value = jnp.sum(jnp.where(mask, times, 0.0), axis=1, keepdims=True)
-        out = jnp.where(lane == slot, value, out)
-    out_ref[...] = out.astype(jnp.int32) - 1
-
-
-def send_lists(pairs, times, counts):
-    return pl.pallas_call(
-        send_kernel,
-        out_shape=jax.ShapeDtypeStruct((PAIRS, 128), jnp.int32),
-        in_specs=[VMEM, VMEM, SMEM],
-        out_specs=VMEM,
-        cost_estimate=pl.CostEstimate(flops=500_000, bytes_accessed=70_000, transcendentals=0),
-        name="send_lists",
-    )(pairs, times, counts)
-
-
 def take_kernel(pair_ref, count_ref, back_ref, chi_ref, snr_ref):
     first, second = list_masks(pair_ref, count_ref)
     for part, out_ref in enumerate((chi_ref, snr_ref)):
@@ -174,8 +212,7 @@
 
 
 def probe_kernel(list_ref, one_ref, two_ref, shift_ref, band_ref, time_ref):
-    lists = list_ref[...].astype(F32).T
-    t = jnp.concatenate([lists[0:1], lists[1:2]], axis=1).astype(jnp.int32)
+    t = jnp.sum(list_ref[...].astype(F32), axis=0, keepdims=True).astype(jnp.int32) - 1
     time_ref[...] = t
     t = jnp.maximum(t, 0)
     step = lax.broadcasted_iota(jnp.int32, (32, SLOTS), 0)
@@ -304,7 +341,7 @@
 
 
 def series_kernel(
-    place, s0_hbm, s1_hbm, result_hbm, rows_hbm, turn_hbm, cols_hbm, out_ref, peak_ref,
+    place, s0_hbm, s1_hbm, result_hbm, rows_hbm, turn_hbm, cols_hbm, out_hbm, peak_ref,
     s0, s1, sigma_ref, rows_ref, turn_ref, cols_ref, x_ref, g_ref, w_ref, v_ref, t_ref, o_ref, sems,
 ):
     copies = [
@@ -315,8 +352,14 @@
                 (s1_hbm.at[:, :8], s1.at[:, :8]),
                 (s0_hbm.at[:, 8:], s0.at[:, 8:]),
                 (s1_hbm.at[:, 8:], s1.at[:, 8:]),
-                (rows_hbm, rows_ref),
-                (turn_hbm, turn_ref),
+                *[
+                    pair
+                    for p in range(4)
+                    for pair in (
+                        (rows_hbm.at[p], rows_ref.at[p]),
+                        (turn_hbm.at[p], turn_ref.at[p]),
+                    )
+                ],
                 (cols_hbm, cols_ref),
                 (result_hbm.at[:8], sigma_ref),
             )
@@ -365,37 +408,38 @@
                 load = lambda o, k, cols: specs[m >> 1][k, 8 + 4 * (m & 1) + o, :, cols]
             fold(det, y ^ distance(m, core == 1), load)
 
-    copies[4].wait()
-    copies[5].wait()
-
     def first(step):
-        g_ref[step % 2] = jnp.dot(
-            rows_ref[step % 4], x_ref[step // 4, step % 4], preferred_element_type=F32
-        )
+        p, det = divmod(step, 2)
+        if det == 0:
+            copies[4 + 2 * p].wait()
+            copies[5 + 2 * p].wait()
+        for j in range(4):
+            cols = pl.ds(256 * j, 256)
+            g_ref[step % 2, :, cols] = jnp.dot(
+                rows_ref[p, j], x_ref[det, p, :, cols], preferred_element_type=F32
+            )
 
     def turn(step):
-        det, p = divmod(step, 4)
+        p, det = divmod(step, 2)
         for r in range(0, 128, 16):
             h = []
             for j in range(4):
                 cols = pl.ds(256 * j, 256)
-                gr = g_ref[step % 2, pl.ds(r, 16), cols]
-                gi = g_ref[step % 2, pl.ds(128 + r, 16), cols]
-                tr = turn_ref[p, 0, pl.ds(r, 16), cols]
-                ti = turn_ref[p, 1, pl.ds(r, 16), cols]
-                h.append((gr * tr - gi * ti, gr * ti + gi * tr))
+                h.append((g_ref[step % 2, pl.ds(r, 16), cols], g_ref[step % 2, pl.ds(128 + r, 16), cols]))
+            tr = turn_ref[p, 0, pl.ds(r, 16), :]
+            ti = turn_ref[p, 1, pl.ds(r, 16), :]
             rows = pl.ds(128 * p + r, 16)
             for k, (re, im) in enumerate(four(h)):
-                w_ref[k, det, rows, :256] = re.astype(BF16)
-                w_ref[k, det, rows, 256:] = im.astype(BF16)
+                w_ref[k, det, rows, :256] = (re * tr - im * ti).astype(BF16)
+                w_ref[k, det, rows, 256:] = (re * ti + im * tr).astype(BF16)
 
     first(0)
     for step in range(8):
         if step < 7:
             first(step + 1)
         turn(step)
-    copies[6].wait()
-    copies[7].wait()
+    copies[12].wait()
+    copies[13].wait()
 
     scale = 1.0 / (2.0 * sigma_ref[0, 4])
 
@@ -427,13 +471,18 @@
             second(k + 1)
         best = power(k, best)
     peak_ref[...] = jnp.max(best, axis=(0, 1), keepdims=True)
-    for k in range(4):
-        for half in range(2):
-            for i in range(4):
+    for i in range(4):
+        for k in range(4):
+            for half in range(2):
                 tile = t_ref[2 * k + half, pl.ds(128 * i, 128), :]
                 o_ref[i, pl.ds(512 * half + k, 128, stride=4), :] = tile.T
-    for i in range(4):
-        out_ref[:, pl.ds(128 * i, 128)] = o_ref[i]
+        copy = pltpu.make_async_copy(
+            o_ref.at[i], out_hbm.at[:, pl.ds(128 * i, 128)], sems.at[14 + i]
+        )
+        copy.start()
+        copies.append(copy)
+    for copy in copies[14:]:
+        copy.wait()
 
 
 def series(place, specs, result, rows, turns, cols):
@@ -445,7 +494,7 @@
             jax.ShapeDtypeStruct((1, 1), F32),
         ),
         in_specs=[SMEM] + [hbm] * 6,
-        out_specs=(VMEM, VMEM),
+        out_specs=(hbm, VMEM),
         scratch_shapes=[
             pltpu.VMEM(specs[0].shape, BF16),
             pltpu.VMEM(specs[1].shape, BF16),
@@ -459,7 +508,7 @@
             pltpu.VMEM((2, 2, ROWS, 512), F32),
             pltpu.VMEM((8, ROWS, 128), F32),
             pltpu.VMEM((4, COLS, 128), F32),
-            pltpu.SemaphoreType.DMA((8,)),
+            pltpu.SemaphoreType.DMA((18,)),
         ],
         compiler_params=pltpu.CompilerParams(vmem_limit_bytes=60 * 1024 * 1024),
         cost_estimate=pl.CostEstimate(
@@ -475,14 +524,8 @@
     place = jnp.stack([device // 4, device % 4, seat // 2, seat % 2]).astype(jnp.int32)
 
     a, b = strain[:, 0, 0][None], strain[:, 1, 0][None]
-    t = templates[:, 0][None]
-    outgoing = send_lists(trig_pair, trig_time, trig_counts)
-    incoming = lax.all_to_all(
-        outgoing, ("tmpl", "seg"), split_axis=0, concat_axis=0, tiled=True
-    )
+    t = pack_lists(templates[:, 0], trig_pair, trig_time, trig_counts)
     for step, (near, far) in enumerate(((1, 3), (3, 1), (1, 3), (3, 1))):
-        if step == 2:
-            a, b, incoming = lax.optimization_barrier((a, b, incoming))
         more_a = swap(a, ("yyzz"[step], near), ("yyzz"[step], far))
         more_b = swap(b, ("zzyy"[step], near), ("zzyy"[step], far))
         if step < 2:
@@ -491,7 +534,10 @@
             a, b = jnp.concatenate([a, more_a]), jnp.concatenate([b, more_b])
     other_t = swap(t, ("core", 1), ("core", 1))
 
+    outgoing = route_lists(place, t, other_t)
+    incoming = lax.all_to_all(outgoing, "tmpl", split_axis=0, concat_axis=0, tiled=True)
     template, power = order_template(place, t, other_t)
+    more_a, more_b, incoming = lax.optimization_barrier((more_a, more_b, incoming))
     specs = spectra(0, place, template, (a, b)), spectra(1, place, template, (more_a, more_b))
     *tables, times = probes(incoming)
     result = veto(place, power, times, tables, specs)

time: 85 us -> 82.9 us (0.975)
  waiting for transfers between devices: 21 us -> 14.5 us
  starting transfers between devices: 28.1 us -> 32.1 us
  other arithmetic: 4.09 us -> 2.55 us
  local copies, waits for them, and re-layouts: 3.93 us -> 5.08 us
  Pallas kernels: 25.8 us -> 26.7 us
    all_to_all x1, starting transfers between devices: 7.06 us -> 12.3 us  [shards(): lax.all_to_all(result, ('tmpl', 'seg'), split_axis=0, concat_axis=0, tile...]
    ppermute x11, waiting for transfers between devices: 15.8 us -> 12.2 us  [swap(): return lax.ppermute(x, ('tmpl', 'seg'), pairs)]
    all_to_all x1, waiting for transfers between devices: 5.25 us -> 2.3 us  [shards(): lax.all_to_all(outgoing, 'tmpl', split_axis=0, concat_axis=0, tiled=True)]
    concatenate x2, other arithmetic: 2.24 us -> 0.17 us  [shards(): t = jnp.concatenate([t, swap(t, ('x', near), ('x', far))])]
    pallas_call x2, Pallas kernels: 3.8 us -> 4.96 us  [spectra(): pl.pallas_call(functools.partial(spectra_kernel, half), out_shape=jax.Sha...]
    pallas_call x1 -> x2, Pallas kernels: 1.54 us -> 2.46 us  [the longest x1 1.71 us: pack_lists(): pl.pallas_call(pack_kernel, out_shape=jax.ShapeDtypeStruct((1, 144, COLS)...]
    all_to_all x1, starting transfers between devices: 7.12 us -> 6.23 us  [shards(): lax.all_to_all(outgoing, 'tmpl', split_axis=0, concat_axis=0, tiled=True)]
    unnamed x16 -> x17, local copies, waits for them, and re-layouts: 2.87 us -> 3.47 us
  transfers between devices with their start and end apart: 13 -> 13, of which waited for: 6 -> 6; matrix products, arithmetic and copies ran while one was open for 8% -> 4% of each run, Pallas kernels for 21% -> 22%
where the time goes in v2:
time: 82.9 us; the launch traced here: 82.5 us
  starting transfers between devices  32.1 us (39%)
  Pallas kernels  26.7 us (32%)
  waiting for transfers between devices  14.5 us (17%)
  local copies, waits for them, and re-layouts  5.08 us (6%)
  other arithmetic  2.55 us (3%)
  between operations  1.51 us (2%)
    ppermute x11, starting transfers between devices, swap(): return lax.ppermute(x, ('tmpl', 'seg'), pairs)  13.6 us
    all_to_all x1, starting transfers between devices, shards(): lax.all_to_all(result, ('tmpl', 'seg'), split_axis=0, concat_axis=0, tile...  12.3 us
    ppermute x11, waiting for transfers between devices, swap(): return lax.ppermute(x, ('tmpl', 'seg'), pairs)  12.2 us
    pallas_call x1, Pallas kernels, series(): pl.pallas_call(series_kernel, out_shape=(jax.ShapeDtypeStruct((COLS, ROWS...  10.7 us
    all_to_all x1, starting transfers between devices, shards(): lax.all_to_all(outgoing, 'tmpl', split_axis=0, concat_axis=0, tiled=True)  6.23 us
    pallas_call x2, Pallas kernels, spectra(): pl.pallas_call(functools.partial(spectra_kernel, half), out_shape=jax.Sha...  4.96 us
    pallas_call x1, Pallas kernels, veto(): pl.pallas_call(veto_kernel, out_shape=jax.ShapeDtypeStruct((PAIRS, 128),...  3.86 us
    unnamed x17, local copies, waits for them, and re-layouts  3.47 us
  transfers between devices with their start and end apart: 13, of which 6 were waited for; matrix products, arithmetic and copies ran while one was open for 4% of the time, Pallas kernels for 22%

profile of v2, /device:TPU:1, one launch (start us, length us, event | category | flops | bytes accessed | tf_op | source)
XLA Modules:
  0.0 82.5 jit_solution(12315702233512295684)
XLA Ops:
  0.6 1.0 %slice_bitcast_fusion = (bf16[1,2,32,1024]{3,2,1,0:T(8,128)(2,1)S(1)}, bf16[1,2,32,1024]{3,2,1,0:T(8,128)(2,1)S(1)}) fusion(bf16[2,2,1,32,1024]{4,3,2,1,0:T(8,128)(2,1)} %param.8), kind=kLoop, calls=%fused_computation.8 | loop fusion | bytes 524288 | tf_op jit(solution)/shard_map/broadcast_in_dim;squeeze | solution.py:526
  1.6 3.6 %collective-permute-start.3 = (bf16[1,2,32,1024]{3,2,1,0:T(8,128)(2,1)S(1)}, bf16[1,2,32,1024]{3,2,1,0:T(8,128)(2,1)S(1)}, u32[]{:S(2)}, u32[]{:S(2)}) collective-permute-start(bf16[1,2,32,1024]{3,2,1,0:T(8,128)(2,1)S(1)} %get-tuple-element.33), channel_id=1, source_target_pairs={{0,8},{1,25},{2,10},{3,27},{4,12},{5,29},{6,14},{7,31},{8,0},{9,17... | collective-permute-start | bytes 393224 | tf_op jit(solution)/shard_map/ppermute | solution.py:75
  5.9 1.7 %pack_lists.1 = bf16[1,144,1024]{2,1,0:T(8,128)(2,1)} custom-call(bf16[2,64,1024]{2,1,0:T(8,128)(2,1)} %bitcast.24, s32[1,256]{1,0:T(1,128)} %pair_ref.3, s32[1,256]{1,0:T(1,128)} %time_ref.1, s32[1]{0:T(128)S(6)} %copy.23.count_ref), custom_call_target="tpu_custom_call" | custom-call | flops 100000 | bytes 600000 | tf_op jit(solution)/shard_map/pack_lists/pallas_call | solution.py:94
  7.6 2.5 %collective-permute-start = (bf16[1,144,1024]{2,1,0:T(8,128)(2,1)}, bf16[1,144,1024]{2,1,0:T(8,128)(2,1)S(1)}, u32[]{:S(2)}, u32[]{:S(2)}) collective-permute-start(bf16[1,144,1024]{2,1,0:T(8,128)(2,1)} %pack_lists.1), channel_id=1, source_target_pairs={{0,2},{1,7},{2,0},{3,5},{4,6},{5,3},{6,4},{7,1},{8,10},{9,15},{10,... | collective-permute-start | bytes 884744 | tf_op jit(solution)/shard_map/ppermute | solution.py:75
  10.1 3.8 %collective-permute-start.6 = (bf16[1,2,32,1024]{3,2,1,0:T(8,128)(2,1)S(1)}, bf16[1,2,32,1024]{3,2,1,0:T(8,128)(2,1)S(1)}, u32[]{:S(2)}, u32[]{:S(2)}) collective-permute-start(bf16[1,2,32,1024]{3,2,1,0:T(8,128)(2,1)S(1)} %get-tuple-element.32), channel_id=1, source_target_pairs={{0,32},{1,97},{2,34},{3,99},{4,36},{5,101},{6,38},{7,103},{8,40},{... | collective-permute-start | bytes 393224 | tf_op jit(solution)/shard_map/ppermute | solution.py:75
  14.0 2.5 %collective-permute-done.6 = bf16[1,2,32,1024]{3,2,1,0:T(8,128)(2,1)S(1)} collective-permute-done((bf16[1,2,32,1024]{3,2,1,0:T(8,128)(2,1)S(1)}, bf16[1,2,32,1024]{3,2,1,0:T(8,128)(2,1)S(1)}, u32[]{:S(2)}, u32[]{:S(2)}) %collective-permute-start.6) | collective-permute-done | bytes 131104 | tf_op jit(solution)/shard_map/ppermute | solution.py:75
  16.8 2.7 %collective-permute-done.4 = bf16[2,2,32,1024]{3,2,1,0:T(8,128)(2,1)S(1)} collective-permute-done((bf16[2,2,32,1024]{3,2,1,0:T(8,128)(2,1)S(1)}, bf16[2,2,32,1024]{3,2,1,0:T(8,128)(2,1)S(1)}, u32[]{:S(2)}, u32[]{:S(2)}) %collective-permute-start.4) | collective-permute-done | bytes 262176 | tf_op jit(solution)/shard_map/ppermute | solution.py:75
  19.6 0.1 collective-permute-start.5
  19.6 2.2 %collective-permute-done.7 = bf16[2,2,32,1024]{3,2,1,0:T(8,128)(2,1)S(1)} collective-permute-done((bf16[2,2,32,1024]{3,2,1,0:T(8,128)(2,1)S(1)}, bf16[2,2,32,1024]{3,2,1,0:T(8,128)(2,1)S(1)}, u32[]{:S(2)}, u32[]{:S(2)}) %collective-permute-start.7) | collective-permute-done | bytes 262176 | tf_op jit(solution)/shard_map/ppermute | solution.py:75
  21.9 0.1 collective-permute-start.8
  22.0 3.8 %collective-permute-done.1 = bf16[2,144,1024]{2,1,0:T(8,128)(2,1)S(1)} collective-permute-done((bf16[2,144,1024]{2,1,0:T(8,128)(2,1)S(1)}, bf16[2,144,1024]{2,1,0:T(8,128)(2,1)S(1)}, u32[]{:S(2)}, u32[]{:S(2)}) %collective-permute-start.1) | collective-permute-done | bytes 589856 | tf_op jit(solution)/shard_map/ppermute | solution.py:75
  25.8 0.1 pad_maximum_fusion.own_ref
  26.0 3.2 %collective-permute-start.2 = (bf16[4,144,1024]{2,1,0:T(8,128)(2,1)S(1)}, bf16[4,144,1024]{2,1,0:T(8,128)(2,1)S(1)}, u32[]{:S(2)}, u32[]{:S(2)}) collective-permute-start(bf16[4,144,1024]{2,1,0:T(8,128)(2,1)S(1)} %pad_maximum_fusion.own_ref), channel_id=1, source_target_pairs={{0,1},{1,0},{2,3},{3,2},{4,5},{5,4},{6,7},{7,6},{8,9},{9,8},{10,11... | collective-permute-start | bytes 3538952 | tf_op jit(solution)/shard_map/ppermute | solution.py:75
  29.2 1.1 %pad_maximum_fusion.1.part0 = bf16[8,2,32,1024]{3,2,1,0:T(8,128)(2,1)} fusion(bf16[4,2,32,1024]{3,2,1,0:T(8,128)(2,1)S(1)} %collective-permute-done.5, bf16[2,2,32,1024]{3,2,1,0:T(8,128)(2,1)S(1)} %collective-permute-done.4, bf16[1,2,32,1024]{3,2,1,0:T(8,128)(2,1)S(1)} %collective-permute-done.3, bf16[1,2,32,1024]{3,2,1,0:T(8,128)(2,1)S(1)} %get-tuple-element.33), kind=kLoop, calls=%fused_computation.1 | loop fusion | flops 1572864 | bytes 2097152 | tf_op jit(solution)/shard_map/concatenate | solution.py:534
  30.3 1.0 %collective-permute-done.8 = bf16[4,2,32,1024]{3,2,1,0:T(8,128)(2,1)S(1)} collective-permute-done((bf16[4,2,32,1024]{3,2,1,0:T(8,128)(2,1)S(1)}, bf16[4,2,32,1024]{3,2,1,0:T(8,128)(2,1)S(1)}, u32[]{:S(2)}, u32[]{:S(2)}) %collective-permute-start.8) | collective-permute-done | bytes 524320 | tf_op jit(solution)/shard_map/ppermute | solution.py:75
  31.2 1.1 %pad_maximum_fusion.2.part1 = bf16[8,2,32,1024]{3,2,1,0:T(8,128)(2,1)} fusion(bf16[4,2,32,1024]{3,2,1,0:T(8,128)(2,1)S(1)} %collective-permute-done.8, bf16[2,2,32,1024]{3,2,1,0:T(8,128)(2,1)S(1)} %collective-permute-done.7, bf16[1,2,32,1024]{3,2,1,0:T(8,128)(2,1)S(1)} %collective-permute-done.6, bf16[1,2,32,1024]{3,2,1,0:T(8,128)(2,1)S(1)} %get-tuple-element.32), kind=kLoop, calls=%fused_computation.2 | loop fusion | flops 1572864 | bytes 2097152 | tf_op jit(solution)/shard_map/concatenate | solution.py:534
  32.4 0.7 route_lists.1
  33.2 0.3 copy-done
  33.4 0.6 copy.16
  34.0 6.2 %all-to-all-start = ((s32[16,1,256]{2,1,0:T(1,128)}), s32[16,1,256]{2,1,0:T(1,128)S(1)}, u32[]{:S(2)}, u32[]{:S(2)}) async-start(s32[16,1,256]{2,1,0:T(1,128)} %copy.16), calls=%async_computation | async-start | bytes 32768 | tf_op jit(solution)/shard_map/all_to_all | solution.py:538
  40.3 1.3 %copy-done.1 = bf16[4,144,1024]{2,1,0:T(8,128)(2,1)S(1)} copy-done((bf16[4,144,1024]{2,1,0:T(8,128)(2,1)S(1)}, bf16[4,144,1024]{2,1,0:T(8,128)(2,1)}, u32[]{:S(2)}) %copy-start.1) | copy-done | bytes 1179672
  41.5 2.3 %order_template.1 = (bf16[2,512,1024]{2,1,0:T(8,128)(2,1)S(1)}, f32[16,256]{1,0:T(8,128)S(1)}) custom-call(s32[4]{0:T(128)S(1)} %pad_add_fusion.place, bf16[4,144,1024]{2,1,0:T(8,128)(2,1)S(1)} %pad_maximum_fusion.own_ref, bf16[4,144,1024]{2,1,0:T(8,128)(2,1)S(1)} %copy-done.1), custom_call_target="tpu_custom_call" | custom-call | flops 3000000 | bytes 4000000 | tf_op jit(solution)/shard_map/order_template/pallas_call | solution.py:166
  43.8 2.4 %spectra_early.1.s0.s0_hbm = bf16[2,16,32,1024]{3,2,1,0:T(8,128)(2,1)S(1)} custom-call(s32[4]{0:T(128)S(1)} %pad_add_fusion.place, bf16[2,512,1024]{2,1,0:T(8,128)(2,1)S(1)} %get-tuple-element.18.template_ref, bf16[8,2,32,1024]{3,2,1,0:T(8,128)(2,1)} %pad_maximum_fusion.1.part0, bf16[8,2,32,1024]{3,2,1,0:T(8,128)(2,1)} %pad_maximum_fusion.2.part1), custom_call_target="tpu_custom_call" | custom-call | flops 3000000 | bytes 6000000 | tf_op jit(solution)/shard_map/spectra_early/pallas_call | solution.py:278
  46.3 1.3 %copy-done.2 = bf16[2,16,32,1024]{3,2,1,0:T(8,128)(2,1)} copy-done((bf16[2,16,32,1024]{3,2,1,0:T(8,128)(2,1)}, bf16[2,16,32,1024]{3,2,1,0:T(8,128)(2,1)S(1)}, u32[]{:S(2)}) %copy-start.2) | copy-done | bytes 2097176
  47.6 2.3 %all-to-all-done = s32[16,1,256]{2,1,0:T(1,128)S(1)} async-done(((s32[16,1,256]{2,1,0:T(1,128)}), s32[16,1,256]{2,1,0:T(1,128)S(1)}, u32[]{:S(2)}, u32[]{:S(2)}) %all-to-all-start) | async-done | bytes 16416 | tf_op jit(solution)/shard_map/all_to_all | solution.py:538
  49.9 0.8 probes.1
  50.7 2.6 %spectra_late.1.s1.s1_hbm = bf16[2,16,32,1024]{3,2,1,0:T(8,128)(2,1)S(1)} custom-call(s32[4]{0:T(128)S(1)} %pad_add_fusion.place, bf16[2,512,1024]{2,1,0:T(8,128)(2,1)S(1)} %get-tuple-element.18.template_ref, bf16[8,2,32,1024]{3,2,1,0:T(8,128)(2,1)} %collective-permute-done.9.part0, bf16[8,2,32,1024]{3,2,1,0:T(8,128)(2,1)} %collective-permute-done.10.part1), custom_call_target="tpu_custom_call" | custom-call | flops 3000000 | bytes 6000000 | tf_op jit(solution)/shard_map/spectra_late/pallas_call | solution.py:278
  53.3 3.9 %veto.1.result_hbm = f32[128,128]{1,0:T(8,128)} custom-call(s32[4]{0:T(128)S(1)} %pad_add_fusion.place, f32[16,256]{1,0:T(8,128)S(1)} %get-tuple-element.21.power_ref, s32[1,256]{1,0:T(1,128)S(1)} %get-tuple-element.23.time_ref, bf16[1024,512]{1,0:T(8,128)(2,1)S(1)} %get-tuple-element.24.one_ref, bf16[1024,512]{1,0:T(8,128)(2,1)S(1)} %get-tuple-element.25.two_ref, ...), custom_call_target="tpu_custom_call" | custom-call | flops 2200000000 | bytes 6000000 | tf_op jit(solution)/shard_map/veto/pallas_call | solution.py:329
  57.1 12.3 %all-to-all-start.1 = ((f32[128,1,128]{2,1,0:T(1,128)}), f32[128,1,128]{2,1,0:T(1,128)S(1)}, u32[]{:S(2)}, u32[]{:S(2)}) async-start(f32[128,1,128]{2,1,0:T(1,128)} %bitcast.10), calls=%async_computation.1 | async-start | bytes 131072 | tf_op jit(solution)/shard_map/all_to_all | solution.py:544
  69.4 10.7 %series.1 = (f32[1024,512]{1,0:T(8,128)}, f32[1,1]{1,0:T(1,128)}) custom-call(s32[4]{0:T(128)} %copy-done.5, bf16[2,16,32,1024]{3,2,1,0:T(8,128)(2,1)} %copy-done.2, bf16[2,16,32,1024]{3,2,1,0:T(8,128)(2,1)} %copy-done.4, f32[128,128]{1,0:T(8,128)} %veto.1.result_hbm, bf16[4,4,256,256]{3,2,1,0:T(8,128)(2,1)} %constant.57.clone.rows_hbm, ...), custom_call_target="tpu_custom_call" | custom-call | flops 3300000000 | bytes 13000000 | tf_op jit(solution)/shard_map/series/pallas_call | solution.py:490
  80.2 0.6 copy-done.7
  80.8 1.7 %take_results.1 = (f32[1,256]{1,0:T(1,128)}, f32[1,256]{1,0:T(1,128)}) custom-call(s32[1,256]{1,0:T(1,128)} %pair_ref.3, s32[1]{0:T(128)S(6)} %copy.23.count_ref, f32[128,128]{1,0:T(8,128)} %bitcast.25), custom_call_target="tpu_custom_call" | custom-call | flops 500000 | bytes 70000 | tf_op jit(solution)/shard_map/take_results/pallas_call | solution.py:199
  (31 shorter events, 0.6 us)
Async XLA Ops:
  1.6 12.2 %collective-permute-start.3 = (bf16[1,2,32,1024]{3,2,1,0:T(8,128)(2,1)S(1)}, bf16[1,2,32,1024]{3,2,1,0:T(8,128)(2,1)S(1)}, u32[]{:S(2)}, u32[]{:S(2)}) collective-permute-start(bf16[1,2,32,1024]{3,2,1,0:T(8,128)(2,1)S(1)} %get-tuple-element.33), channel_id=1, source_target_pairs={{0,8},{1,25},{2,10},{3,27},{4,12},{5,29},{6,14},{7,31},{8,0},{9,17... | collective-permute-start | bytes 393224 | tf_op jit(solution)/shard_map/ppermute | solution.py:75
  7.6 9.0 %copy-start.6 = (bf16[1,144,1024]{2,1,0:T(8,128)(2,1)S(1)}, bf16[1,144,1024]{2,1,0:T(8,128)(2,1)}, u32[]{:S(2)}) copy-start(bf16[1,144,1024]{2,1,0:T(8,128)(2,1)} %pack_lists.1) | copy-start | bytes 884740
  7.6 9.0 %collective-permute-start = (bf16[1,144,1024]{2,1,0:T(8,128)(2,1)}, bf16[1,144,1024]{2,1,0:T(8,128)(2,1)S(1)}, u32[]{:S(2)}, u32[]{:S(2)}) collective-permute-start(bf16[1,144,1024]{2,1,0:T(8,128)(2,1)} %pack_lists.1), channel_id=1, source_target_pairs={{0,2},{1,7},{2,0},{3,5},{4,6},{5,3},{6,4},{7,1},{8,10},{9,15},{10,... | collective-permute-start | bytes 884744 | tf_op jit(solution)/shard_map/ppermute | solution.py:75
  10.1 6.4 %collective-permute-start.6 = (bf16[1,2,32,1024]{3,2,1,0:T(8,128)(2,1)S(1)}, bf16[1,2,32,1024]{3,2,1,0:T(8,128)(2,1)S(1)}, u32[]{:S(2)}, u32[]{:S(2)}) collective-permute-start(bf16[1,2,32,1024]{3,2,1,0:T(8,128)(2,1)S(1)} %get-tuple-element.32), channel_id=1, source_target_pairs={{0,32},{1,97},{2,34},{3,99},{4,36},{5,101},{6,38},{7,103},{8,40},{... | collective-permute-start | bytes 393224 | tf_op jit(solution)/shard_map/ppermute | solution.py:75
  13.9 5.6 %collective-permute-start.4 = (bf16[2,2,32,1024]{3,2,1,0:T(8,128)(2,1)S(1)}, bf16[2,2,32,1024]{3,2,1,0:T(8,128)(2,1)S(1)}, u32[]{:S(2)}, u32[]{:S(2)}) collective-permute-start(bf16[2,2,32,1024]{3,2,1,0:T(8,128)(2,1)S(1)} %pad_maximum_fusion.6), channel_id=1, source_target_pairs={{0,24},{1,9},{2,26},{3,11},{4,28},{5,13},{6,30},{7,15},{8,16},{9,1... | collective-permute-start | bytes 786440 | tf_op jit(solution)/shard_map/ppermute | solution.py:75
  16.5 5.3 %collective-permute-start.7 = (bf16[2,2,32,1024]{3,2,1,0:T(8,128)(2,1)S(1)}, bf16[2,2,32,1024]{3,2,1,0:T(8,128)(2,1)S(1)}, u32[]{:S(2)}, u32[]{:S(2)}) collective-permute-start(bf16[2,2,32,1024]{3,2,1,0:T(8,128)(2,1)S(1)} %pad_maximum_fusion.7), channel_id=1, source_target_pairs={{0,96},{1,33},{2,98},{3,35},{4,100},{5,37},{6,102},{7,39},{8,104},... | collective-permute-start | bytes 786440 | tf_op jit(solution)/shard_map/ppermute | solution.py:75
  16.7 9.1 %collective-permute-start.1 = (bf16[2,144,1024]{2,1,0:T(8,128)(2,1)S(1)}, bf16[2,144,1024]{2,1,0:T(8,128)(2,1)S(1)}, u32[]{:S(2)}, u32[]{:S(2)}) collective-permute-start(bf16[2,144,1024]{2,1,0:T(8,128)(2,1)S(1)} %pad_maximum_fusion.3), channel_id=1, source_target_pairs={{0,6},{1,3},{2,4},{3,1},{4,2},{5,7},{6,0},{7,5},{8,14},{9,11},{10,... | collective-permute-start | bytes 1769480 | tf_op jit(solution)/shard_map/ppermute | solution.py:75
  19.6 9.6 %collective-permute-start.5 = (bf16[4,2,32,1024]{3,2,1,0:T(8,128)(2,1)S(1)}, bf16[4,2,32,1024]{3,2,1,0:T(8,128)(2,1)S(1)}, u32[]{:S(2)}, u32[]{:S(2)}) collective-permute-start(bf16[4,2,32,1024]{3,2,1,0:T(8,128)(2,1)S(1)} %pad_maximum_fusion.4), channel_id=1, source_target_pairs={{0,32},{1,97},{2,34},{3,99},{4,36},{5,101},{6,38},{7,103},{8,40},{... | collective-permute-start | bytes 1572872 | tf_op jit(solution)/shard_map/ppermute | solution.py:75
  21.9 9.3 %collective-permute-start.8 = (bf16[4,2,32,1024]{3,2,1,0:T(8,128)(2,1)S(1)}, bf16[4,2,32,1024]{3,2,1,0:T(8,128)(2,1)S(1)}, u32[]{:S(2)}, u32[]{:S(2)}) collective-permute-start(bf16[4,2,32,1024]{3,2,1,0:T(8,128)(2,1)S(1)} %pad_maximum_fusion.5), channel_id=1, source_target_pairs={{0,8},{1,25},{2,10},{3,27},{4,12},{5,29},{6,14},{7,31},{8,0},{9,17... | collective-permute-start | bytes 1572872 | tf_op jit(solution)/shard_map/ppermute | solution.py:75
  26.0 6.4 %collective-permute-start.2 = (bf16[4,144,1024]{2,1,0:T(8,128)(2,1)S(1)}, bf16[4,144,1024]{2,1,0:T(8,128)(2,1)S(1)}, u32[]{:S(2)}, u32[]{:S(2)}) collective-permute-start(bf16[4,144,1024]{2,1,0:T(8,128)(2,1)S(1)} %pad_maximum_fusion.own_ref), channel_id=1, source_target_pairs={{0,1},{1,0},{2,3},{3,2},{4,5},{5,4},{6,7},{7,6},{8,9},{9,8},{10,11... | collective-permute-start | bytes 3538952 | tf_op jit(solution)/shard_map/ppermute | solution.py:75
  30.3 19.6 %collective-permute-start.9 = (bf16[8,2,32,1024]{3,2,1,0:T(8,128)(2,1)}, bf16[8,2,32,1024]{3,2,1,0:T(8,128)(2,1)}, u32[]{:S(2)}, u32[]{:S(2)}) collective-permute-start(bf16[8,2,32,1024]{3,2,1,0:T(8,128)(2,1)} %pad_maximum_fusion.1.part0), channel_id=1, source_target_pairs={{0,96},{1,33},{2,98},{3,35},{4,100},{5,37},{6,102},{7,39},{8,104},... | collective-permute-start | bytes 3145736 | tf_op jit(solution)/shard_map/ppermute | solution.py:75
  32.3 17.6 %collective-permute-start.10 = (bf16[8,2,32,1024]{3,2,1,0:T(8,128)(2,1)}, bf16[8,2,32,1024]{3,2,1,0:T(8,128)(2,1)}, u32[]{:S(2)}, u32[]{:S(2)}) collective-permute-start(bf16[8,2,32,1024]{3,2,1,0:T(8,128)(2,1)} %pad_maximum_fusion.2.part1), channel_id=1, source_target_pairs={{0,24},{1,9},{2,26},{3,11},{4,28},{5,13},{6,30},{7,15},{8,16},{9,1... | collective-permute-start | bytes 3145736 | tf_op jit(solution)/shard_map/ppermute | solution.py:75
  32.4 20.9 %copy-start.5 = (s32[4]{0:T(128)}, s32[4]{0:T(128)S(1)}, u32[]{:S(2)}) copy-start(s32[4]{0:T(128)S(1)} %pad_add_fusion.place) | copy-start | bytes 52
  32.4 1.0 %copy-start = (bf16[4,144,1024]{2,1,0:T(8,128)(2,1)}, bf16[4,144,1024]{2,1,0:T(8,128)(2,1)S(1)}, u32[]{:S(2)}) copy-start(bf16[4,144,1024]{2,1,0:T(8,128)(2,1)S(1)} %collective-permute-done.2.other_ref) | copy-start | bytes 3538948
  34.0 15.9 %all-to-all-start = ((s32[16,1,256]{2,1,0:T(1,128)}), s32[16,1,256]{2,1,0:T(1,128)S(1)}, u32[]{:S(2)}, u32[]{:S(2)}) async-start(s32[16,1,256]{2,1,0:T(1,128)} %copy.16), calls=%async_computation | async-start | bytes 32768 | tf_op jit(solution)/shard_map/all_to_all | solution.py:538
  40.3 1.3 %copy-start.1 = (bf16[4,144,1024]{2,1,0:T(8,128)(2,1)S(1)}, bf16[4,144,1024]{2,1,0:T(8,128)(2,1)}, u32[]{:S(2)}) copy-start(bf16[4,144,1024]{2,1,0:T(8,128)(2,1)} %copy-done) | copy-start | bytes 3538948
  46.3 1.3 %copy-start.2 = (bf16[2,16,32,1024]{3,2,1,0:T(8,128)(2,1)}, bf16[2,16,32,1024]{3,2,1,0:T(8,128)(2,1)S(1)}, u32[]{:S(2)}) copy-start(bf16[2,16,32,1024]{3,2,1,0:T(8,128)(2,1)S(1)} %spectra_early.1.s0.s0_hbm) | copy-start | bytes 6291460
  50.7 2.6 %copy-start.3 = (bf16[2,16,32,1024]{3,2,1,0:T(8,128)(2,1)S(1)}, bf16[2,16,32,1024]{3,2,1,0:T(8,128)(2,1)}, u32[]{:S(2)}) copy-start(bf16[2,16,32,1024]{3,2,1,0:T(8,128)(2,1)} %copy-done.2) | copy-start | bytes 6291460
  53.2 3.9 %copy-start.4 = (bf16[2,16,32,1024]{3,2,1,0:T(8,128)(2,1)}, bf16[2,16,32,1024]{3,2,1,0:T(8,128)(2,1)S(1)}, u32[]{:S(2)}) copy-start(bf16[2,16,32,1024]{3,2,1,0:T(8,128)(2,1)S(1)} %spectra_late.1.s1.s1_hbm) | copy-start | bytes 6291460
  57.1 23.1 %all-to-all-start.1 = ((f32[128,1,128]{2,1,0:T(1,128)}), f32[128,1,128]{2,1,0:T(1,128)S(1)}, u32[]{:S(2)}, u32[]{:S(2)}) async-start(f32[128,1,128]{2,1,0:T(1,128)} %bitcast.10), calls=%async_computation.1 | async-start | bytes 131072 | tf_op jit(solution)/shard_map/all_to_all | solution.py:544
  80.2 0.6 copy-start.7

commit v3 on v2

--- a/solution.py
+++ b/solution.py
@@ -80,7 +80,10 @@
     return jnp.where(swapped, (4 - apart) & 3, apart)
 
 
-def pack_kernel(template_ref, pair_ref, time_ref, count_ref, out_ref):
+def pack_kernel(strain_ref, template_ref, pair_ref, time_ref, count_ref, a_ref, b_ref, out_ref):
+    for part in range(2):
+        a_ref[0, part] = strain_ref[part, 0, 0]
+        b_ref[0, part] = strain_ref[part, 1, 0]
     out_ref[0, :64] = template_ref[0]
     out_ref[0, 64:128] = template_ref[1]
     time = time_ref[...]
@@ -90,15 +93,19 @@
     out_ref[0, 128:] = jnp.broadcast_to(line.astype(F32), (16, COLS)).astype(BF16)
 
 
-def pack_lists(template, pairs, times, counts):
+def pack_lists(strain, template, pairs, times, counts):
     return pl.pallas_call(
         pack_kernel,
-        out_shape=jax.ShapeDtypeStruct((1, 144, COLS), BF16),
-        in_specs=[VMEM, VMEM, VMEM, SMEM],
-        out_specs=VMEM,
+        out_shape=(
+            jax.ShapeDtypeStruct((1, 2, 32, COLS), BF16),
+            jax.ShapeDtypeStruct((1, 2, 32, COLS), BF16),
+            jax.ShapeDtypeStruct((1, 144, COLS), BF16),
+        ),
+        in_specs=[VMEM, VMEM, VMEM, VMEM, SMEM],
+        out_specs=(VMEM,) * 3,
         cost_estimate=pl.CostEstimate(flops=100_000, bytes_accessed=600_000, transcendentals=0),
         name="pack_lists",
-    )(template, pairs, times, counts)
+    )(strain, template, pairs, times, counts)
 
 
 def route_kernel(place, own_ref, other_ref, out_ref):
@@ -523,8 +530,7 @@
     seat = lax.axis_index("seg")
     place = jnp.stack([device // 4, device % 4, seat // 2, seat % 2]).astype(jnp.int32)
 
-    a, b = strain[:, 0, 0][None], strain[:, 1, 0][None]
-    t = pack_lists(templates[:, 0], trig_pair, trig_time, trig_counts)
+    a, b, t = pack_lists(strain, templates[:, 0], trig_pair, trig_time, trig_counts)
     for step, (near, far) in enumerate(((1, 3), (3, 1), (1, 3), (3, 1))):
         more_a = swap(a, ("yyzz"[step], near), ("yyzz"[step], far))
         more_b = swap(b, ("zzyy"[step], near), ("zzyy"[step], far))

time: 82.9 us -> 79.3 us (0.957)
  local copies, waits for them, and re-layouts: 5.08 us -> 11.4 us
  waiting for transfers between devices: 14.5 us -> 8.69 us
  other arithmetic: 2.55 us -> 0.29 us
  starting transfers between devices: 32.1 us -> 30.1 us
    unnamed x17 -> x28, local copies, waits for them, and re-layouts: 3.47 us -> 9.08 us
    ppermute x11, waiting for transfers between devices: 12.2 us -> 7.92 us  [swap(): return lax.ppermute(x, ('tmpl', 'seg'), pairs)]
    concatenate x6 -> x4, other arithmetic: 2.3 us -> 0.16 us  [shards(): a, b = (jnp.concatenate([a, more_a]), jnp.concatenate([b, more_b]))]
    all_to_all x1, starting transfers between devices: 6.23 us -> 4.48 us  [shards(): lax.all_to_all(outgoing, 'tmpl', split_axis=0, concat_axis=0, tiled=True)]
    concatenate x0 -> x3, local copies, waits for them, and re-layouts: none -> 1.74 us  [the longest x2 1.7 us: shards(): a, b = (jnp.concatenate([a, more_a]), jnp.concatenate([b, more_b]))]
    all_to_all x1, waiting for transfers between devices: 2.3 us -> 0.76 us  [shards(): lax.all_to_all(outgoing, 'tmpl', split_axis=0, concat_axis=0, tiled=True)]
    another operation x1 -> x0, local copies, waits for them, and re-layouts: 0.99 us -> none  [shards(): a, b = (strain[:, 0, 0][None], strain[:, 1, 0][None])]
  transfers between devices with their start and end apart: 13 -> 13, of which waited for: 6 -> 5; matrix products, arithmetic and copies ran while one was open for 4% -> 10% of each run, Pallas kernels for 22% -> 20%
where the time goes in v3:
time: 79.3 us; the launch traced here: 79 us
  starting transfers between devices  30.1 us (38%)
  Pallas kernels  26.9 us (34%)
  local copies, waits for them, and re-layouts  11.4 us (14%)
  waiting for transfers between devices  8.69 us (11%)
  between operations  1.52 us (2%)
    ppermute x11, starting transfers between devices, swap(): return lax.ppermute(x, ('tmpl', 'seg'), pairs)  14.2 us
    all_to_all x1, starting transfers between devices, shards(): lax.all_to_all(result, ('tmpl', 'seg'), split_axis=0, concat_axis=0, tile...  11.5 us
    pallas_call x1, Pallas kernels, series(): pl.pallas_call(series_kernel, out_shape=(jax.ShapeDtypeStruct((COLS, ROWS...  10.7 us
    unnamed x28, local copies, waits for them, and re-layouts  9.08 us
    ppermute x11, waiting for transfers between devices, swap(): return lax.ppermute(x, ('tmpl', 'seg'), pairs)  7.92 us
    pallas_call x2, Pallas kernels, spectra(): pl.pallas_call(functools.partial(spectra_kernel, half), out_shape=jax.Sha...  4.96 us
    all_to_all x1, starting transfers between devices, shards(): lax.all_to_all(outgoing, 'tmpl', split_axis=0, concat_axis=0, tiled=True)  4.48 us
    pallas_call x1, Pallas kernels, veto(): pl.pallas_call(veto_kernel, out_shape=jax.ShapeDtypeStruct((PAIRS, 128),...  3.87 us
  transfers between devices with their start and end apart: 13, of which 5 were waited for; matrix products, arithmetic and copies ran while one was open for 10% of the time, Pallas kernels for 20%

profile of v3, /device:TPU:1, one launch (start us, length us, event | category | flops | bytes accessed | tf_op | source)
XLA Modules:
  0.0 79.0 jit_solution(737355040649345066)
XLA Ops:
  1.3 1.8 %pack_lists.1 = (bf16[1,2,32,1024]{3,2,1,0:T(8,128)(2,1)}, bf16[1,2,32,1024]{3,2,1,0:T(8,128)(2,1)}, bf16[1,144,1024]{2,1,0:T(8,128)(2,1)}) custom-call(bf16[2,2,1,32,1024]{4,3,2,1,0:T(8,128)(2,1)} %strain_ref.1, bf16[2,64,1024]{2,1,0:T(8,128)(2,1)} %bitcast.16, s32[1,256]{1,0:T(1,128)} %pair_ref.3, s32[1,256]{1,0:T(1,128)} %time_ref.1, s32[1]{0:T(128)S(6)} %copy.25.count_ref), custom_call_target="tpu_custom_call" | custom-call | flops 100000 | bytes 600000 | tf_op jit(solution)/shard_map/pack_lists/pallas_call | solution.py:97
  3.1 3.6 %collective-permute-start.3 = (bf16[1,2,32,1024]{3,2,1,0:T(8,128)(2,1)}, bf16[1,2,32,1024]{3,2,1,0:T(8,128)(2,1)S(1)}, u32[]{:S(2)}, u32[]{:S(2)}) collective-permute-start(bf16[1,2,32,1024]{3,2,1,0:T(8,128)(2,1)} %get-tuple-element.23), channel_id=1, source_target_pairs={{0,8},{1,25},{2,10},{3,27},{4,12},{5,29},{6,14},{7,31},{8,0},{9,17... | collective-permute-start | bytes 393224 | tf_op jit(solution)/shard_map/ppermute | solution.py:75
  6.7 3.8 %collective-permute-start.6 = (bf16[1,2,32,1024]{3,2,1,0:T(8,128)(2,1)}, bf16[1,2,32,1024]{3,2,1,0:T(8,128)(2,1)S(1)}, u32[]{:S(2)}, u32[]{:S(2)}) collective-permute-start(bf16[1,2,32,1024]{3,2,1,0:T(8,128)(2,1)} %get-tuple-element.24), channel_id=1, source_target_pairs={{0,32},{1,97},{2,34},{3,99},{4,36},{5,101},{6,38},{7,103},{8,40},{... | collective-permute-start | bytes 393224 | tf_op jit(solution)/shard_map/ppermute | solution.py:75
  10.4 2.5 %collective-permute-start = (bf16[1,144,1024]{2,1,0:T(8,128)(2,1)}, bf16[1,144,1024]{2,1,0:T(8,128)(2,1)S(1)}, u32[]{:S(2)}, u32[]{:S(2)}) collective-permute-start(bf16[1,144,1024]{2,1,0:T(8,128)(2,1)} %get-tuple-element.21), channel_id=1, source_target_pairs={{0,2},{1,7},{2,0},{3,5},{4,6},{5,3},{6,4},{7,1},{8,10},{9,15},{10,... | collective-permute-start | bytes 884744 | tf_op jit(solution)/shard_map/ppermute | solution.py:75
  12.9 1.0 %constant_dynamic-update-slice_fusion.2 = bf16[4,144,1024]{2,1,0:T(8,128)(2,1)S(1)} fusion(bf16[1,144,1024]{2,1,0:T(8,128)(2,1)} %get-tuple-element.21), kind=kLoop, calls=%fused_computation.7 | loop fusion | bytes 589824
  14.0 1.7 %constant_dynamic-update-slice_fusion.6 = (bf16[8,2,32,1024]{3,2,1,0:T(8,128)(2,1)}, bf16[8,2,32,1024]{3,2,1,0:T(8,128)(2,1)}) fusion(bf16[1,2,32,1024]{3,2,1,0:T(8,128)(2,1)} %get-tuple-element.23, bf16[1,2,32,1024]{3,2,1,0:T(8,128)(2,1)} %get-tuple-element.24), kind=kLoop, calls=%fused_computation.11 | loop fusion | bytes 524288
  16.0 0.7 constant_dynamic-update-slice_fusion.5
  16.6 0.7 constant_dynamic-update-slice_fusion.9
  17.9 3.6 %collective-permute-done.7 = bf16[2,2,32,1024]{3,2,1,0:T(8,128)(2,1)S(1)} collective-permute-done((bf16[2,2,32,1024]{3,2,1,0:T(8,128)(2,1)S(1)}, bf16[2,2,32,1024]{3,2,1,0:T(8,128)(2,1)S(1)}, u32[]{:S(2)}, u32[]{:S(2)}) %collective-permute-start.7) | collective-permute-done | bytes 262176 | tf_op jit(solution)/shard_map/ppermute | solution.py:75
  21.5 0.7 collective-permute-start.8
  22.4 0.7 constant_dynamic-update-slice_fusion.4
  23.1 0.7 constant_dynamic-update-slice_fusion.8
  23.9 3.0 %collective-permute-done.1 = bf16[2,144,1024]{2,1,0:T(8,128)(2,1)S(1)} collective-permute-done((bf16[2,144,1024]{2,1,0:T(8,128)(2,1)S(1)}, bf16[2,144,1024]{2,1,0:T(8,128)(2,1)S(1)}, u32[]{:S(2)}, u32[]{:S(2)}) %collective-permute-start.1) | collective-permute-done | bytes 589856 | tf_op jit(solution)/shard_map/ppermute | solution.py:75
  27.0 3.1 %collective-permute-start.2 = (bf16[4,144,1024]{2,1,0:T(8,128)(2,1)S(1)}, bf16[4,144,1024]{2,1,0:T(8,128)(2,1)S(1)}, u32[]{:S(2)}, u32[]{:S(2)}) collective-permute-start(bf16[4,144,1024]{2,1,0:T(8,128)(2,1)S(1)} %constant_dynamic-update-slice_fusion.own_ref), channel_id=1, source_target_pairs={{0,1},{1,0},{2,3},{3,2},{4,5},{5,4},{6,7},{7,6},{8,9},{9,8},{10,11... | collective-permute-start | bytes 3538952 | tf_op jit(solution)/shard_map/ppermute | solution.py:75
  30.0 0.8 %collective-permute-done.8 = bf16[4,2,32,1024]{3,2,1,0:T(8,128)(2,1)S(1)} collective-permute-done((bf16[4,2,32,1024]{3,2,1,0:T(8,128)(2,1)S(1)}, bf16[4,2,32,1024]{3,2,1,0:T(8,128)(2,1)S(1)}, u32[]{:S(2)}, u32[]{:S(2)}) %collective-permute-start.8) | collective-permute-done | bytes 524320 | tf_op jit(solution)/shard_map/ppermute | solution.py:75
  30.8 0.9 %constant_dynamic-update-slice_fusion.7.part1 = bf16[8,2,32,1024]{3,2,1,0:T(8,128)(2,1)} fusion(bf16[8,2,32,1024]{3,2,1,0:T(8,128)(2,1)} %constant_dynamic-update-slice_fusion.8, bf16[4,2,32,1024]{3,2,1,0:T(8,128)(2,1)S(1)} %collective-permute-done.8), kind=kLoop, calls=%fused_computation.12 | loop fusion | bytes 1048576 | tf_op jit(solution)/shard_map/concatenate | solution.py:540
  31.9 0.8 %constant_dynamic-update-slice_fusion.3.part0 = bf16[8,2,32,1024]{3,2,1,0:T(8,128)(2,1)} fusion(bf16[8,2,32,1024]{3,2,1,0:T(8,128)(2,1)} %constant_dynamic-update-slice_fusion.4, bf16[4,2,32,1024]{3,2,1,0:T(8,128)(2,1)S(1)} %collective-permute-done.5), kind=kLoop, calls=%fused_computation.8 | loop fusion | bytes 1048576 | tf_op jit(solution)/shard_map/concatenate | solution.py:540
  32.9 0.7 route_lists.1
  33.9 0.6 copy.12
  34.6 4.5 %all-to-all-start = ((s32[16,1,256]{2,1,0:T(1,128)}), s32[16,1,256]{2,1,0:T(1,128)S(1)}, u32[]{:S(2)}, u32[]{:S(2)}) async-start(s32[16,1,256]{2,1,0:T(1,128)} %copy.12), calls=%async_computation | async-start | bytes 32768 | tf_op jit(solution)/shard_map/all_to_all | solution.py:544
  39.1 1.3 %copy-done.1 = bf16[4,144,1024]{2,1,0:T(8,128)(2,1)S(1)} copy-done((bf16[4,144,1024]{2,1,0:T(8,128)(2,1)S(1)}, bf16[4,144,1024]{2,1,0:T(8,128)(2,1)}, u32[]{:S(2)}) %copy-start.1) | copy-done | bytes 1179672
  40.3 2.3 %order_template.1 = (bf16[2,512,1024]{2,1,0:T(8,128)(2,1)S(1)}, f32[16,256]{1,0:T(8,128)S(1)}) custom-call(s32[4]{0:T(128)S(1)} %pad_add_fusion.place, bf16[4,144,1024]{2,1,0:T(8,128)(2,1)S(1)} %constant_dynamic-update-slice_fusion.own_ref, bf16[4,144,1024]{2,1,0:T(8,128)(2,1)S(1)} %copy-done.1), custom_call_target="tpu_custom_call" | custom-call | flops 3000000 | bytes 4000000 | tf_op jit(solution)/shard_map/order_template/pallas_call | solution.py:173
  42.6 2.4 %spectra_early.1.s0.s0_hbm = bf16[2,16,32,1024]{3,2,1,0:T(8,128)(2,1)S(1)} custom-call(s32[4]{0:T(128)S(1)} %pad_add_fusion.place, bf16[2,512,1024]{2,1,0:T(8,128)(2,1)S(1)} %get-tuple-element.22.template_ref, bf16[8,2,32,1024]{3,2,1,0:T(8,128)(2,1)} %constant_dynamic-update-slice_fusion.3.part0, ...), custom_call_target="tpu_custom_call" | custom-call | flops 3000000 | bytes 6000000 | tf_op jit(solution)/shard_map/spectra_early/pallas_call | solution.py:285
  45.1 1.3 %copy-done.2 = bf16[2,16,32,1024]{3,2,1,0:T(8,128)(2,1)} copy-done((bf16[2,16,32,1024]{3,2,1,0:T(8,128)(2,1)}, bf16[2,16,32,1024]{3,2,1,0:T(8,128)(2,1)S(1)}, u32[]{:S(2)}) %copy-start.2) | copy-done | bytes 2097176
  46.4 0.8 all-to-all-done
  47.2 0.8 probes.1
  48.0 2.6 %spectra_late.1.s1.s1_hbm = bf16[2,16,32,1024]{3,2,1,0:T(8,128)(2,1)S(1)} custom-call(s32[4]{0:T(128)S(1)} %pad_add_fusion.place, bf16[2,512,1024]{2,1,0:T(8,128)(2,1)S(1)} %get-tuple-element.22.template_ref, bf16[8,2,32,1024]{3,2,1,0:T(8,128)(2,1)} %collective-permute-done.9.part0, bf16[8,2,32,1024]{3,2,1,0:T(8,128)(2,1)} %collective-permute-done.10.part1), custom_call_target="tpu_custom_call" | custom-call | flops 3000000 | bytes 6000000 | tf_op jit(solution)/shard_map/spectra_late/pallas_call | solution.py:285
  50.5 3.9 %veto.1.result_hbm = f32[128,128]{1,0:T(8,128)} custom-call(s32[4]{0:T(128)S(1)} %pad_add_fusion.place, f32[16,256]{1,0:T(8,128)S(1)} %get-tuple-element.27.power_ref, s32[1,256]{1,0:T(1,128)S(1)} %get-tuple-element.29.time_ref, bf16[1024,512]{1,0:T(8,128)(2,1)S(1)} %get-tuple-element.30.one_ref, bf16[1024,512]{1,0:T(8,128)(2,1)S(1)} %get-tuple-element.31.two_ref, ...), custom_call_target="tpu_custom_call" | custom-call | flops 2200000000 | bytes 6000000 | tf_op jit(solution)/shard_map/veto/pallas_call | solution.py:336
  54.4 11.5 %all-to-all-start.1 = ((f32[128,1,128]{2,1,0:T(1,128)}), f32[128,1,128]{2,1,0:T(1,128)S(1)}, u32[]{:S(2)}, u32[]{:S(2)}) async-start(f32[128,1,128]{2,1,0:T(1,128)} %bitcast.8), calls=%async_computation.1 | async-start | bytes 131072 | tf_op jit(solution)/shard_map/all_to_all | solution.py:550
  65.9 10.7 %series.1 = (f32[1024,512]{1,0:T(8,128)}, f32[1,1]{1,0:T(1,128)}) custom-call(s32[4]{0:T(128)} %copy-done.5, bf16[2,16,32,1024]{3,2,1,0:T(8,128)(2,1)} %copy-done.2, bf16[2,16,32,1024]{3,2,1,0:T(8,128)(2,1)} %copy-done.4, f32[128,128]{1,0:T(8,128)} %veto.1.result_hbm, bf16[4,4,256,256]{3,2,1,0:T(8,128)(2,1)} %constant.57.clone.rows_hbm, ...), custom_call_target="tpu_custom_call" | custom-call | flops 3300000000 | bytes 13000000 | tf_op jit(solution)/shard_map/series/pallas_call | solution.py:497
  76.7 0.6 copy-done.9
  77.3 1.7 %take_results.1 = (f32[1,256]{1,0:T(1,128)}, f32[1,256]{1,0:T(1,128)}) custom-call(s32[1,256]{1,0:T(1,128)} %pair_ref.3, s32[1]{0:T(128)S(6)} %copy.25.count_ref, f32[128,128]{1,0:T(8,128)} %bitcast.17), custom_call_target="tpu_custom_call" | custom-call | flops 500000 | bytes 70000 | tf_op jit(solution)/shard_map/take_results/pallas_call | solution.py:206
  (41 shorter events, 1.8 us)
Async XLA Ops:
  3.1 12.6 %copy-start.7 = (bf16[1,2,32,1024]{3,2,1,0:T(8,128)(2,1)S(1)}, bf16[1,2,32,1024]{3,2,1,0:T(8,128)(2,1)}, u32[]{:S(2)}) copy-start(bf16[1,2,32,1024]{3,2,1,0:T(8,128)(2,1)} %get-tuple-element.23) | copy-start | bytes 393220
  3.1 12.7 %copy-start.8 = (bf16[1,2,32,1024]{3,2,1,0:T(8,128)(2,1)S(1)}, bf16[1,2,32,1024]{3,2,1,0:T(8,128)(2,1)}, u32[]{:S(2)}) copy-start(bf16[1,2,32,1024]{3,2,1,0:T(8,128)(2,1)} %get-tuple-element.24) | copy-start | bytes 393220
  3.1 12.6 %collective-permute-start.3 = (bf16[1,2,32,1024]{3,2,1,0:T(8,128)(2,1)}, bf16[1,2,32,1024]{3,2,1,0:T(8,128)(2,1)S(1)}, u32[]{:S(2)}, u32[]{:S(2)}) collective-permute-start(bf16[1,2,32,1024]{3,2,1,0:T(8,128)(2,1)} %get-tuple-element.23), channel_id=1, source_target_pairs={{0,8},{1,25},{2,10},{3,27},{4,12},{5,29},{6,14},{7,31},{8,0},{9,17... | collective-permute-start | bytes 393224 | tf_op jit(solution)/shard_map/ppermute | solution.py:75
  6.7 9.1 %collective-permute-start.6 = (bf16[1,2,32,1024]{3,2,1,0:T(8,128)(2,1)}, bf16[1,2,32,1024]{3,2,1,0:T(8,128)(2,1)S(1)}, u32[]{:S(2)}, u32[]{:S(2)}) collective-permute-start(bf16[1,2,32,1024]{3,2,1,0:T(8,128)(2,1)} %get-tuple-element.24), channel_id=1, source_target_pairs={{0,32},{1,97},{2,34},{3,99},{4,36},{5,101},{6,38},{7,103},{8,40},{... | collective-permute-start | bytes 393224 | tf_op jit(solution)/shard_map/ppermute | solution.py:75
  10.4 7.3 %collective-permute-start = (bf16[1,144,1024]{2,1,0:T(8,128)(2,1)}, bf16[1,144,1024]{2,1,0:T(8,128)(2,1)S(1)}, u32[]{:S(2)}, u32[]{:S(2)}) collective-permute-start(bf16[1,144,1024]{2,1,0:T(8,128)(2,1)} %get-tuple-element.21), channel_id=1, source_target_pairs={{0,2},{1,7},{2,0},{3,5},{4,6},{5,3},{6,4},{7,1},{8,10},{9,15},{10,... | collective-permute-start | bytes 884744 | tf_op jit(solution)/shard_map/ppermute | solution.py:75
  13.9 3.8 %copy-start.6 = (bf16[1,144,1024]{2,1,0:T(8,128)(2,1)S(1)}, bf16[1,144,1024]{2,1,0:T(8,128)(2,1)}, u32[]{:S(2)}) copy-start(bf16[1,144,1024]{2,1,0:T(8,128)(2,1)} %get-tuple-element.21) | copy-start | bytes 884740
  15.7 6.5 %collective-permute-start.4 = (bf16[2,2,32,1024]{3,2,1,0:T(8,128)(2,1)S(1)}, bf16[2,2,32,1024]{3,2,1,0:T(8,128)(2,1)S(1)}, u32[]{:S(2)}, u32[]{:S(2)}) collective-permute-start(bf16[2,2,32,1024]{3,2,1,0:T(8,128)(2,1)S(1)} %pad_maximum_fusion.3), channel_id=1, source_target_pairs={{0,24},{1,9},{2,26},{3,11},{4,28},{5,13},{6,30},{7,15},{8,16},{9,1... | collective-permute-start | bytes 786440 | tf_op jit(solution)/shard_map/ppermute | solution.py:75
  15.9 5.6 %collective-permute-start.7 = (bf16[2,2,32,1024]{3,2,1,0:T(8,128)(2,1)S(1)}, bf16[2,2,32,1024]{3,2,1,0:T(8,128)(2,1)S(1)}, u32[]{:S(2)}, u32[]{:S(2)}) collective-permute-start(bf16[2,2,32,1024]{3,2,1,0:T(8,128)(2,1)S(1)} %pad_maximum_fusion.4), channel_id=1, source_target_pairs={{0,96},{1,33},{2,98},{3,35},{4,100},{5,37},{6,102},{7,39},{8,104},... | collective-permute-start | bytes 786440 | tf_op jit(solution)/shard_map/ppermute | solution.py:75
  17.8 9.1 %collective-permute-start.1 = (bf16[2,144,1024]{2,1,0:T(8,128)(2,1)S(1)}, bf16[2,144,1024]{2,1,0:T(8,128)(2,1)S(1)}, u32[]{:S(2)}, u32[]{:S(2)}) collective-permute-start(bf16[2,144,1024]{2,1,0:T(8,128)(2,1)S(1)} %pad_maximum_fusion), channel_id=1, source_target_pairs={{0,6},{1,3},{2,4},{3,1},{4,2},{5,7},{6,0},{7,5},{8,14},{9,11},{10,... | collective-permute-start | bytes 1769480 | tf_op jit(solution)/shard_map/ppermute | solution.py:75
  21.5 9.3 %collective-permute-start.8 = (bf16[4,2,32,1024]{3,2,1,0:T(8,128)(2,1)S(1)}, bf16[4,2,32,1024]{3,2,1,0:T(8,128)(2,1)S(1)}, u32[]{:S(2)}, u32[]{:S(2)}) collective-permute-start(bf16[4,2,32,1024]{3,2,1,0:T(8,128)(2,1)S(1)} %pad_maximum_fusion.2), channel_id=1, source_target_pairs={{0,8},{1,25},{2,10},{3,27},{4,12},{5,29},{6,14},{7,31},{8,0},{9,17... | collective-permute-start | bytes 1572872 | tf_op jit(solution)/shard_map/ppermute | solution.py:75
  22.3 9.7 %collective-permute-start.5 = (bf16[4,2,32,1024]{3,2,1,0:T(8,128)(2,1)S(1)}, bf16[4,2,32,1024]{3,2,1,0:T(8,128)(2,1)S(1)}, u32[]{:S(2)}, u32[]{:S(2)}) collective-permute-start(bf16[4,2,32,1024]{3,2,1,0:T(8,128)(2,1)S(1)} %pad_maximum_fusion.1), channel_id=1, source_target_pairs={{0,32},{1,97},{2,34},{3,99},{4,36},{5,101},{6,38},{7,103},{8,40},{... | collective-permute-start | bytes 1572872 | tf_op jit(solution)/shard_map/ppermute | solution.py:75
  27.0 6.0 %collective-permute-start.2 = (bf16[4,144,1024]{2,1,0:T(8,128)(2,1)S(1)}, bf16[4,144,1024]{2,1,0:T(8,128)(2,1)S(1)}, u32[]{:S(2)}, u32[]{:S(2)}) collective-permute-start(bf16[4,144,1024]{2,1,0:T(8,128)(2,1)S(1)} %constant_dynamic-update-slice_fusion.own_ref), channel_id=1, source_target_pairs={{0,1},{1,0},{2,3},{3,2},{4,5},{5,4},{6,7},{7,6},{8,9},{9,8},{10,11... | collective-permute-start | bytes 3538952 | tf_op jit(solution)/shard_map/ppermute | solution.py:75
  31.7 15.5 %collective-permute-start.10 = (bf16[8,2,32,1024]{3,2,1,0:T(8,128)(2,1)}, bf16[8,2,32,1024]{3,2,1,0:T(8,128)(2,1)}, u32[]{:S(2)}, u32[]{:S(2)}) collective-permute-start(bf16[8,2,32,1024]{3,2,1,0:T(8,128)(2,1)} %constant_dynamic-update-slice_fusion.7.part1), channel_id=1, source_target_pairs={{0,24},{1,9},{2,26},{3,11},{4,28},{5,13},{6,30},{7,15},{8,16},{9,1... | collective-permute-start | bytes 3145736 | tf_op jit(solution)/shard_map/ppermute | solution.py:75
  32.8 14.4 %collective-permute-start.9 = (bf16[8,2,32,1024]{3,2,1,0:T(8,128)(2,1)}, bf16[8,2,32,1024]{3,2,1,0:T(8,128)(2,1)}, u32[]{:S(2)}, u32[]{:S(2)}) collective-permute-start(bf16[8,2,32,1024]{3,2,1,0:T(8,128)(2,1)} %constant_dynamic-update-slice_fusion.3.part0), channel_id=1, source_target_pairs={{0,96},{1,33},{2,98},{3,35},{4,100},{5,37},{6,102},{7,39},{8,104},... | collective-permute-start | bytes 3145736 | tf_op jit(solution)/shard_map/ppermute | solution.py:75
  32.9 17.6 %copy-start.5 = (s32[4]{0:T(128)}, s32[4]{0:T(128)S(1)}, u32[]{:S(2)}) copy-start(s32[4]{0:T(128)S(1)} %pad_add_fusion.place) | copy-start | bytes 52
  32.9 1.0 %copy-start = (bf16[4,144,1024]{2,1,0:T(8,128)(2,1)}, bf16[4,144,1024]{2,1,0:T(8,128)(2,1)S(1)}, u32[]{:S(2)}) copy-start(bf16[4,144,1024]{2,1,0:T(8,128)(2,1)S(1)} %collective-permute-done.2.other_ref) | copy-start | bytes 3538948
  34.6 12.6 %all-to-all-start = ((s32[16,1,256]{2,1,0:T(1,128)}), s32[16,1,256]{2,1,0:T(1,128)S(1)}, u32[]{:S(2)}, u32[]{:S(2)}) async-start(s32[16,1,256]{2,1,0:T(1,128)} %copy.12), calls=%async_computation | async-start | bytes 32768 | tf_op jit(solution)/shard_map/all_to_all | solution.py:544
  39.1 1.3 %copy-start.1 = (bf16[4,144,1024]{2,1,0:T(8,128)(2,1)S(1)}, bf16[4,144,1024]{2,1,0:T(8,128)(2,1)}, u32[]{:S(2)}) copy-start(bf16[4,144,1024]{2,1,0:T(8,128)(2,1)} %copy-done) | copy-start | bytes 3538948
  45.0 1.4 %copy-start.2 = (bf16[2,16,32,1024]{3,2,1,0:T(8,128)(2,1)}, bf16[2,16,32,1024]{3,2,1,0:T(8,128)(2,1)S(1)}, u32[]{:S(2)}) copy-start(bf16[2,16,32,1024]{3,2,1,0:T(8,128)(2,1)S(1)} %spectra_early.1.s0.s0_hbm) | copy-start | bytes 6291460
  47.9 2.6 %copy-start.3 = (bf16[2,16,32,1024]{3,2,1,0:T(8,128)(2,1)S(1)}, bf16[2,16,32,1024]{3,2,1,0:T(8,128)(2,1)}, u32[]{:S(2)}) copy-start(bf16[2,16,32,1024]{3,2,1,0:T(8,128)(2,1)} %copy-done.2) | copy-start | bytes 6291460
  50.5 3.9 %copy-start.4 = (bf16[2,16,32,1024]{3,2,1,0:T(8,128)(2,1)}, bf16[2,16,32,1024]{3,2,1,0:T(8,128)(2,1)S(1)}, u32[]{:S(2)}) copy-start(bf16[2,16,32,1024]{3,2,1,0:T(8,128)(2,1)S(1)} %spectra_late.1.s1.s1_hbm) | copy-start | bytes 6291460
  54.4 22.2 %all-to-all-start.1 = ((f32[128,1,128]{2,1,0:T(1,128)}), f32[128,1,128]{2,1,0:T(1,128)S(1)}, u32[]{:S(2)}, u32[]{:S(2)}) async-start(f32[128,1,128]{2,1,0:T(1,128)} %bitcast.8), calls=%async_computation.1 | async-start | bytes 131072 | tf_op jit(solution)/shard_map/all_to_all | solution.py:550
  76.7 0.6 copy-start.9

commit v4 on v3

--- a/solution.py
+++ b/solution.py
@@ -129,13 +129,15 @@
             for slot, mask in enumerate(masks):
                 value = jnp.sum(jnp.where(mask, time, 0.0), axis=1, keepdims=True)
                 out = jnp.where(lane == PAIRS * slot + source, value, out)
-    out_ref[...] = out.astype(jnp.int32)
+    out = out.astype(jnp.int32)
+    for line in range(16):
+        out_ref[line] = out[line : line + 1]
 
 
 def route_lists(place, own, other):
     return pl.pallas_call(
         route_kernel,
-        out_shape=jax.ShapeDtypeStruct((16, SLOTS), jnp.int32),
+        out_shape=jax.ShapeDtypeStruct((16, 1, SLOTS), jnp.int32),
         in_specs=[SMEM, VMEM, VMEM],
         out_specs=VMEM,
         compiler_params=pltpu.CompilerParams(vmem_limit_bytes=8 * 1024 * 1024),
@@ -545,7 +547,7 @@
     template, power = order_template(place, t, other_t)
     more_a, more_b, incoming = lax.optimization_barrier((more_a, more_b, incoming))
     specs = spectra(0, place, template, (a, b)), spectra(1, place, template, (more_a, more_b))
-    *tables, times = probes(incoming)
+    *tables, times = probes(incoming.reshape(16, SLOTS))
     result = veto(place, power, times, tables, specs)
     back = lax.all_to_all(result, ("tmpl", "seg"), split_axis=0, concat_axis=0, tiled=True)
     snr_series, peak = series(

time: 79.3 us -> 79.1 us (level)
  local copies, waits for them, and re-layouts: 11.4 us -> 10.6 us
    ppermute x11, waiting for transfers between devices: 7.92 us -> 8.93 us  [swap(): return lax.ppermute(x, ('tmpl', 'seg'), pairs)]
  transfers between devices with their start and end apart: 13 -> 13, of which waited for: 5 -> 5; matrix products, arithmetic and copies ran while one was open for 10% -> 10% of each run, Pallas kernels for 20% -> 21%
where the time goes in v4:
time: 79.1 us; the launch traced here: 78.7 us
  starting transfers between devices  29.9 us (38%)
  Pallas kernels  27.5 us (35%)
  local copies, waits for them, and re-layouts  10.6 us (13%)
  waiting for transfers between devices  8.95 us (11%)
  between operations  1.51 us (2%)
    ppermute x11, starting transfers between devices, swap(): return lax.ppermute(x, ('tmpl', 'seg'), pairs)  14.2 us
    all_to_all x1, starting transfers between devices, shards(): lax.all_to_all(result, ('tmpl', 'seg'), split_axis=0, concat_axis=0, tile...  11.2 us
    pallas_call x1, Pallas kernels, series(): pl.pallas_call(series_kernel, out_shape=(jax.ShapeDtypeStruct((COLS, ROWS...  10.7 us
    ppermute x11, waiting for transfers between devices, swap(): return lax.ppermute(x, ('tmpl', 'seg'), pairs)  8.93 us
    unnamed x28, local copies, waits for them, and re-layouts  8.83 us
    pallas_call x2, Pallas kernels, spectra(): pl.pallas_call(functools.partial(spectra_kernel, half), out_shape=jax.Sha...  4.96 us
    all_to_all x1, starting transfers between devices, shards(): lax.all_to_all(outgoing, 'tmpl', split_axis=0, concat_axis=0, tiled=True)  4.48 us
    pallas_call x1, Pallas kernels, veto(): pl.pallas_call(veto_kernel, out_shape=jax.ShapeDtypeStruct((PAIRS, 128),...  3.87 us
  transfers between devices with their start and end apart: 13, of which 5 were waited for; matrix products, arithmetic and copies ran while one was open for 10% of the time, Pallas kernels for 21%

profile of v4, /device:TPU:1, one launch (start us, length us, event | category | flops | bytes accessed | tf_op | source)
XLA Modules:
  0.0 78.7 jit_solution(9662860676772009546)
XLA Ops:
  1.3 1.8 %pack_lists.1 = (bf16[1,2,32,1024]{3,2,1,0:T(8,128)(2,1)}, bf16[1,2,32,1024]{3,2,1,0:T(8,128)(2,1)}, bf16[1,144,1024]{2,1,0:T(8,128)(2,1)}) custom-call(bf16[2,2,1,32,1024]{4,3,2,1,0:T(8,128)(2,1)} %strain_ref.1, bf16[2,64,1024]{2,1,0:T(8,128)(2,1)} %bitcast.14, s32[1,256]{1,0:T(1,128)} %pair_ref.3, s32[1,256]{1,0:T(1,128)} %time_ref.1, s32[1]{0:T(128)S(6)} %copy.25.count_ref), custom_call_target="tpu_custom_call" | custom-call | flops 100000 | bytes 600000 | tf_op jit(solution)/shard_map/pack_lists/pallas_call | solution.py:97
  3.1 3.6 %collective-permute-start.3 = (bf16[1,2,32,1024]{3,2,1,0:T(8,128)(2,1)}, bf16[1,2,32,1024]{3,2,1,0:T(8,128)(2,1)S(1)}, u32[]{:S(2)}, u32[]{:S(2)}) collective-permute-start(bf16[1,2,32,1024]{3,2,1,0:T(8,128)(2,1)} %get-tuple-element.23), channel_id=1, source_target_pairs={{0,8},{1,25},{2,10},{3,27},{4,12},{5,29},{6,14},{7,31},{8,0},{9,17... | collective-permute-start | bytes 393224 | tf_op jit(solution)/shard_map/ppermute | solution.py:75
  6.7 3.8 %collective-permute-start.6 = (bf16[1,2,32,1024]{3,2,1,0:T(8,128)(2,1)}, bf16[1,2,32,1024]{3,2,1,0:T(8,128)(2,1)S(1)}, u32[]{:S(2)}, u32[]{:S(2)}) collective-permute-start(bf16[1,2,32,1024]{3,2,1,0:T(8,128)(2,1)} %get-tuple-element.24), channel_id=1, source_target_pairs={{0,32},{1,97},{2,34},{3,99},{4,36},{5,101},{6,38},{7,103},{8,40},{... | collective-permute-start | bytes 393224 | tf_op jit(solution)/shard_map/ppermute | solution.py:75
  10.4 2.5 %collective-permute-start = (bf16[1,144,1024]{2,1,0:T(8,128)(2,1)}, bf16[1,144,1024]{2,1,0:T(8,128)(2,1)S(1)}, u32[]{:S(2)}, u32[]{:S(2)}) collective-permute-start(bf16[1,144,1024]{2,1,0:T(8,128)(2,1)} %get-tuple-element.21), channel_id=1, source_target_pairs={{0,2},{1,7},{2,0},{3,5},{4,6},{5,3},{6,4},{7,1},{8,10},{9,15},{10,... | collective-permute-start | bytes 884744 | tf_op jit(solution)/shard_map/ppermute | solution.py:75
  12.9 1.0 %constant_dynamic-update-slice_fusion.2 = bf16[4,144,1024]{2,1,0:T(8,128)(2,1)S(1)} fusion(bf16[1,144,1024]{2,1,0:T(8,128)(2,1)} %get-tuple-element.21), kind=kLoop, calls=%fused_computation.7 | loop fusion | bytes 589824
  14.0 1.7 %constant_dynamic-update-slice_fusion.6 = (bf16[8,2,32,1024]{3,2,1,0:T(8,128)(2,1)}, bf16[8,2,32,1024]{3,2,1,0:T(8,128)(2,1)}) fusion(bf16[1,2,32,1024]{3,2,1,0:T(8,128)(2,1)} %get-tuple-element.23, bf16[1,2,32,1024]{3,2,1,0:T(8,128)(2,1)} %get-tuple-element.24), kind=kLoop, calls=%fused_computation.11 | loop fusion | bytes 524288
  16.0 0.7 constant_dynamic-update-slice_fusion.5
  16.6 0.7 constant_dynamic-update-slice_fusion.9
  17.3 0.4 collective-permute-done
  17.9 3.6 %collective-permute-done.7 = bf16[2,2,32,1024]{3,2,1,0:T(8,128)(2,1)S(1)} collective-permute-done((bf16[2,2,32,1024]{3,2,1,0:T(8,128)(2,1)S(1)}, bf16[2,2,32,1024]{3,2,1,0:T(8,128)(2,1)S(1)}, u32[]{:S(2)}, u32[]{:S(2)}) %collective-permute-start.7) | collective-permute-done | bytes 262176 | tf_op jit(solution)/shard_map/ppermute | solution.py:75
  21.5 0.7 collective-permute-start.8
  22.4 0.7 constant_dynamic-update-slice_fusion.4
  23.1 0.7 constant_dynamic-update-slice_fusion.8
  23.9 3.0 %collective-permute-done.1 = bf16[2,144,1024]{2,1,0:T(8,128)(2,1)S(1)} collective-permute-done((bf16[2,144,1024]{2,1,0:T(8,128)(2,1)S(1)}, bf16[2,144,1024]{2,1,0:T(8,128)(2,1)S(1)}, u32[]{:S(2)}, u32[]{:S(2)}) %collective-permute-start.1) | collective-permute-done | bytes 589856 | tf_op jit(solution)/shard_map/ppermute | solution.py:75
  27.0 3.1 %collective-permute-start.2 = (bf16[4,144,1024]{2,1,0:T(8,128)(2,1)S(1)}, bf16[4,144,1024]{2,1,0:T(8,128)(2,1)S(1)}, u32[]{:S(2)}, u32[]{:S(2)}) collective-permute-start(bf16[4,144,1024]{2,1,0:T(8,128)(2,1)S(1)} %constant_dynamic-update-slice_fusion.own_ref), channel_id=1, source_target_pairs={{0,1},{1,0},{2,3},{3,2},{4,5},{5,4},{6,7},{7,6},{8,9},{9,8},{10,11... | collective-permute-start | bytes 3538952 | tf_op jit(solution)/shard_map/ppermute | solution.py:75
  30.0 0.8 %collective-permute-done.8 = bf16[4,2,32,1024]{3,2,1,0:T(8,128)(2,1)S(1)} collective-permute-done((bf16[4,2,32,1024]{3,2,1,0:T(8,128)(2,1)S(1)}, bf16[4,2,32,1024]{3,2,1,0:T(8,128)(2,1)S(1)}, u32[]{:S(2)}, u32[]{:S(2)}) %collective-permute-start.8) | collective-permute-done | bytes 524320 | tf_op jit(solution)/shard_map/ppermute | solution.py:75
  30.8 0.9 %constant_dynamic-update-slice_fusion.7.part1 = bf16[8,2,32,1024]{3,2,1,0:T(8,128)(2,1)} fusion(bf16[8,2,32,1024]{3,2,1,0:T(8,128)(2,1)} %constant_dynamic-update-slice_fusion.8, bf16[4,2,32,1024]{3,2,1,0:T(8,128)(2,1)S(1)} %collective-permute-done.8), kind=kLoop, calls=%fused_computation.12 | loop fusion | bytes 1048576 | tf_op jit(solution)/shard_map/concatenate | solution.py:542
  31.9 0.8 %constant_dynamic-update-slice_fusion.3.part0 = bf16[8,2,32,1024]{3,2,1,0:T(8,128)(2,1)} fusion(bf16[8,2,32,1024]{3,2,1,0:T(8,128)(2,1)} %constant_dynamic-update-slice_fusion.4, bf16[4,2,32,1024]{3,2,1,0:T(8,128)(2,1)S(1)} %collective-permute-done.5), kind=kLoop, calls=%fused_computation.8 | loop fusion | bytes 1048576 | tf_op jit(solution)/shard_map/concatenate | solution.py:542
  32.9 1.4 %route_lists.1 = s32[16,1,256]{2,1,0:T(1,128)} custom-call(s32[4]{0:T(128)S(1)} %pad_add_fusion.place, bf16[4,144,1024]{2,1,0:T(8,128)(2,1)S(1)} %constant_dynamic-update-slice_fusion.own_ref, bf16[4,144,1024]{2,1,0:T(8,128)(2,1)S(1)} %collective-permute-done.2.other_ref), custom_call_target="tpu_custom_call" | custom-call | flops 1000000 | bytes 300000 | tf_op jit(solution)/shard_map/route_lists/pallas_call | solution.py:138
  34.3 4.5 %all-to-all-start = ((s32[16,1,256]{2,1,0:T(1,128)}), s32[16,1,256]{2,1,0:T(1,128)S(1)}, u32[]{:S(2)}, u32[]{:S(2)}) async-start(s32[16,1,256]{2,1,0:T(1,128)} %route_lists.1), calls=%async_computation | async-start | bytes 32768 | tf_op jit(solution)/shard_map/all_to_all | solution.py:546
  38.8 1.3 %copy-done.1 = bf16[4,144,1024]{2,1,0:T(8,128)(2,1)S(1)} copy-done((bf16[4,144,1024]{2,1,0:T(8,128)(2,1)S(1)}, bf16[4,144,1024]{2,1,0:T(8,128)(2,1)}, u32[]{:S(2)}) %copy-start.1) | copy-done | bytes 1179672
  40.1 2.3 %order_template.1 = (bf16[2,512,1024]{2,1,0:T(8,128)(2,1)S(1)}, f32[16,256]{1,0:T(8,128)S(1)}) custom-call(s32[4]{0:T(128)S(1)} %pad_add_fusion.place, bf16[4,144,1024]{2,1,0:T(8,128)(2,1)S(1)} %constant_dynamic-update-slice_fusion.own_ref, bf16[4,144,1024]{2,1,0:T(8,128)(2,1)S(1)} %copy-done.1), custom_call_target="tpu_custom_call" | custom-call | flops 3000000 | bytes 4000000 | tf_op jit(solution)/shard_map/order_template/pallas_call | solution.py:175
  42.4 2.4 %spectra_early.1.s0.s0_hbm = bf16[2,16,32,1024]{3,2,1,0:T(8,128)(2,1)S(1)} custom-call(s32[4]{0:T(128)S(1)} %pad_add_fusion.place, bf16[2,512,1024]{2,1,0:T(8,128)(2,1)S(1)} %get-tuple-element.22.template_ref, bf16[8,2,32,1024]{3,2,1,0:T(8,128)(2,1)} %constant_dynamic-update-slice_fusion.3.part0, ...), custom_call_target="tpu_custom_call" | custom-call | flops 3000000 | bytes 6000000 | tf_op jit(solution)/shard_map/spectra_early/pallas_call | solution.py:287
  44.8 1.3 %copy-done.2 = bf16[2,16,32,1024]{3,2,1,0:T(8,128)(2,1)} copy-done((bf16[2,16,32,1024]{3,2,1,0:T(8,128)(2,1)}, bf16[2,16,32,1024]{3,2,1,0:T(8,128)(2,1)S(1)}, u32[]{:S(2)}) %copy-start.2) | copy-done | bytes 2097176
  46.1 1.0 %collective-permute-done.9.part0 = bf16[8,2,32,1024]{3,2,1,0:T(8,128)(2,1)} collective-permute-done((bf16[8,2,32,1024]{3,2,1,0:T(8,128)(2,1)}, bf16[8,2,32,1024]{3,2,1,0:T(8,128)(2,1)}, u32[]{:S(2)}, u32[]{:S(2)}) %collective-permute-start.9) | collective-permute-done | bytes 1048608 | tf_op jit(solution)/shard_map/ppermute | solution.py:75
  47.2 0.8 probes.1
  47.9 2.6 %spectra_late.1.s1.s1_hbm = bf16[2,16,32,1024]{3,2,1,0:T(8,128)(2,1)S(1)} custom-call(s32[4]{0:T(128)S(1)} %pad_add_fusion.place, bf16[2,512,1024]{2,1,0:T(8,128)(2,1)S(1)} %get-tuple-element.22.template_ref, bf16[8,2,32,1024]{3,2,1,0:T(8,128)(2,1)} %collective-permute-done.9.part0, bf16[8,2,32,1024]{3,2,1,0:T(8,128)(2,1)} %collective-permute-done.10.part1), custom_call_target="tpu_custom_call" | custom-call | flops 3000000 | bytes 6000000 | tf_op jit(solution)/shard_map/spectra_late/pallas_call | solution.py:287
  50.5 3.9 %veto.1.result_hbm = f32[128,128]{1,0:T(8,128)} custom-call(s32[4]{0:T(128)S(1)} %pad_add_fusion.place, f32[16,256]{1,0:T(8,128)S(1)} %get-tuple-element.27.power_ref, s32[1,256]{1,0:T(1,128)S(1)} %get-tuple-element.29.time_ref, bf16[1024,512]{1,0:T(8,128)(2,1)S(1)} %get-tuple-element.30.one_ref, bf16[1024,512]{1,0:T(8,128)(2,1)S(1)} %get-tuple-element.31.two_ref, ...), custom_call_target="tpu_custom_call" | custom-call | flops 2200000000 | bytes 6000000 | tf_op jit(solution)/shard_map/veto/pallas_call | solution.py:338
  54.4 11.2 %all-to-all-start.1 = ((f32[128,1,128]{2,1,0:T(1,128)}), f32[128,1,128]{2,1,0:T(1,128)S(1)}, u32[]{:S(2)}, u32[]{:S(2)}) async-start(f32[128,1,128]{2,1,0:T(1,128)} %bitcast.7), calls=%async_computation.1 | async-start | bytes 131072 | tf_op jit(solution)/shard_map/all_to_all | solution.py:552
  65.6 10.7 %series.1 = (f32[1024,512]{1,0:T(8,128)}, f32[1,1]{1,0:T(1,128)}) custom-call(s32[4]{0:T(128)} %copy-done.5, bf16[2,16,32,1024]{3,2,1,0:T(8,128)(2,1)} %copy-done.2, bf16[2,16,32,1024]{3,2,1,0:T(8,128)(2,1)} %copy-done.4, f32[128,128]{1,0:T(8,128)} %veto.1.result_hbm, bf16[4,4,256,256]{3,2,1,0:T(8,128)(2,1)} %constant.57.clone.rows_hbm, ...), custom_call_target="tpu_custom_call" | custom-call | flops 3300000000 | bytes 13000000 | tf_op jit(solution)/shard_map/series/pallas_call | solution.py:499
  76.4 0.6 copy-done.9
  77.0 1.7 %take_results.1 = (f32[1,256]{1,0:T(1,128)}, f32[1,256]{1,0:T(1,128)}) custom-call(s32[1,256]{1,0:T(1,128)} %pair_ref.3, s32[1]{0:T(128)S(6)} %copy.25.count_ref, f32[128,128]{1,0:T(8,128)} %bitcast.15), custom_call_target="tpu_custom_call" | custom-call | flops 500000 | bytes 70000 | tf_op jit(solution)/shard_map/take_results/pallas_call | solution.py:208
  (40 shorter events, 1.1 us)
Async XLA Ops:
  3.1 12.6 %copy-start.7 = (bf16[1,2,32,1024]{3,2,1,0:T(8,128)(2,1)S(1)}, bf16[1,2,32,1024]{3,2,1,0:T(8,128)(2,1)}, u32[]{:S(2)}) copy-start(bf16[1,2,32,1024]{3,2,1,0:T(8,128)(2,1)} %get-tuple-element.23) | copy-start | bytes 393220
  3.1 12.7 %copy-start.8 = (bf16[1,2,32,1024]{3,2,1,0:T(8,128)(2,1)S(1)}, bf16[1,2,32,1024]{3,2,1,0:T(8,128)(2,1)}, u32[]{:S(2)}) copy-start(bf16[1,2,32,1024]{3,2,1,0:T(8,128)(2,1)} %get-tuple-element.24) | copy-start | bytes 393220
  3.1 12.6 %collective-permute-start.3 = (bf16[1,2,32,1024]{3,2,1,0:T(8,128)(2,1)}, bf16[1,2,32,1024]{3,2,1,0:T(8,128)(2,1)S(1)}, u32[]{:S(2)}, u32[]{:S(2)}) collective-permute-start(bf16[1,2,32,1024]{3,2,1,0:T(8,128)(2,1)} %get-tuple-element.23), channel_id=1, source_target_pairs={{0,8},{1,25},{2,10},{3,27},{4,12},{5,29},{6,14},{7,31},{8,0},{9,17... | collective-permute-start | bytes 393224 | tf_op jit(solution)/shard_map/ppermute | solution.py:75
  6.7 9.1 %collective-permute-start.6 = (bf16[1,2,32,1024]{3,2,1,0:T(8,128)(2,1)}, bf16[1,2,32,1024]{3,2,1,0:T(8,128)(2,1)S(1)}, u32[]{:S(2)}, u32[]{:S(2)}) collective-permute-start(bf16[1,2,32,1024]{3,2,1,0:T(8,128)(2,1)} %get-tuple-element.24), channel_id=1, source_target_pairs={{0,32},{1,97},{2,34},{3,99},{4,36},{5,101},{6,38},{7,103},{8,40},{... | collective-permute-start | bytes 393224 | tf_op jit(solution)/shard_map/ppermute | solution.py:75
  10.4 7.3 %collective-permute-start = (bf16[1,144,1024]{2,1,0:T(8,128)(2,1)}, bf16[1,144,1024]{2,1,0:T(8,128)(2,1)S(1)}, u32[]{:S(2)}, u32[]{:S(2)}) collective-permute-start(bf16[1,144,1024]{2,1,0:T(8,128)(2,1)} %get-tuple-element.21), channel_id=1, source_target_pairs={{0,2},{1,7},{2,0},{3,5},{4,6},{5,3},{6,4},{7,1},{8,10},{9,15},{10,... | collective-permute-start | bytes 884744 | tf_op jit(solution)/shard_map/ppermute | solution.py:75
  13.9 3.8 %copy-start.6 = (bf16[1,144,1024]{2,1,0:T(8,128)(2,1)S(1)}, bf16[1,144,1024]{2,1,0:T(8,128)(2,1)}, u32[]{:S(2)}) copy-start(bf16[1,144,1024]{2,1,0:T(8,128)(2,1)} %get-tuple-element.21) | copy-start | bytes 884740
  15.7 6.5 %collective-permute-start.4 = (bf16[2,2,32,1024]{3,2,1,0:T(8,128)(2,1)S(1)}, bf16[2,2,32,1024]{3,2,1,0:T(8,128)(2,1)S(1)}, u32[]{:S(2)}, u32[]{:S(2)}) collective-permute-start(bf16[2,2,32,1024]{3,2,1,0:T(8,128)(2,1)S(1)} %pad_maximum_fusion.3), channel_id=1, source_target_pairs={{0,24},{1,9},{2,26},{3,11},{4,28},{5,13},{6,30},{7,15},{8,16},{9,1... | collective-permute-start | bytes 786440 | tf_op jit(solution)/shard_map/ppermute | solution.py:75
  15.9 5.6 %collective-permute-start.7 = (bf16[2,2,32,1024]{3,2,1,0:T(8,128)(2,1)S(1)}, bf16[2,2,32,1024]{3,2,1,0:T(8,128)(2,1)S(1)}, u32[]{:S(2)}, u32[]{:S(2)}) collective-permute-start(bf16[2,2,32,1024]{3,2,1,0:T(8,128)(2,1)S(1)} %pad_maximum_fusion.4), channel_id=1, source_target_pairs={{0,96},{1,33},{2,98},{3,35},{4,100},{5,37},{6,102},{7,39},{8,104},... | collective-permute-start | bytes 786440 | tf_op jit(solution)/shard_map/ppermute | solution.py:75
  17.8 9.1 %collective-permute-start.1 = (bf16[2,144,1024]{2,1,0:T(8,128)(2,1)S(1)}, bf16[2,144,1024]{2,1,0:T(8,128)(2,1)S(1)}, u32[]{:S(2)}, u32[]{:S(2)}) collective-permute-start(bf16[2,144,1024]{2,1,0:T(8,128)(2,1)S(1)} %pad_maximum_fusion), channel_id=1, source_target_pairs={{0,6},{1,3},{2,4},{3,1},{4,2},{5,7},{6,0},{7,5},{8,14},{9,11},{10,... | collective-permute-start | bytes 1769480 | tf_op jit(solution)/shard_map/ppermute | solution.py:75
  21.5 9.3 %collective-permute-start.8 = (bf16[4,2,32,1024]{3,2,1,0:T(8,128)(2,1)S(1)}, bf16[4,2,32,1024]{3,2,1,0:T(8,128)(2,1)S(1)}, u32[]{:S(2)}, u32[]{:S(2)}) collective-permute-start(bf16[4,2,32,1024]{3,2,1,0:T(8,128)(2,1)S(1)} %pad_maximum_fusion.2), channel_id=1, source_target_pairs={{0,8},{1,25},{2,10},{3,27},{4,12},{5,29},{6,14},{7,31},{8,0},{9,17... | collective-permute-start | bytes 1572872 | tf_op jit(solution)/shard_map/ppermute | solution.py:75
  22.3 9.7 %collective-permute-start.5 = (bf16[4,2,32,1024]{3,2,1,0:T(8,128)(2,1)S(1)}, bf16[4,2,32,1024]{3,2,1,0:T(8,128)(2,1)S(1)}, u32[]{:S(2)}, u32[]{:S(2)}) collective-permute-start(bf16[4,2,32,1024]{3,2,1,0:T(8,128)(2,1)S(1)} %pad_maximum_fusion.1), channel_id=1, source_target_pairs={{0,32},{1,97},{2,34},{3,99},{4,36},{5,101},{6,38},{7,103},{8,40},{... | collective-permute-start | bytes 1572872 | tf_op jit(solution)/shard_map/ppermute | solution.py:75
  27.0 6.0 %collective-permute-start.2 = (bf16[4,144,1024]{2,1,0:T(8,128)(2,1)S(1)}, bf16[4,144,1024]{2,1,0:T(8,128)(2,1)S(1)}, u32[]{:S(2)}, u32[]{:S(2)}) collective-permute-start(bf16[4,144,1024]{2,1,0:T(8,128)(2,1)S(1)} %constant_dynamic-update-slice_fusion.own_ref), channel_id=1, source_target_pairs={{0,1},{1,0},{2,3},{3,2},{4,5},{5,4},{6,7},{7,6},{8,9},{9,8},{10,11... | collective-permute-start | bytes 3538952 | tf_op jit(solution)/shard_map/ppermute | solution.py:75
  31.7 14.4 %collective-permute-start.10 = (bf16[8,2,32,1024]{3,2,1,0:T(8,128)(2,1)}, bf16[8,2,32,1024]{3,2,1,0:T(8,128)(2,1)}, u32[]{:S(2)}, u32[]{:S(2)}) collective-permute-start(bf16[8,2,32,1024]{3,2,1,0:T(8,128)(2,1)} %constant_dynamic-update-slice_fusion.7.part1), channel_id=1, source_target_pairs={{0,24},{1,9},{2,26},{3,11},{4,28},{5,13},{6,30},{7,15},{8,16},{9,1... | collective-permute-start | bytes 3145736 | tf_op jit(solution)/shard_map/ppermute | solution.py:75
  32.8 14.4 %collective-permute-start.9 = (bf16[8,2,32,1024]{3,2,1,0:T(8,128)(2,1)}, bf16[8,2,32,1024]{3,2,1,0:T(8,128)(2,1)}, u32[]{:S(2)}, u32[]{:S(2)}) collective-permute-start(bf16[8,2,32,1024]{3,2,1,0:T(8,128)(2,1)} %constant_dynamic-update-slice_fusion.3.part0), channel_id=1, source_target_pairs={{0,96},{1,33},{2,98},{3,35},{4,100},{5,37},{6,102},{7,39},{8,104},... | collective-permute-start | bytes 3145736 | tf_op jit(solution)/shard_map/ppermute | solution.py:75
  32.9 17.6 %copy-start.5 = (s32[4]{0:T(128)}, s32[4]{0:T(128)S(1)}, u32[]{:S(2)}) copy-start(s32[4]{0:T(128)S(1)} %pad_add_fusion.place) | copy-start | bytes 52
  32.9 1.4 %copy-start = (bf16[4,144,1024]{2,1,0:T(8,128)(2,1)}, bf16[4,144,1024]{2,1,0:T(8,128)(2,1)S(1)}, u32[]{:S(2)}) copy-start(bf16[4,144,1024]{2,1,0:T(8,128)(2,1)S(1)} %collective-permute-done.2.other_ref) | copy-start | bytes 3538948
  34.3 12.9 %all-to-all-start = ((s32[16,1,256]{2,1,0:T(1,128)}), s32[16,1,256]{2,1,0:T(1,128)S(1)}, u32[]{:S(2)}, u32[]{:S(2)}) async-start(s32[16,1,256]{2,1,0:T(1,128)} %route_lists.1), calls=%async_computation | async-start | bytes 32768 | tf_op jit(solution)/shard_map/all_to_all | solution.py:546
  38.8 1.3 %copy-start.1 = (bf16[4,144,1024]{2,1,0:T(8,128)(2,1)S(1)}, bf16[4,144,1024]{2,1,0:T(8,128)(2,1)}, u32[]{:S(2)}) copy-start(bf16[4,144,1024]{2,1,0:T(8,128)(2,1)} %copy-done) | copy-start | bytes 3538948
  44.8 1.4 %copy-start.2 = (bf16[2,16,32,1024]{3,2,1,0:T(8,128)(2,1)}, bf16[2,16,32,1024]{3,2,1,0:T(8,128)(2,1)S(1)}, u32[]{:S(2)}) copy-start(bf16[2,16,32,1024]{3,2,1,0:T(8,128)(2,1)S(1)} %spectra_early.1.s0.s0_hbm) | copy-start | bytes 6291460
  47.9 2.6 %copy-start.3 = (bf16[2,16,32,1024]{3,2,1,0:T(8,128)(2,1)S(1)}, bf16[2,16,32,1024]{3,2,1,0:T(8,128)(2,1)}, u32[]{:S(2)}) copy-start(bf16[2,16,32,1024]{3,2,1,0:T(8,128)(2,1)} %copy-done.2) | copy-start | bytes 6291460
  50.5 3.9 %copy-start.4 = (bf16[2,16,32,1024]{3,2,1,0:T(8,128)(2,1)}, bf16[2,16,32,1024]{3,2,1,0:T(8,128)(2,1)S(1)}, u32[]{:S(2)}) copy-start(bf16[2,16,32,1024]{3,2,1,0:T(8,128)(2,1)S(1)} %spectra_late.1.s1.s1_hbm) | copy-start | bytes 6291460
  54.4 22.0 %all-to-all-start.1 = ((f32[128,1,128]{2,1,0:T(1,128)}), f32[128,1,128]{2,1,0:T(1,128)S(1)}, u32[]{:S(2)}, u32[]{:S(2)}) async-start(f32[128,1,128]{2,1,0:T(1,128)} %bitcast.7), calls=%async_computation.1 | async-start | bytes 131072 | tf_op jit(solution)/shard_map/all_to_all | solution.py:552
  76.4 0.6 copy-start.9
